TPU v7x, 32 devices: a whole 2x2x4 slice. The times are simulated.
32 devices in a mesh: parts: 2 (over y), expert: 4 (over x, core), etp: 4 (over z).
Axes of the slice: x: 2, y: 2, z: 4, core: 2. Of those that a mesh axis runs over, the one named last changes fastest.
Arguments:
- out_grad: bfloat16 [512, 3072], P(('parts', 'expert'), 'etp'), parts along dimension 0, may hold values from -6 to 6
- router_logits: float32 [512, 2], P(('parts', 'expert')), parts along dimension 0, may hold values from -6 to 6
- slot_of: int32 [512, 2], P(('parts', 'expert')), parts along dimension 0, may hold values from 0 to 3, all different within a row; in each aligned block of 64 rows (0 to 63, 64 to 127, ...) at most 64 rows name the same one
- gate_pre: bfloat16 [2048, 2048], P(('parts', 'expert'), 'etp'), parts along dimension 0, may hold values from -6 to 6
- up_pre: bfloat16 [2048, 2048], P(('parts', 'expert'), 'etp'), parts along dimension 0, may hold values from -6 to 6
- down_weight: bfloat16 [4, 2048, 3072], P('expert', 'etp'), may hold values from -0.125 to 0.125
Outputs:
- grad_gate: bfloat16 [2048, 2048], P(('parts', 'expert'), 'etp'), parts along dimension 0
- grad_up: bfloat16 [2048, 2048], P(('parts', 'expert'), 'etp'), parts along dimension 0
- logit_grad: float32 [512, 2], P(('parts', 'expert')), parts along dimension 0
There are 2 independent parts, one for each index of `parts`. A program takes and returns all parts, laid end to end along the dimension named above; an argument that names none is the same for every part. Nothing has to cross between parts.
Inputs may be any that keep to these rules, and one draw needn't show every extreme that they name: `slot_of`: A token's two slots differ; at most 64 of the choices of one block of 64 tokens name one slot, a bound that some block reaches.
All inputs are finite; a program needn't handle non-finite values.
Results may differ from a plain program's by a relative error of at most 0.007.
Values may be sent and summed in bfloat16 or wider, within the bound.
No kernel may reach another device: no remote copies, remote signals or barrier semaphores. Data moves between devices by JAX's collectives and lax.ppermute only.
A program may use at most 64 MiB of HBM per device.

v0:
```python
import jax
import jax.numpy as jnp
from jax import lax
from jax.sharding import PartitionSpec as P


def body(out_grad, router_logits, slot_of, gate_pre, up_pre, down_weight):
    slots = lax.axis_size("expert")
    total_rows = gate_pre.shape[0]
    capacity = total_rows // slots
    weight = down_weight[0]
    first = jax.nn.sigmoid(router_logits[:, 0] - router_logits[:, 1])
    probs = jnp.stack([first, 1.0 - first], axis=1)
    probs_b = probs.astype(jnp.bfloat16)
    flat_slot = slot_of.reshape(-1)
    onehot = (flat_slot[:, None] == jnp.arange(slots, dtype=jnp.int32)[None, :]).astype(jnp.int32)
    earlier = (jnp.cumsum(onehot, axis=0) - onehot) * onehot
    position = jnp.sum(earlier, axis=1)
    dest = flat_slot * capacity + position
    placing = dest[:, None] == jnp.arange(total_rows, dtype=jnp.int32)[None, :]
    place_b = placing.astype(jnp.bfloat16)
    place_f = placing.astype(jnp.float32)
    rows_dy = jnp.repeat(out_grad, 2, axis=0)
    send_rows = lax.dot_general(
        place_b, rows_dy, (((0,), (0,)), ((), ())), preferred_element_type=jnp.float32
    ).astype(jnp.bfloat16)
    send_weight = jnp.dot(probs_b.reshape(-1).astype(jnp.float32), place_f).astype(jnp.bfloat16)
    received, row_weight = (
        lax.all_to_all(send_rows, "expert", split_axis=0, concat_axis=0, tiled=True),
        lax.all_to_all(send_weight, "expert", split_axis=0, concat_axis=0, tiled=True),
    )
    z_local = lax.dot_general(
        lax.all_gather(received, "etp", axis=1, tiled=True),
        weight,
        (((1,), (1,)), ((), ())),
        preferred_element_type=jnp.float32,
    )
    g = gate_pre.astype(jnp.float32)
    u = up_pre.astype(jnp.float32)
    sig = jax.nn.sigmoid(g)
    act = g * sig
    hb = (act * u).astype(jnp.bfloat16)
    dh = row_weight.astype(jnp.float32)[:, None] * z_local
    grad_up = (dh * act).astype(jnp.bfloat16)
    grad_gate = (dh * u * sig * (1.0 + g * (1.0 - sig))).astype(jnp.bfloat16)
    partial_dp = jnp.sum(hb.astype(jnp.float32) * z_local, axis=1)
    row_dp = lax.psum(partial_dp, "etp")
    returned = lax.all_to_all(row_dp, "expert", split_axis=0, concat_axis=0, tiled=True)
    picked = jnp.dot(place_f, returned).reshape(probs.shape)
    mean_term = jnp.sum(probs * picked, axis=1, keepdims=True)
    logit_grad = probs * (picked - mean_term)
    return (grad_gate, grad_up, logit_grad)


def solution(mesh):
    return jax.shard_map(
        body,
        mesh=mesh,
        in_specs=(
            P(("parts", "expert"), "etp"),
            P(("parts", "expert"), None),
            P(("parts", "expert"), None),
            P(("parts", "expert"), "etp"),
            P(("parts", "expert"), "etp"),
            P("expert", "etp", None),
        ),
        out_specs=(
            P(("parts", "expert"), "etp"),
            P(("parts", "expert"), "etp"),
            P(("parts", "expert"), None),
        ),
        check_vma=False,
    )
```

profile of v0, /device:TPU:0, one launch (start us, length us, event | category | flops | bytes accessed | tf_op | source)
XLA Modules:
  0.0 89.6 jit_solution(4454019511473320622)
XLA Ops:
  7.2 0.9 %copy.26 = s32[64,2]{1,0:T(8,128)S(1)} copy(s32[64,2]{0,1:T(2,128)} %param.8) | data formatting | bytes 1024 | tf_op args[2]
  8.1 0.1 reshape.63
  8.4 0.2 reduce_window_sum.11
  8.6 0.2 select_reduce_fusion
  8.7 1.0 %broadcast_in_dim.2 = bf16[64,2,768]{2,1,0:T(2,128)(2,1)S(1)} broadcast(bf16[64,768]{1,0:T(8,128)(2,1)} %param.6), dimensions={0,2} | broadcast | bytes 294912 | tf_op jit(solution)/shard_map/broadcast_in_dim | solution.py:23
  9.8 0.4 convolution_convert_fusion
  10.2 11.6 %all_to_all.34 = bf16[4,64,768]{2,1,0:T(8,128)(2,1)} all-to-all(bf16[4,64,768]{2,1,0:T(8,128)(2,1)S(1)} %bitcast.21), channel_id=1, replica_groups=mesh['parts'=2,'expert'=4,'etp'=4] {'expert'}, dimensions={0} | all-to-all | bytes 786432 | tf_op jit(solution)/shard_map/all_to_all | solution.py:29
  21.8 0.8 broadcast_subtract_fusion
  22.6 0.1 copy.25
  22.7 0.2 reshape.66
  22.8 0.2 fusion.10
  23.1 0.7 all_to_all.30
  23.7 3.2 %all-to-all-start = ((bf16[4,64,1]{1,2,0:T(2,128)(2,1)}), bf16[4,64,1]{1,2,0:T(2,128)(2,1)S(1)}, u32[]{:S(2)}, u32[]{:S(2)}) async-start(bf16[4,64,1]{1,2,0:T(2,128)(2,1)} %all_to_all.30), calls=%async_computation | async-start | bytes 4096 | tf_op jit(solution)/shard_map/all_to_all | solution.py:30
  27.0 0.1 reduce_sum.30
  27.2 3.4 %all-to-all-done = bf16[4,64,1]{1,2,0:T(2,128)(2,1)S(1)} async-done(((bf16[4,64,1]{1,2,0:T(2,128)(2,1)}), bf16[4,64,1]{1,2,0:T(2,128)(2,1)S(1)}, u32[]{:S(2)}, u32[]{:S(2)}) %all-to-all-start) | async-done | bytes 544 | tf_op jit(solution)/shard_map/all_to_all | solution.py:30
  30.7 29.1 %all-gather.2.cloned.1.call-done = bf16[256,3072]{1,0:T(8,128)(2,1)} async-done(((bf16[256,768]{1,0:T(8,128)(2,1)}), bf16[256,3072]{1,0:T(8,128)(2,1)}) %all-gather.2.cloned.1.call-update) | async-done | bytes 1572880 | tf_op jit(solution)/shard_map/all_gather | solution.py:33
  59.8 3.6 %multiply_reduce_fusion = (f32[256]{0:T(256)S(1)}, bf16[256,512]{1,0:T(8,128)(2,1)}, bf16[256,512]{1,0:T(8,128)(2,1)}) fusion(bf16[256,512]{1,0:T(8,128)(2,1)} %param.10, bf16[256,512]{1,0:T(8,128)(2,1)} %param.9, f32[256]{0:T(256)S(1)} %reshape.65, bf16[256,3072]{1,0:T(8,128)(2,1)} %all-gather.2.cloned.1.call-done, bf16[1,512,3072]{2,1,0:T(8,128)(2,1)S(1)} %copy-done), kind=kOutput, calls=%fused_computation.16 | convolution fusion | flops 808058624 | bytes 5769216 | tf_op jit(solution)/shard_map/dot_general | solution.py:32
  63.5 10.2 %psum.7 = f32[4,64,1]{1,0,2:T(4,128)} all-reduce(f32[4,64,1]{1,0,2:T(4,128)S(1)} %all_to_all.27), channel_id=1, replica_groups=mesh['parts'=2,'expert'=4,'etp'=4] {'etp'}, use_global_device_ids=true, to_apply=%region_3.4 | all-reduce | flops 256 | bytes 2048 | tf_op jit(solution)/shard_map/psum | solution.py:47
  73.6 3.2 %all-to-all-start.2 = ((f32[4,64,1]{1,2,0:T(1,128)}), f32[4,64,1]{1,2,0:T(1,128)S(1)}, u32[]{:S(2)}, u32[]{:S(2)}) async-start(f32[4,64,1]{1,2,0:T(1,128)} %bitcast.5), calls=%async_computation.2 | async-start | bytes 4096 | tf_op jit(solution)/shard_map/all_to_all | solution.py:48
  76.9 3.7 %all-to-all-done.2 = f32[4,64,1]{1,2,0:T(1,128)S(1)} async-done(((f32[4,64,1]{1,2,0:T(1,128)}), f32[4,64,1]{1,2,0:T(1,128)S(1)}, u32[]{:S(2)}, u32[]{:S(2)}) %all-to-all-start.2) | async-done | bytes 1056 | tf_op jit(solution)/shard_map/all_to_all | solution.py:48
  80.6 0.5 broadcast.57
  81.1 0.7 reduce.7
  81.9 0.2 fusion.12
  82.1 0.6 subtract_multiply_fusion
  (18 shorter events, 0.7 us)
Async XLA Ops:
  7.2 52.6 %copy-start = (bf16[1,512,3072]{2,1,0:T(8,128)(2,1)S(1)}, bf16[1,512,3072]{2,1,0:T(8,128)(2,1)}, u32[]{:S(2)}) copy-start(bf16[1,512,3072]{2,1,0:T(8,128)(2,1)} %param.11) | copy-start | bytes 9437188
  7.2 52.6 %all-gather.2.cloned.1.call-start = ((), (), s32[]{:S(2)}) async-start(), calls=%async_computation.3 | async-start | bytes 1966080 | tf_op jit(solution)/shard_map/all_gather | solution.py:33
  23.7 6.9 %all-to-all-start = ((bf16[4,64,1]{1,2,0:T(2,128)(2,1)}), bf16[4,64,1]{1,2,0:T(2,128)(2,1)S(1)}, u32[]{:S(2)}, u32[]{:S(2)}) async-start(bf16[4,64,1]{1,2,0:T(2,128)(2,1)} %all_to_all.30), calls=%async_computation | async-start | bytes 4096 | tf_op jit(solution)/shard_map/all_to_all | solution.py:30
  30.7 46.2 %copy-start.1 = (s32[64,2]{0,1:T(2,128)S(1)}, s32[64,2]{0,1:T(2,128)}, u32[]{:S(2)}) copy-start(s32[64,2]{0,1:T(2,128)} %param.8) | copy-start | bytes 1540
  73.6 7.0 %all-to-all-start.2 = ((f32[4,64,1]{1,2,0:T(1,128)}), f32[4,64,1]{1,2,0:T(1,128)S(1)}, u32[]{:S(2)}, u32[]{:S(2)}) async-start(f32[4,64,1]{1,2,0:T(1,128)} %bitcast.5), calls=%async_computation.2 | async-start | bytes 4096 | tf_op jit(solution)/shard_map/all_to_all | solution.py:48
Sparse Core Ops, SparseCore 0:
  21.9 37.8 all-gather.1
where the time goes:
time: 89.9 us; the launch traced here: 89.6 us
  waiting for transfers between devices  36.2 us (40%)
  blocking collectives  21.7 us (24%)
  between operations  14.1 us (16%)
  starting transfers between devices  6.5 us (7%)
  matrix products  4.39 us (5%)
  local copies, waits for them, and re-layouts  4.06 us (5%)
  other arithmetic  2.54 us (3%)
    all_gather x1, waiting for transfers between devices, body(): lax.all_gather(received, 'etp', axis=1, tiled=True)  29.1 us
    all_to_all x1, blocking collectives, body(): lax.all_to_all(send_rows, 'expert', split_axis=0, concat_axis=0, tiled=True)  11.6 us
    psum x1, blocking collectives, body(): row_dp = lax.psum(partial_dp, 'etp')  10.2 us
    all_to_all x1, waiting for transfers between devices, body(): lax.all_to_all(row_dp, 'expert', split_axis=0, concat_axis=0, tiled=True)  3.7 us
    dot_general x1, matrix products, body(): lax.dot_general(lax.all_gather(received, 'etp', axis=1, tiled=True), weig...  3.61 us
    all_to_all x1, waiting for transfers between devices, body(): lax.all_to_all(send_weight, 'expert', split_axis=0, concat_axis=0, tiled=...  3.43 us
    all_to_all x1, starting transfers between devices, body(): lax.all_to_all(row_dp, 'expert', split_axis=0, concat_axis=0, tiled=True)  3.24 us
    all_to_all x1, starting transfers between devices, body(): lax.all_to_all(send_weight, 'expert', split_axis=0, concat_axis=0, tiled=...  3.22 us
  transfers between devices with their start and end apart: 3, of which 3 were waited for; matrix products, arithmetic and copies ran while one was open for 2% of the time, Pallas kernels for 0%

commit v1 on v0

--- a/solution.py
+++ b/solution.py
@@ -1,7 +1,246 @@
 import jax
 import jax.numpy as jnp
 from jax import lax
+from jax.experimental import pallas as pl
+from jax.experimental.pallas import tpu as pltpu
 from jax.sharding import PartitionSpec as P
+
+BF16 = jnp.bfloat16
+F32 = jnp.float32
+NT = (((1,), (1,)), ((), ()))
+META = 16
+
+
+def vmem_specs(count):
+    return [pl.BlockSpec(memory_space=pltpu.VMEM)] * count
+
+
+def call(kernel, outs, args, scratch=(), flops=0, limit=16):
+    out_bytes = sum(o.size * o.dtype.itemsize for o in outs)
+    in_bytes = sum(a.size * a.dtype.itemsize for a in args)
+    return pl.pallas_call(
+        kernel,
+        out_shape=tuple(outs),
+        in_specs=vmem_specs(len(args)),
+        out_specs=tuple(vmem_specs(len(outs))),
+        scratch_shapes=list(scratch),
+        compiler_params=pltpu.CompilerParams(vmem_limit_bytes=limit * 2**20),
+        cost_estimate=pl.CostEstimate(
+            flops=flops, bytes_accessed=out_bytes + in_bytes, transcendentals=0
+        ),
+    )(*args)
+
+
+def pack_kernel(rows_ref, logits_ref, slots_ref, out_ref):
+    tokens, width = rows_ref.shape
+    first = jax.nn.sigmoid(logits_ref[0:1, :] - logits_ref[1:2, :])
+    facts = jnp.concatenate(
+        [
+            slots_ref[...].astype(F32),
+            first,
+            1.0 - first,
+            jnp.zeros((META - 4, tokens), F32),
+        ],
+        axis=0,
+    )
+    out_ref[:tokens, :] = rows_ref[...]
+    out_ref[tokens:, :] = jnp.concatenate(
+        [facts, jnp.zeros((META, width - tokens), F32)], axis=1
+    ).astype(BF16)
+
+
+def place_rows(target, index, blocks, mine, tokens):
+    for other, block in enumerate(blocks):
+        start = pl.multiple_of((mine ^ other) * tokens, tokens)
+        target[index, pl.ds(start, tokens), :] = block
+
+
+def first_kernel(
+    own_ref, x_ref, z1_ref, d1_ref, sib_ref, weight_ref, gate_ref, up_ref,
+    total_ref, hb_ref, place_ref, chosen_ref, row_weight_ref,
+    rows_s, facts_s,
+):
+    mine, deep = lax.axis_index("expert"), lax.axis_index("etp")
+    tokens, width = z1_ref.shape
+    long = tokens + META
+    groups = total_ref.shape[0] // tokens
+    sib = (0, long, long + tokens, 2 * long + tokens)
+    place_rows(
+        rows_s, 0,
+        (own_ref[:tokens, :], sib_ref[sib[0] : sib[0] + tokens, :], x_ref[:tokens, :], sib_ref[sib[2] : sib[2] + tokens, :]),
+        mine, tokens,
+    )
+    place_rows(
+        rows_s, 1,
+        (z1_ref[...], sib_ref[sib[1] : sib[1] + tokens, :], d1_ref[...], sib_ref[sib[3] : sib[3] + tokens, :]),
+        mine, tokens,
+    )
+    for other, (ref, start) in enumerate(
+        ((own_ref, 0), (sib_ref, sib[0]), (x_ref, 0), (sib_ref, sib[2]))
+    ):
+        facts_s[mine ^ other] = ref[start + tokens : start + long, :tokens].astype(F32)
+    total = None
+    for index in range(2):
+        start = pl.multiple_of((deep ^ index) * width, 128)
+        part = lax.dot_general(
+            rows_s[index], weight_ref[:, pl.ds(start, width)], NT, preferred_element_type=F32
+        )
+        total = part if total is None else total + part
+    total_ref[...] = total
+    g = gate_ref[...].astype(F32)
+    hb_ref[...] = (g * jax.nn.sigmoid(g) * up_ref[...].astype(F32)).astype(BF16)
+    slot = mine.astype(F32)
+    row = lax.broadcasted_iota(jnp.int32, (tokens, tokens), 0)
+    lane = lax.broadcasted_iota(jnp.int32, (tokens, tokens), 1)
+    before = (row < lane).astype(BF16)
+    row_f = row.astype(F32)
+    firsts = [(facts_s[j, 0:1, :] == slot).astype(F32) for j in range(groups)]
+    seconds = [(facts_s[j, 1:2, :] == slot).astype(F32) for j in range(groups)]
+    chosen = jnp.concatenate(firsts + seconds, axis=0)
+    chosen_ref[...] = chosen
+    match = chosen[:groups] + chosen[groups:]
+    position = jnp.dot(
+        jnp.concatenate([match, match], axis=0).astype(BF16), before, preferred_element_type=F32
+    )
+    for j in range(groups):
+        hit = (position[j : j + 1] == row_f) & (match[j : j + 1] > 0.5)
+        place = hit.astype(F32)
+        weight = firsts[j] * facts_s[j, 2:3, :] + seconds[j] * facts_s[j, 3:4, :]
+        place_ref[j] = place
+        row_weight_ref[j * tokens : (j + 1) * tokens, :] = jnp.sum(
+            place * weight, axis=1, keepdims=True
+        )
+
+
+def second_kernel(
+    total_ref, z2_ref, z3_ref, x2_ref, d3_ref, sib_a_ref, sib_b_ref, weight_ref,
+    hb_ref, place_ref, chosen_ref, row_weight_ref,
+    dh_ref, share_ref,
+    rows_s,
+):
+    mine, deep = lax.axis_index("expert"), lax.axis_index("etp")
+    tokens, width = z2_ref.shape
+    groups = total_ref.shape[0] // tokens
+    last = sib_a_ref.shape[0] - tokens
+    place_rows(
+        rows_s, 0,
+        (z2_ref[...], sib_a_ref[last:, :], x2_ref[...], sib_b_ref[tokens : 2 * tokens, :]),
+        mine, tokens,
+    )
+    place_rows(
+        rows_s, 1,
+        (z3_ref[...], sib_b_ref[:tokens, :], d3_ref[...], sib_b_ref[2 * tokens :, :]),
+        mine, tokens,
+    )
+    total = total_ref[...]
+    for index in range(2):
+        start = pl.multiple_of((deep ^ (2 + index)) * width, 128)
+        total = total + lax.dot_general(
+            rows_s[index], weight_ref[:, pl.ds(start, width)], NT, preferred_element_type=F32
+        )
+    sums = []
+    for j in range(groups):
+        part = slice(j * tokens, (j + 1) * tokens)
+        place = place_ref[j]
+        place_b = place.astype(BF16)
+        high = total[part].astype(BF16)
+        low = (total[part] - high.astype(F32)).astype(BF16)
+        z = jnp.dot(place_b, high, preferred_element_type=F32) + jnp.dot(
+            place_b, low, preferred_element_type=F32
+        )
+        dh_ref[part, :] = row_weight_ref[part, :] * z
+        dp = jnp.sum(hb_ref[part, :].astype(F32) * z, axis=1, keepdims=True)
+        sums.append(jnp.sum(place * dp, axis=0, keepdims=True))
+    sums = jnp.concatenate(sums, axis=0)
+    share_ref[...] = chosen_ref[...] * jnp.concatenate([sums, sums], axis=0)
+
+
+def grads_kernel(dh_ref, gate_ref, up_ref, grad_gate_ref, grad_up_ref):
+    g = gate_ref[...].astype(F32)
+    u = up_ref[...].astype(F32)
+    dh = dh_ref[...]
+    sig = jax.nn.sigmoid(g)
+    grad_up_ref[...] = (dh * (g * sig)).astype(BF16)
+    grad_gate_ref[...] = (dh * u * sig * (1.0 + g * (1.0 - sig))).astype(BF16)
+
+
+def logits_kernel(a_ref, b_ref, c_ref, d_ref, logits_ref, out_ref, sum_s):
+    mine = lax.axis_index("expert")
+    groups = a_ref.shape[0] // 2
+    sum_s[...] = (a_ref[...] + b_ref[...]) + (c_ref[...] + d_ref[...])
+    picked_0 = sum_s[pl.ds(mine, 1), :]
+    picked_1 = sum_s[pl.ds(mine + groups, 1), :]
+    first = jax.nn.sigmoid(logits_ref[0:1, :] - logits_ref[1:2, :])
+    second = 1.0 - first
+    mean = first * picked_0 + second * picked_1
+    out_ref[...] = jnp.concatenate([first * (picked_0 - mean), second * (picked_1 - mean)], axis=0)
+
+
+def small_body(out_grad, router_logits, slot_of, gate_pre, up_pre, down_weight):
+    tokens, width = out_grad.shape
+    rows, hidden = gate_pre.shape
+    weight = down_weight[0]
+    slots, deep = lax.axis_size("expert"), lax.axis_size("etp")
+
+    def swap(value, dx, dc, dz):
+        mask = (dx * 2 + dc) * deep + dz
+        return lax.ppermute(
+            value, ("expert", "etp"), [(i, i ^ mask) for i in range(slots * deep)]
+        )
+
+    logits_t, slots_t = router_logits.T, slot_of.T
+    (own,) = call(
+        pack_kernel,
+        [jax.ShapeDtypeStruct((tokens + META, width), BF16)],
+        [out_grad, logits_t, slots_t],
+    )
+    z2 = swap(out_grad, 0, 0, 2)
+    z1 = swap(out_grad, 0, 0, 1)
+    xo = swap(own, 1, 0, 0)
+    d1 = swap(out_grad, 1, 0, 1)
+    z3 = swap(z2, 0, 0, 1)
+    x2 = swap(z2, 1, 0, 0)
+    d3 = swap(z2, 1, 0, 1)
+    sib_a = swap(jnp.concatenate([own, z1, xo, d1, z2], axis=0), 0, 1, 0)
+    sib_b = swap(jnp.concatenate([z3, x2, d3], axis=0), 0, 1, 0)
+    half_flops = 2 * rows * hidden * width * 2
+    total, hb, place, chosen, row_weight = call(
+        first_kernel,
+        [
+            jax.ShapeDtypeStruct((rows, hidden), F32),
+            jax.ShapeDtypeStruct((rows, hidden), BF16),
+            jax.ShapeDtypeStruct((slots, tokens, tokens), F32),
+            jax.ShapeDtypeStruct((2 * slots, tokens), F32),
+            jax.ShapeDtypeStruct((rows, 1), F32),
+        ],
+        [own, xo, z1, d1, sib_a, weight, gate_pre, up_pre],
+        scratch=[pltpu.VMEM((2, rows, width), BF16), pltpu.VMEM((slots, META, tokens), F32)],
+        flops=half_flops,
+    )
+    dh, share = call(
+        second_kernel,
+        [
+            jax.ShapeDtypeStruct((rows, hidden), F32),
+            jax.ShapeDtypeStruct((2 * slots, tokens), F32),
+        ],
+        [total, z2, z3, x2, d3, sib_a, sib_b, weight, hb, place, chosen, row_weight],
+        scratch=[pltpu.VMEM((2, rows, width), BF16)],
+        flops=half_flops,
+    )
+    share = share + swap(share, 0, 1, 0) + swap(share, 1, 0, 0) + swap(share, 1, 1, 0)
+    pieces = [share] + [swap(share, 0, 0, dz) for dz in range(1, deep)]
+    grad_gate, grad_up = call(
+        grads_kernel,
+        [jax.ShapeDtypeStruct((rows, hidden), BF16)] * 2,
+        [dh, gate_pre, up_pre],
+    )
+    (logit_grad,) = call(
+        logits_kernel,
+        [jax.ShapeDtypeStruct((2, tokens), F32)],
+        [*pieces, logits_t],
+        scratch=[pltpu.VMEM((2 * slots, tokens), F32)],
+    )
+    return grad_gate, grad_up, logit_grad.T
 
 
 def body(out_grad, router_logits, slot_of, gate_pre, up_pre, down_weight):
@@ -53,8 +292,9 @@
 
 
 def solution(mesh):
+    small = mesh.shape["expert"] == 4 and mesh.shape["etp"] == 4
     return jax.shard_map(
-        body,
+        small_body if small else body,
         mesh=mesh,
         in_specs=(
             P(("parts", "expert"), "etp"),

time: 89.9 us -> 42.1 us (0.47)
  waiting for transfers between devices: 36.2 us -> 12.5 us
  blocking collectives: 21.7 us -> 0 us
  between operations: 14.1 us -> 0.76 us
  starting transfers between devices: 6.5 us -> 18 us
  matrix products: 4.39 us -> 0 us
  Pallas kernels: 0 us -> 3.33 us
  local copies, waits for them, and re-layouts: 4.06 us -> 7.18 us
  other arithmetic: 2.54 us -> 0.03 us
    all_gather x1 -> x0, waiting for transfers between devices: 29.1 us -> none  [body(): lax.all_gather(received, 'etp', axis=1, tiled=True)]
    ppermute x0 -> x15, starting transfers between devices: none -> 18 us  [swap(): lax.ppermute(value, ('expert', 'etp'), [(i, i ^ mask) for i in range(slot...]
    ppermute x0 -> x15, waiting for transfers between devices: none -> 12.5 us  [swap(): lax.ppermute(value, ('expert', 'etp'), [(i, i ^ mask) for i in range(slot...]
    all_to_all x1 -> x0, blocking collectives: 11.6 us -> none  [body(): lax.all_to_all(send_rows, 'expert', split_axis=0, concat_axis=0, tiled=True)]
    psum x1 -> x0, blocking collectives: 10.2 us -> none  [body(): row_dp = lax.psum(partial_dp, 'etp')]
    all_to_all x2 -> x0, waiting for transfers between devices: 7.12 us -> none  [the longest x1 3.7 us: body(): lax.all_to_all(row_dp, 'expert', split_axis=0, concat_axis=0, tiled=True)]
    all_to_all x2 -> x0, starting transfers between devices: 6.47 us -> none  [the longest x1 3.24 us: body(): lax.all_to_all(row_dp, 'expert', split_axis=0, concat_axis=0, tiled=True)]
    unnamed x5 -> x24, local copies, waits for them, and re-layouts: 0.93 us -> 7.17 us
  transfers between devices with their start and end apart: 3 -> 15, of which waited for: 3 -> 6; matrix products, arithmetic and copies ran while one was open for 2% -> 0% of each run, Pallas kernels for 0% -> 4%
where the time goes in v1:
time: 42.1 us; the launch traced here: 41.8 us
  starting transfers between devices  18 us (43%)
  waiting for transfers between devices  12.5 us (30%)
  local copies, waits for them, and re-layouts  7.18 us (17%)
  Pallas kernels  3.33 us (8%)
  between operations  0.76 us (2%)
    ppermute x15, starting transfers between devices, swap(): lax.ppermute(value, ('expert', 'etp'), [(i, i ^ mask) for i in range(slot...  18 us
    ppermute x15, waiting for transfers between devices, swap(): lax.ppermute(value, ('expert', 'etp'), [(i, i ^ mask) for i in range(slot...  12.5 us
    unnamed x24, local copies, waits for them, and re-layouts  7.17 us
    pallas_call x5, Pallas kernels, call(): pl.pallas_call(kernel, out_shape=tuple(outs), in_specs=vmem_specs(len(arg...  3.33 us
  transfers between devices with their start and end apart: 15, of which 6 were waited for; matrix products, arithmetic and copies ran while one was open for 0% of the time, Pallas kernels for 4%

profile of v1, /device:TPU:0, one launch (start us, length us, event | category | flops | bytes accessed | tf_op | source)
XLA Modules:
  0.0 41.8 jit_solution(7946256411966286351)
XLA Ops:
  0.6 3.1 %collective-permute-start.1 = (bf16[64,768]{1,0:T(8,128)(2,1)}, bf16[64,768]{1,0:T(8,128)(2,1)S(1)}, u32[]{:S(2)}, u32[]{:S(2)}) collective-permute-start(bf16[64,768]{1,0:T(8,128)(2,1)} %rows_ref.1), channel_id=1, source_target_pairs={{0,1},{1,0},{2,3},{3,2},{4,5},{5,4},{6,7},{7,6},{8,9},{9,8},{10,11... | collective-permute-start | bytes 294920 | tf_op jit(solution)/shard_map/ppermute | solution.py:187
  3.7 2.6 %collective-permute-start.3 = (bf16[64,768]{1,0:T(8,128)(2,1)}, bf16[64,768]{1,0:T(8,128)(2,1)S(1)}, u32[]{:S(2)}, u32[]{:S(2)}) collective-permute-start(bf16[64,768]{1,0:T(8,128)(2,1)} %rows_ref.1), channel_id=1, source_target_pairs={{0,2},{1,3},{2,0},{3,1},{4,6},{5,7},{6,4},{7,5},{8,10},{9,11},{10,... | collective-permute-start | bytes 294920 | tf_op jit(solution)/shard_map/ppermute | solution.py:187
  6.3 1.4 %collective-permute-start.2 = (bf16[64,768]{1,0:T(8,128)(2,1)}, bf16[64,768]{1,0:T(8,128)(2,1)S(1)}, u32[]{:S(2)}, u32[]{:S(2)}) collective-permute-start(bf16[64,768]{1,0:T(8,128)(2,1)} %rows_ref.1), channel_id=1, source_target_pairs={{0,9},{1,8},{2,11},{3,10},{4,13},{5,12},{6,15},{7,14},{8,1},{9,0},... | collective-permute-start | bytes 294920 | tf_op jit(solution)/shard_map/ppermute | solution.py:187
  7.7 0.9 %copy-done.6 = bf16[64,768]{1,0:T(8,128)(2,1)S(1)} copy-done((bf16[64,768]{1,0:T(8,128)(2,1)S(1)}, bf16[64,768]{1,0:T(8,128)(2,1)}, u32[]{:S(2)}) %copy-start.6) | copy-done | bytes 98328
  10.6 4.4 %collective-permute-done.x_ref = bf16[80,768]{1,0:T(8,128)(2,1)S(1)} collective-permute-done((bf16[80,768]{1,0:T(8,128)(2,1)S(1)}, bf16[80,768]{1,0:T(8,128)(2,1)S(1)}, u32[]{:S(2)}, u32[]{:S(2)}) %collective-permute-start) | collective-permute-done | bytes 122912 | tf_op jit(solution)/shard_map/ppermute | solution.py:187
  15.2 1.5 %collective-permute-start.7 = (bf16[64,768]{1,0:T(8,128)(2,1)S(1)}, bf16[64,768]{1,0:T(8,128)(2,1)S(1)}, u32[]{:S(2)}, u32[]{:S(2)}) collective-permute-start(bf16[64,768]{1,0:T(8,128)(2,1)S(1)} %collective-permute-done.3.z2_ref), channel_id=1, source_target_pairs={{0,9},{1,8},{2,11},{3,10},{4,13},{5,12},{6,15},{7,14},{8,1},{9,0},... | collective-permute-start | bytes 294920 | tf_op jit(solution)/shard_map/ppermute | solution.py:187
  16.7 1.5 %collective-permute-start.6 = (bf16[64,768]{1,0:T(8,128)(2,1)S(1)}, bf16[64,768]{1,0:T(8,128)(2,1)S(1)}, u32[]{:S(2)}, u32[]{:S(2)}) collective-permute-start(bf16[64,768]{1,0:T(8,128)(2,1)S(1)} %collective-permute-done.3.z2_ref), channel_id=1, source_target_pairs={{0,8},{1,9},{2,10},{3,11},{4,12},{5,13},{6,14},{7,15},{8,0},{9,1},... | collective-permute-start | bytes 294920 | tf_op jit(solution)/shard_map/ppermute | solution.py:187
  18.8 3.0 %collective-permute-done.7.d3_ref = bf16[64,768]{1,0:T(8,128)(2,1)S(1)} collective-permute-done((bf16[64,768]{1,0:T(8,128)(2,1)S(1)}, bf16[64,768]{1,0:T(8,128)(2,1)S(1)}, u32[]{:S(2)}, u32[]{:S(2)}) %collective-permute-start.7) | collective-permute-done | bytes 98336 | tf_op jit(solution)/shard_map/ppermute | solution.py:187
  21.8 1.7 %collective-permute-done.6.x2_ref = bf16[64,768]{1,0:T(8,128)(2,1)S(1)} collective-permute-done((bf16[64,768]{1,0:T(8,128)(2,1)S(1)}, bf16[64,768]{1,0:T(8,128)(2,1)S(1)}, u32[]{:S(2)}, u32[]{:S(2)}) %collective-permute-start.6) | collective-permute-done | bytes 98336 | tf_op jit(solution)/shard_map/ppermute | solution.py:187
  23.6 1.9 %copy-done = bf16[1,512,3072]{2,1,0:T(8,128)(2,1)S(1)} copy-done((bf16[1,512,3072]{2,1,0:T(8,128)(2,1)S(1)}, bf16[1,512,3072]{2,1,0:T(8,128)(2,1)}, u32[]{:S(2)}) %copy-start) | copy-done | bytes 3145752
  25.5 0.9 %copy-done.2 = bf16[256,512]{1,0:T(8,128)(2,1)S(1)} copy-done((bf16[256,512]{1,0:T(8,128)(2,1)S(1)}, bf16[256,512]{1,0:T(8,128)(2,1)}, u32[]{:S(2)}) %copy-start.2) | copy-done | bytes 262168
  26.4 0.9 %copy-done.4 = bf16[256,512]{1,0:T(8,128)(2,1)S(1)} copy-done((bf16[256,512]{1,0:T(8,128)(2,1)S(1)}, bf16[256,512]{1,0:T(8,128)(2,1)}, u32[]{:S(2)}) %copy-start.4) | copy-done | bytes 262168
  27.4 0.8 %shard_map.86 = (f32[256,512]{1,0:T(8,128)S(1)}, bf16[256,512]{1,0:T(8,128)(2,1)S(1)}, f32[4,64,64]{2,1,0:T(8,128)S(1)}, f32[8,64]{1,0:T(8,128)S(1)}, f32[256,1]{1,0:T(8,128)S(1)}) custom-call(bf16[80,768]{1,0:T(8,128)(2,1)S(1)} %shard_map.85.own_ref, bf16[80,768]{1,0:T(8,128)(2,1)S(1)} %collective-permute-done.x_ref, ...), custom_call_target="tpu_custom_call" | custom-call | flops 402653184 | bytes 5508096 | tf_op jit(solution)/shard_map/pallas_call | solution.py:21
  28.2 1.0 %copy-done.1 = bf16[1,512,3072]{2,1,0:T(8,128)(2,1)S(1)} copy-done((bf16[1,512,3072]{2,1,0:T(8,128)(2,1)S(1)}, bf16[1,512,3072]{2,1,0:T(8,128)(2,1)}, u32[]{:S(2)}) %copy-start.1) | copy-done | bytes 3145752
  29.3 1.0 %shard_map.87 = (f32[256,512]{1,0:T(8,128)S(1)}, f32[8,64]{1,0:T(8,128)S(1)}) custom-call(f32[256,512]{1,0:T(8,128)S(1)} %get-tuple-element.12.total_ref, bf16[64,768]{1,0:T(8,128)(2,1)S(1)} %collective-permute-done.3.z2_ref, bf16[64,768]{1,0:T(8,128)(2,1)S(1)} %collective-permute-done.5.z3_ref, bf16[64,768]{1,0:T(8,128)(2,1)S(1)} %collective-permute-done.6.x2_ref, ...), custom_call_target="tpu_custom_call" | custom-call | flops 402653184 | bytes 5755904 | tf_op jit(solution)/shard_map/pallas_call | solution.py:21
  30.2 1.2 %collective-permute-start.11 = (f32[8,64]{1,0:T(8,128)S(1)}, f32[8,64]{1,0:T(8,128)S(1)}, u32[]{:S(2)}, u32[]{:S(2)}) collective-permute-start(f32[8,64]{1,0:T(8,128)S(1)} %get-tuple-element.20), channel_id=1, source_target_pairs={{0,12},{1,13},{2,14},{3,15},{4,8},{5,9},{6,10},{7,11},{8,4},{9,5},... | collective-permute-start | bytes 6152 | tf_op jit(solution)/shard_map/ppermute | solution.py:187
  31.4 1.0 %collective-permute-start.10 = (f32[8,64]{1,0:T(8,128)S(1)}, f32[8,64]{1,0:T(8,128)S(1)}, u32[]{:S(2)}, u32[]{:S(2)}) collective-permute-start(f32[8,64]{1,0:T(8,128)S(1)} %get-tuple-element.20), channel_id=1, source_target_pairs={{0,8},{1,9},{2,10},{3,11},{4,12},{5,13},{6,14},{7,15},{8,0},{9,1},... | collective-permute-start | bytes 6152 | tf_op jit(solution)/shard_map/ppermute | solution.py:187
  32.4 0.9 %collective-permute-done.11 = f32[8,64]{1,0:T(8,128)S(1)} collective-permute-done((f32[8,64]{1,0:T(8,128)S(1)}, f32[8,64]{1,0:T(8,128)S(1)}, u32[]{:S(2)}, u32[]{:S(2)}) %collective-permute-start.11) | collective-permute-done | bytes 2080 | tf_op jit(solution)/shard_map/ppermute | solution.py:187
  33.3 1.7 %collective-permute-done.10 = f32[8,64]{1,0:T(8,128)S(1)} collective-permute-done((f32[8,64]{1,0:T(8,128)S(1)}, f32[8,64]{1,0:T(8,128)S(1)}, u32[]{:S(2)}, u32[]{:S(2)}) %collective-permute-start.10) | collective-permute-done | bytes 2080 | tf_op jit(solution)/shard_map/ppermute | solution.py:187
  35.0 1.7 %collective-permute-start.14 = (f32[8,64]{1,0:T(8,128)S(1)}, f32[8,64]{1,0:T(8,128)S(1)}, u32[]{:S(2)}, u32[]{:S(2)}) collective-permute-start(f32[8,64]{1,0:T(8,128)S(1)} %add_add_fusion.a_ref), channel_id=1, source_target_pairs={{0,3},{1,2},{2,1},{3,0},{4,7},{5,6},{6,5},{7,4},{8,11},{9,10},{10,... | collective-permute-start | bytes 6152 | tf_op jit(solution)/shard_map/ppermute | solution.py:187
  36.7 0.9 %collective-permute-start.13 = (f32[8,64]{1,0:T(8,128)S(1)}, f32[8,64]{1,0:T(8,128)S(1)}, u32[]{:S(2)}, u32[]{:S(2)}) collective-permute-start(f32[8,64]{1,0:T(8,128)S(1)} %add_add_fusion.a_ref), channel_id=1, source_target_pairs={{0,2},{1,3},{2,0},{3,1},{4,6},{5,7},{6,4},{7,5},{8,10},{9,11},{10,... | collective-permute-start | bytes 6152 | tf_op jit(solution)/shard_map/ppermute | solution.py:187
  37.6 1.9 %collective-permute-start.12 = (f32[8,64]{1,0:T(8,128)S(1)}, f32[8,64]{1,0:T(8,128)S(1)}, u32[]{:S(2)}, u32[]{:S(2)}) collective-permute-start(f32[8,64]{1,0:T(8,128)S(1)} %add_add_fusion.a_ref), channel_id=1, source_target_pairs={{0,1},{1,0},{2,3},{3,2},{4,5},{5,4},{6,7},{7,6},{8,9},{9,8},{10,11... | collective-permute-start | bytes 6152 | tf_op jit(solution)/shard_map/ppermute | solution.py:187
  39.5 1.0 %shard_map.88 = (bf16[256,512]{1,0:T(8,128)(2,1)}, bf16[256,512]{1,0:T(8,128)(2,1)}) custom-call(f32[256,512]{1,0:T(8,128)S(1)} %get-tuple-element.17.dh_ref, bf16[256,512]{1,0:T(8,128)(2,1)S(1)} %copy-done.3, bf16[256,512]{1,0:T(8,128)(2,1)S(1)} %copy-done.5), custom_call_target="tpu_custom_call" | custom-call | bytes 1572864 | tf_op jit(solution)/shard_map/pallas_call | solution.py:21
  40.5 0.7 %collective-permute-done.13.c_ref = f32[8,64]{1,0:T(8,128)S(1)} collective-permute-done((f32[8,64]{1,0:T(8,128)S(1)}, f32[8,64]{1,0:T(8,128)S(1)}, u32[]{:S(2)}, u32[]{:S(2)}) %collective-permute-start.13) | collective-permute-done | bytes 2080 | tf_op jit(solution)/shard_map/ppermute | solution.py:187
  (38 shorter events, 3.5 us)
Async XLA Ops:
  0.6 10.0 %collective-permute-start.1 = (bf16[64,768]{1,0:T(8,128)(2,1)}, bf16[64,768]{1,0:T(8,128)(2,1)S(1)}, u32[]{:S(2)}, u32[]{:S(2)}) collective-permute-start(bf16[64,768]{1,0:T(8,128)(2,1)} %rows_ref.1), channel_id=1, source_target_pairs={{0,1},{1,0},{2,3},{3,2},{4,5},{5,4},{6,7},{7,6},{8,9},{9,8},{10,11... | collective-permute-start | bytes 294920 | tf_op jit(solution)/shard_map/ppermute | solution.py:187
  3.7 11.4 %collective-permute-start.3 = (bf16[64,768]{1,0:T(8,128)(2,1)}, bf16[64,768]{1,0:T(8,128)(2,1)S(1)}, u32[]{:S(2)}, u32[]{:S(2)}) collective-permute-start(bf16[64,768]{1,0:T(8,128)(2,1)} %rows_ref.1), channel_id=1, source_target_pairs={{0,2},{1,3},{2,0},{3,1},{4,6},{5,7},{6,4},{7,5},{8,10},{9,11},{10,... | collective-permute-start | bytes 294920 | tf_op jit(solution)/shard_map/ppermute | solution.py:187
  6.3 8.8 %collective-permute-start.2 = (bf16[64,768]{1,0:T(8,128)(2,1)}, bf16[64,768]{1,0:T(8,128)(2,1)S(1)}, u32[]{:S(2)}, u32[]{:S(2)}) collective-permute-start(bf16[64,768]{1,0:T(8,128)(2,1)} %rows_ref.1), channel_id=1, source_target_pairs={{0,9},{1,8},{2,11},{3,10},{4,13},{5,12},{6,15},{7,14},{8,1},{9,0},... | collective-permute-start | bytes 294920 | tf_op jit(solution)/shard_map/ppermute | solution.py:187
  7.7 0.9 %copy-start.6 = (bf16[64,768]{1,0:T(8,128)(2,1)S(1)}, bf16[64,768]{1,0:T(8,128)(2,1)}, u32[]{:S(2)}) copy-start(bf16[64,768]{1,0:T(8,128)(2,1)} %rows_ref.1) | copy-start | bytes 294916
  8.6 0.7 %copy-start.7 = (f32[64,2]{0,1:T(2,128)S(1)}, f32[64,2]{0,1:T(2,128)}, u32[]{:S(2)}) copy-start(f32[64,2]{0,1:T(2,128)} %param.7) | copy-start | bytes 1540
  10.0 5.1 %collective-permute-start = (bf16[80,768]{1,0:T(8,128)(2,1)S(1)}, bf16[80,768]{1,0:T(8,128)(2,1)S(1)}, u32[]{:S(2)}, u32[]{:S(2)}) collective-permute-start(bf16[80,768]{1,0:T(8,128)(2,1)S(1)} %shard_map.85.own_ref), channel_id=1, source_target_pairs={{0,8},{1,9},{2,10},{3,11},{4,12},{5,13},{6,14},{7,15},{8,0},{9,1},... | collective-permute-start | bytes 368648 | tf_op jit(solution)/shard_map/ppermute | solution.py:187
  15.1 8.4 %collective-permute-start.4 = (bf16[352,768]{1,0:T(8,128)(2,1)S(1)}, bf16[352,768]{1,0:T(8,128)(2,1)S(1)}, u32[]{:S(2)}, u32[]{:S(2)}) collective-permute-start(bf16[352,768]{1,0:T(8,128)(2,1)S(1)} %constant_dynamic-update-slice_fusion), channel_id=1, source_target_pairs={{0,4},{1,5},{2,6},{3,7},{4,0},{5,1},{6,2},{7,3},{8,12},{9,13},{10,... | collective-permute-start | bytes 1622024 | tf_op jit(solution)/shard_map/ppermute | solution.py:187
  15.2 6.6 %collective-permute-start.7 = (bf16[64,768]{1,0:T(8,128)(2,1)S(1)}, bf16[64,768]{1,0:T(8,128)(2,1)S(1)}, u32[]{:S(2)}, u32[]{:S(2)}) collective-permute-start(bf16[64,768]{1,0:T(8,128)(2,1)S(1)} %collective-permute-done.3.z2_ref), channel_id=1, source_target_pairs={{0,9},{1,8},{2,11},{3,10},{4,13},{5,12},{6,15},{7,14},{8,1},{9,0},... | collective-permute-start | bytes 294920 | tf_op jit(solution)/shard_map/ppermute | solution.py:187
  16.7 6.7 %collective-permute-start.6 = (bf16[64,768]{1,0:T(8,128)(2,1)S(1)}, bf16[64,768]{1,0:T(8,128)(2,1)S(1)}, u32[]{:S(2)}, u32[]{:S(2)}) collective-permute-start(bf16[64,768]{1,0:T(8,128)(2,1)S(1)} %collective-permute-done.3.z2_ref), channel_id=1, source_target_pairs={{0,8},{1,9},{2,10},{3,11},{4,12},{5,13},{6,14},{7,15},{8,0},{9,1},... | collective-permute-start | bytes 294920 | tf_op jit(solution)/shard_map/ppermute | solution.py:187
  18.2 5.3 %collective-permute-start.5 = (bf16[64,768]{1,0:T(8,128)(2,1)S(1)}, bf16[64,768]{1,0:T(8,128)(2,1)S(1)}, u32[]{:S(2)}, u32[]{:S(2)}) collective-permute-start(bf16[64,768]{1,0:T(8,128)(2,1)S(1)} %collective-permute-done.3.z2_ref), channel_id=1, source_target_pairs={{0,1},{1,0},{2,3},{3,2},{4,5},{5,4},{6,7},{7,6},{8,9},{9,8},{10,11... | collective-permute-start | bytes 294920 | tf_op jit(solution)/shard_map/ppermute | solution.py:187
  23.5 4.7 %collective-permute-start.8 = (bf16[192,768]{1,0:T(8,128)(2,1)S(1)}, bf16[192,768]{1,0:T(8,128)(2,1)S(1)}, u32[]{:S(2)}, u32[]{:S(2)}) collective-permute-start(bf16[192,768]{1,0:T(8,128)(2,1)S(1)} %pad_maximum_fusion), channel_id=1, source_target_pairs={{0,4},{1,5},{2,6},{3,7},{4,0},{5,1},{6,2},{7,3},{8,12},{9,13},{10,... | collective-permute-start | bytes 884744 | tf_op jit(solution)/shard_map/ppermute | solution.py:187
  23.6 1.9 %copy-start = (bf16[1,512,3072]{2,1,0:T(8,128)(2,1)S(1)}, bf16[1,512,3072]{2,1,0:T(8,128)(2,1)}, u32[]{:S(2)}) copy-start(bf16[1,512,3072]{2,1,0:T(8,128)(2,1)} %param.11) | copy-start | bytes 9437188
  25.5 0.9 %copy-start.2 = (bf16[256,512]{1,0:T(8,128)(2,1)S(1)}, bf16[256,512]{1,0:T(8,128)(2,1)}, u32[]{:S(2)}) copy-start(bf16[256,512]{1,0:T(8,128)(2,1)} %gate_ref.3) | copy-start | bytes 786436
  26.4 0.9 %copy-start.4 = (bf16[256,512]{1,0:T(8,128)(2,1)S(1)}, bf16[256,512]{1,0:T(8,128)(2,1)}, u32[]{:S(2)}) copy-start(bf16[256,512]{1,0:T(8,128)(2,1)} %up_ref.3) | copy-start | bytes 786436
  27.4 1.9 %copy-start.1 = (bf16[1,512,3072]{2,1,0:T(8,128)(2,1)S(1)}, bf16[1,512,3072]{2,1,0:T(8,128)(2,1)}, u32[]{:S(2)}) copy-start(bf16[1,512,3072]{2,1,0:T(8,128)(2,1)} %param.11) | copy-start | bytes 9437188
  28.2 11.3 %copy-start.3 = (bf16[256,512]{1,0:T(8,128)(2,1)S(1)}, bf16[256,512]{1,0:T(8,128)(2,1)}, u32[]{:S(2)}) copy-start(bf16[256,512]{1,0:T(8,128)(2,1)} %gate_ref.3) | copy-start | bytes 786436
  28.2 11.3 %copy-start.5 = (bf16[256,512]{1,0:T(8,128)(2,1)S(1)}, bf16[256,512]{1,0:T(8,128)(2,1)}, u32[]{:S(2)}) copy-start(bf16[256,512]{1,0:T(8,128)(2,1)} %up_ref.3) | copy-start | bytes 786436
  29.3 11.9 %copy-start.8 = (f32[64,2]{0,1:T(2,128)S(1)}, f32[64,2]{0,1:T(2,128)}, u32[]{:S(2)}) copy-start(f32[64,2]{0,1:T(2,128)} %param.7) | copy-start | bytes 1540
  30.2 3.1 %collective-permute-start.11 = (f32[8,64]{1,0:T(8,128)S(1)}, f32[8,64]{1,0:T(8,128)S(1)}, u32[]{:S(2)}, u32[]{:S(2)}) collective-permute-start(f32[8,64]{1,0:T(8,128)S(1)} %get-tuple-element.20), channel_id=1, source_target_pairs={{0,12},{1,13},{2,14},{3,15},{4,8},{5,9},{6,10},{7,11},{8,4},{9,5},... | collective-permute-start | bytes 6152 | tf_op jit(solution)/shard_map/ppermute | solution.py:187
  31.4 3.6 %collective-permute-start.10 = (f32[8,64]{1,0:T(8,128)S(1)}, f32[8,64]{1,0:T(8,128)S(1)}, u32[]{:S(2)}, u32[]{:S(2)}) collective-permute-start(f32[8,64]{1,0:T(8,128)S(1)} %get-tuple-element.20), channel_id=1, source_target_pairs={{0,8},{1,9},{2,10},{3,11},{4,12},{5,13},{6,14},{7,15},{8,0},{9,1},... | collective-permute-start | bytes 6152 | tf_op jit(solution)/shard_map/ppermute | solution.py:187
  32.4 2.6 %collective-permute-start.9 = (f32[8,64]{1,0:T(8,128)S(1)}, f32[8,64]{1,0:T(8,128)S(1)}, u32[]{:S(2)}, u32[]{:S(2)}) collective-permute-start(f32[8,64]{1,0:T(8,128)S(1)} %get-tuple-element.20), channel_id=1, source_target_pairs={{0,4},{1,5},{2,6},{3,7},{4,0},{5,1},{6,2},{7,3},{8,12},{9,13},{10,... | collective-permute-start | bytes 6152 | tf_op jit(solution)/shard_map/ppermute | solution.py:187
  35.0 5.5 %collective-permute-start.14 = (f32[8,64]{1,0:T(8,128)S(1)}, f32[8,64]{1,0:T(8,128)S(1)}, u32[]{:S(2)}, u32[]{:S(2)}) collective-permute-start(f32[8,64]{1,0:T(8,128)S(1)} %add_add_fusion.a_ref), channel_id=1, source_target_pairs={{0,3},{1,2},{2,1},{3,0},{4,7},{5,6},{6,5},{7,4},{8,11},{9,10},{10,... | collective-permute-start | bytes 6152 | tf_op jit(solution)/shard_map/ppermute | solution.py:187
  36.7 4.5 %collective-permute-start.13 = (f32[8,64]{1,0:T(8,128)S(1)}, f32[8,64]{1,0:T(8,128)S(1)}, u32[]{:S(2)}, u32[]{:S(2)}) collective-permute-start(f32[8,64]{1,0:T(8,128)S(1)} %add_add_fusion.a_ref), channel_id=1, source_target_pairs={{0,2},{1,3},{2,0},{3,1},{4,6},{5,7},{6,4},{7,5},{8,10},{9,11},{10,... | collective-permute-start | bytes 6152 | tf_op jit(solution)/shard_map/ppermute | solution.py:187
  37.6 3.7 %collective-permute-start.12 = (f32[8,64]{1,0:T(8,128)S(1)}, f32[8,64]{1,0:T(8,128)S(1)}, u32[]{:S(2)}, u32[]{:S(2)}) collective-permute-start(f32[8,64]{1,0:T(8,128)S(1)} %add_add_fusion.a_ref), channel_id=1, source_target_pairs={{0,1},{1,0},{2,3},{3,2},{4,5},{5,4},{6,7},{7,6},{8,9},{9,8},{10,11... | collective-permute-start | bytes 6152 | tf_op jit(solution)/shard_map/ppermute | solution.py:187
  (1 other events, 0.7 us)

commit v2 on v1

--- a/solution.py
+++ b/solution.py
@@ -11,18 +11,19 @@
 META = 16
 
 
-def vmem_specs(count):
-    return [pl.BlockSpec(memory_space=pltpu.VMEM)] * count
-
-
-def call(kernel, outs, args, scratch=(), flops=0, limit=16):
+VMEM = pl.BlockSpec(memory_space=pltpu.VMEM)
+HBM = pl.BlockSpec(memory_space=pltpu.HBM)
+
+
+def call(kernel, outs, args, scratch=(), flops=0, limit=16, hbm=0):
+    args = [pltpu.with_memory_space_constraint(a, pltpu.HBM) for a in args[:hbm]] + list(args[hbm:])
     out_bytes = sum(o.size * o.dtype.itemsize for o in outs)
     in_bytes = sum(a.size * a.dtype.itemsize for a in args)
     return pl.pallas_call(
         kernel,
         out_shape=tuple(outs),
-        in_specs=vmem_specs(len(args)),
-        out_specs=tuple(vmem_specs(len(outs))),
+        in_specs=[HBM] * hbm + [VMEM] * (len(args) - hbm),
+        out_specs=tuple([VMEM] * len(outs)),
         scratch_shapes=list(scratch),
         compiler_params=pltpu.CompilerParams(vmem_limit_bytes=limit * 2**20),
         cost_estimate=pl.CostEstimate(
@@ -31,22 +32,55 @@
     )(*args)
 
 
-def pack_kernel(rows_ref, logits_ref, slots_ref, out_ref):
-    tokens, width = rows_ref.shape
+def facts_kernel(logits_hbm, slots_hbm, out_ref, logits_ref, slots_ref, sems):
+    meta, width = out_ref.shape
+    tokens = logits_ref.shape[1]
+    copies = [
+        pltpu.make_async_copy(logits_hbm, logits_ref, sems.at[0]),
+        pltpu.make_async_copy(slots_hbm, slots_ref, sems.at[1]),
+    ]
+    for copy in copies:
+        copy.start()
+    for copy in copies:
+        copy.wait()
     first = jax.nn.sigmoid(logits_ref[0:1, :] - logits_ref[1:2, :])
     facts = jnp.concatenate(
-        [
-            slots_ref[...].astype(F32),
-            first,
-            1.0 - first,
-            jnp.zeros((META - 4, tokens), F32),
-        ],
+        [slots_ref[...].astype(F32), first, 1.0 - first, jnp.zeros((meta - 4, tokens), F32)],
         axis=0,
     )
-    out_ref[:tokens, :] = rows_ref[...]
-    out_ref[tokens:, :] = jnp.concatenate(
-        [facts, jnp.zeros((META, width - tokens), F32)], axis=1
+    out_ref[...] = jnp.concatenate(
+        [facts, jnp.zeros((meta, width - tokens), F32)], axis=1
     ).astype(BF16)
+
+
+def load_kernel(
+    weight_hbm, gate_hbm, up_hbm, rows_hbm, facts_ref,
+    weight_ref, gate_ref, up_ref, hb_ref, own_ref,
+    sems,
+):
+    tokens = rows_hbm.shape[0]
+    copies = [
+        pltpu.make_async_copy(gate_hbm, gate_ref, sems.at[0]),
+        pltpu.make_async_copy(up_hbm, up_ref, sems.at[1]),
+        pltpu.make_async_copy(weight_hbm, weight_ref, sems.at[2]),
+        pltpu.make_async_copy(rows_hbm, own_ref.at[pl.ds(0, tokens)], sems.at[3]),
+    ]
+    for copy in copies:
+        copy.start()
+    own_ref[tokens:, :] = facts_ref[...]
+    copies[0].wait()
+    copies[1].wait()
+    g = gate_ref[...].astype(F32)
+    hb_ref[...] = (g * jax.nn.sigmoid(g) * up_ref[...].astype(F32)).astype(BF16)
+    copies[2].wait()
+    copies[3].wait()
+
+
+def bundle_kernel(a_ref, b_ref, c_ref, order_ref, out_ref):
+    tokens = a_ref.shape[0]
+    out_ref[:tokens, :] = a_ref[...]
+    out_ref[tokens : 2 * tokens, :] = b_ref[...]
+    out_ref[2 * tokens :, :] = c_ref[...]
 
 
 def place_rows(target, index, blocks, mine, tokens):
@@ -56,29 +90,31 @@
 
 
 def first_kernel(
-    own_ref, x_ref, z1_ref, d1_ref, sib_ref, weight_ref, gate_ref, up_ref,
-    total_ref, hb_ref, place_ref, chosen_ref, row_weight_ref,
+    own_ref, x_facts_ref, x_ref, z1_ref, d1_ref, sib_ref, weight_ref,
+    total_ref, place_ref, chosen_ref, row_weight_ref,
     rows_s, facts_s,
 ):
     mine, deep = lax.axis_index("expert"), lax.axis_index("etp")
     tokens, width = z1_ref.shape
     long = tokens + META
     groups = total_ref.shape[0] // tokens
-    sib = (0, long, long + tokens, 2 * long + tokens)
+    sib_z1 = long + META
+    sib_x = sib_z1 + tokens
+    sib_d1 = sib_x + tokens
     place_rows(
         rows_s, 0,
-        (own_ref[:tokens, :], sib_ref[sib[0] : sib[0] + tokens, :], x_ref[:tokens, :], sib_ref[sib[2] : sib[2] + tokens, :]),
+        (own_ref[:tokens, :], sib_ref[:tokens, :], x_ref[...], sib_ref[sib_x:sib_d1, :]),
         mine, tokens,
     )
     place_rows(
         rows_s, 1,
-        (z1_ref[...], sib_ref[sib[1] : sib[1] + tokens, :], d1_ref[...], sib_ref[sib[3] : sib[3] + tokens, :]),
+        (z1_ref[...], sib_ref[sib_z1:sib_x, :], d1_ref[...], sib_ref[sib_d1 : sib_d1 + tokens, :]),
         mine, tokens,
     )
     for other, (ref, start) in enumerate(
-        ((own_ref, 0), (sib_ref, sib[0]), (x_ref, 0), (sib_ref, sib[2]))
+        ((own_ref, tokens), (sib_ref, tokens), (x_facts_ref, 0), (sib_ref, long))
     ):
-        facts_s[mine ^ other] = ref[start + tokens : start + long, :tokens].astype(F32)
+        facts_s[mine ^ other] = ref[start : start + META, :tokens].astype(F32)
     total = None
     for index in range(2):
         start = pl.multiple_of((deep ^ index) * width, 128)
@@ -87,8 +123,6 @@
         )
         total = part if total is None else total + part
     total_ref[...] = total
-    g = gate_ref[...].astype(F32)
-    hb_ref[...] = (g * jax.nn.sigmoid(g) * up_ref[...].astype(F32)).astype(BF16)
     slot = mine.astype(F32)
     row = lax.broadcasted_iota(jnp.int32, (tokens, tokens), 0)
     lane = lax.broadcasted_iota(jnp.int32, (tokens, tokens), 1)
@@ -189,34 +223,58 @@
         )
 
     logits_t, slots_t = router_logits.T, slot_of.T
-    (own,) = call(
-        pack_kernel,
-        [jax.ShapeDtypeStruct((tokens + META, width), BF16)],
-        [out_grad, logits_t, slots_t],
-    )
     z2 = swap(out_grad, 0, 0, 2)
     z1 = swap(out_grad, 0, 0, 1)
-    xo = swap(own, 1, 0, 0)
+    xo = swap(out_grad, 1, 0, 0)
     d1 = swap(out_grad, 1, 0, 1)
+    (facts,) = call(
+        facts_kernel,
+        [jax.ShapeDtypeStruct((META, width), BF16)],
+        [logits_t, slots_t],
+        scratch=[
+            pltpu.VMEM((2, tokens), F32),
+            pltpu.VMEM((2, tokens), jnp.int32),
+            pltpu.SemaphoreType.DMA((2,)),
+        ],
+        hbm=2,
+    )
+    x_facts = swap(facts, 1, 0, 0)
+    weight, gate, up, hb, own = call(
+        load_kernel,
+        [
+            jax.ShapeDtypeStruct(weight.shape, BF16),
+            jax.ShapeDtypeStruct((rows, hidden), BF16),
+            jax.ShapeDtypeStruct((rows, hidden), BF16),
+            jax.ShapeDtypeStruct((rows, hidden), BF16),
+            jax.ShapeDtypeStruct((tokens + META, width), BF16),
+        ],
+        [weight, gate_pre, up_pre, out_grad, facts],
+        scratch=[pltpu.SemaphoreType.DMA((4,))],
+        hbm=4,
+    )
     z3 = swap(z2, 0, 0, 1)
     x2 = swap(z2, 1, 0, 0)
     d3 = swap(z2, 1, 0, 1)
-    sib_a = swap(jnp.concatenate([own, z1, xo, d1, z2], axis=0), 0, 1, 0)
-    sib_b = swap(jnp.concatenate([z3, x2, d3], axis=0), 0, 1, 0)
+    sib_a = swap(jnp.concatenate([own, x_facts, z1, xo, d1, z2], axis=0), 0, 1, 0)
     half_flops = 2 * rows * hidden * width * 2
-    total, hb, place, chosen, row_weight = call(
+    total, place, chosen, row_weight = call(
         first_kernel,
         [
             jax.ShapeDtypeStruct((rows, hidden), F32),
-            jax.ShapeDtypeStruct((rows, hidden), BF16),
             jax.ShapeDtypeStruct((slots, tokens, tokens), F32),
             jax.ShapeDtypeStruct((2 * slots, tokens), F32),
             jax.ShapeDtypeStruct((rows, 1), F32),
         ],
-        [own, xo, z1, d1, sib_a, weight, gate_pre, up_pre],
+        [own, x_facts, xo, z1, d1, sib_a, weight],
         scratch=[pltpu.VMEM((2, rows, width), BF16), pltpu.VMEM((slots, META, tokens), F32)],
         flops=half_flops,
     )
+    (bundle,) = call(
+        bundle_kernel,
+        [jax.ShapeDtypeStruct((3 * tokens, width), BF16)],
+        [z3, x2, d3, chosen],
+    )
+    sib_b = swap(bundle, 0, 1, 0)
     dh, share = call(
         second_kernel,
         [
@@ -232,7 +290,7 @@
     grad_gate, grad_up = call(
         grads_kernel,
         [jax.ShapeDtypeStruct((rows, hidden), BF16)] * 2,
-        [dh, gate_pre, up_pre],
+        [dh, gate, up],
     )
     (logit_grad,) = call(
         logits_kernel,

time: 42.1 us -> 36.3 us (0.86)
  local copies, waits for them, and re-layouts: 7.18 us -> 0.05 us
  Pallas kernels: 3.33 us -> 6.09 us
  waiting for transfers between devices: 12.5 us -> 9.98 us
  starting transfers between devices: 18 us -> 19.3 us
    unnamed x24 -> x7, local copies, waits for them, and re-layouts: 7.17 us -> 0.04 us
    pallas_call x5 -> x7, Pallas kernels: 3.33 us -> 6.09 us  [call(): pl.pallas_call(kernel, out_shape=tuple(outs), in_specs=[HBM] * hbm + [VME...]
    ppermute x15 -> x16, waiting for transfers between devices: 12.5 us -> 9.98 us  [swap(): lax.ppermute(value, ('expert', 'etp'), [(i, i ^ mask) for i in range(slot...]
    ppermute x15 -> x16, starting transfers between devices: 18 us -> 19.3 us  [swap(): lax.ppermute(value, ('expert', 'etp'), [(i, i ^ mask) for i in range(slot...]
  transfers between devices with their start and end apart: 15 -> 16, of which waited for: 6 -> 8; matrix products, arithmetic and copies ran while one was open for 0% -> 0% of each run, Pallas kernels for 4% -> 13%
where the time goes in v2:
time: 36.3 us; the launch traced here: 36.1 us
  starting transfers between devices  19.3 us (53%)
  waiting for transfers between devices  9.98 us (27%)
  Pallas kernels  6.09 us (17%)
  between operations  0.75 us (2%)
    ppermute x16, starting transfers between devices, swap(): lax.ppermute(value, ('expert', 'etp'), [(i, i ^ mask) for i in range(slot...  19.3 us
    ppermute x16, waiting for transfers between devices, swap(): lax.ppermute(value, ('expert', 'etp'), [(i, i ^ mask) for i in range(slot...  9.98 us
    pallas_call x7, Pallas kernels, call(): pl.pallas_call(kernel, out_shape=tuple(outs), in_specs=[HBM] * hbm + [VME...  6.09 us
  transfers between devices with their start and end apart: 16, of which 8 were waited for; matrix products, arithmetic and copies ran while one was open for 0% of the time, Pallas kernels for 13%

profile of v2, /device:TPU:0, one launch (start us, length us, event | category | flops | bytes accessed | tf_op | source)
XLA Modules:
  0.0 36.1 jit_solution(1063152956102452739)
XLA Ops:
  0.6 3.1 %collective-permute-start.2 = (bf16[64,768]{1,0:T(8,128)(2,1)}, bf16[64,768]{1,0:T(8,128)(2,1)S(1)}, u32[]{:S(2)}, u32[]{:S(2)}) collective-permute-start(bf16[64,768]{1,0:T(8,128)(2,1)} %rows_hbm.1), channel_id=1, source_target_pairs={{0,1},{1,0},{2,3},{3,2},{4,5},{5,4},{6,7},{7,6},{8,9},{9,8},{10,11... | collective-permute-start | bytes 294920 | tf_op jit(solution)/shard_map/ppermute | solution.py:221
  3.7 1.5 %collective-permute-start.1 = (bf16[64,768]{1,0:T(8,128)(2,1)}, bf16[64,768]{1,0:T(8,128)(2,1)S(1)}, u32[]{:S(2)}, u32[]{:S(2)}) collective-permute-start(bf16[64,768]{1,0:T(8,128)(2,1)} %rows_hbm.1), channel_id=1, source_target_pairs={{0,8},{1,9},{2,10},{3,11},{4,12},{5,13},{6,14},{7,15},{8,0},{9,1},... | collective-permute-start | bytes 294920 | tf_op jit(solution)/shard_map/ppermute | solution.py:221
  5.2 2.6 %collective-permute-start.4 = (bf16[64,768]{1,0:T(8,128)(2,1)}, bf16[64,768]{1,0:T(8,128)(2,1)S(1)}, u32[]{:S(2)}, u32[]{:S(2)}) collective-permute-start(bf16[64,768]{1,0:T(8,128)(2,1)} %rows_hbm.1), channel_id=1, source_target_pairs={{0,2},{1,3},{2,0},{3,1},{4,6},{5,7},{6,4},{7,5},{8,10},{9,11},{10,... | collective-permute-start | bytes 294920 | tf_op jit(solution)/shard_map/ppermute | solution.py:221
  8.2 0.7 %shard_map.85.facts_ref = bf16[16,768]{1,0:T(8,128)(2,1)S(1)} custom-call(f32[2,64]{1,0:T(2,128)} %bitcast.4, s32[2,64]{1,0:T(2,128)} %bitcast.8), custom_call_target="tpu_custom_call" | custom-call | bytes 25600 | tf_op jit(solution)/shard_map/pallas_call | solution.py:22
  9.0 1.6 %collective-permute-start = (bf16[16,768]{1,0:T(8,128)(2,1)S(1)}, bf16[16,768]{1,0:T(8,128)(2,1)S(1)}, u32[]{:S(2)}, u32[]{:S(2)}) collective-permute-start(bf16[16,768]{1,0:T(8,128)(2,1)S(1)} %shard_map.85.facts_ref), channel_id=1, source_target_pairs={{0,8},{1,9},{2,10},{3,11},{4,12},{5,13},{6,14},{7,15},{8,0},{9,1},... | collective-permute-start | bytes 73736 | tf_op jit(solution)/shard_map/ppermute | solution.py:221
  10.5 2.1 %shard_map.86 = (bf16[512,3072]{1,0:T(8,128)(2,1)S(1)}, bf16[256,512]{1,0:T(8,128)(2,1)S(1)}, bf16[256,512]{1,0:T(8,128)(2,1)S(1)}, bf16[256,512]{1,0:T(8,128)(2,1)S(1)}, bf16[80,768]{1,0:T(8,128)(2,1)S(1)}) custom-call(bf16[512,3072]{1,0:T(8,128)(2,1)} %bitcast.6, bf16[256,512]{1,0:T(8,128)(2,1)} %gate_hbm.1, bf16[256,512]{1,0:T(8,128)(2,1)} %up_hbm.1, ...), custom_call_target="tpu_custom_call" | custom-call | bytes 7847936 | tf_op jit(solution)/shard_map/pallas_call | solution.py:22
  12.6 1.2 %collective-permute-done.x_facts_ref = bf16[16,768]{1,0:T(8,128)(2,1)S(1)} collective-permute-done((bf16[16,768]{1,0:T(8,128)(2,1)S(1)}, bf16[16,768]{1,0:T(8,128)(2,1)S(1)}, u32[]{:S(2)}, u32[]{:S(2)}) %collective-permute-start) | collective-permute-done | bytes 24608 | tf_op jit(solution)/shard_map/ppermute | solution.py:221
  14.0 1.6 %collective-permute-start.8 = (bf16[64,768]{1,0:T(8,128)(2,1)S(1)}, bf16[64,768]{1,0:T(8,128)(2,1)S(1)}, u32[]{:S(2)}, u32[]{:S(2)}) collective-permute-start(bf16[64,768]{1,0:T(8,128)(2,1)S(1)} %collective-permute-done.4.z2_ref), channel_id=1, source_target_pairs={{0,9},{1,8},{2,11},{3,10},{4,13},{5,12},{6,15},{7,14},{8,1},{9,0},... | collective-permute-start | bytes 294920 | tf_op jit(solution)/shard_map/ppermute | solution.py:221
  16.1 1.4 %collective-permute-start.6 = (bf16[64,768]{1,0:T(8,128)(2,1)S(1)}, bf16[64,768]{1,0:T(8,128)(2,1)S(1)}, u32[]{:S(2)}, u32[]{:S(2)}) collective-permute-start(bf16[64,768]{1,0:T(8,128)(2,1)S(1)} %collective-permute-done.4.z2_ref), channel_id=1, source_target_pairs={{0,1},{1,0},{2,3},{3,2},{4,5},{5,4},{6,7},{7,6},{8,9},{9,8},{10,11... | collective-permute-start | bytes 294920 | tf_op jit(solution)/shard_map/ppermute | solution.py:221
  17.5 0.7 %shard_map.87 = (f32[256,512]{1,0:T(8,128)S(1)}, f32[4,64,64]{2,1,0:T(8,128)S(1)}, f32[8,64]{1,0:T(8,128)S(1)}, f32[256,1]{1,0:T(8,128)S(1)}) custom-call(bf16[80,768]{1,0:T(8,128)(2,1)S(1)} %get-tuple-element.16.own_ref, bf16[16,768]{1,0:T(8,128)(2,1)S(1)} %collective-permute-done.x_facts_ref, bf16[64,768]{1,0:T(8,128)(2,1)S(1)} %collective-permute-done.1.x_ref, ...), custom_call_target="tpu_custom_call" | custom-call | flops 402653184 | bytes 4721664 | tf_op jit(solution)/shard_map/pallas_call | solution.py:22
  18.3 2.3 %collective-permute-done.8.c_ref.d3_ref = bf16[64,768]{1,0:T(8,128)(2,1)S(1)} collective-permute-done((bf16[64,768]{1,0:T(8,128)(2,1)S(1)}, bf16[64,768]{1,0:T(8,128)(2,1)S(1)}, u32[]{:S(2)}, u32[]{:S(2)}) %collective-permute-start.8) | collective-permute-done | bytes 98336 | tf_op jit(solution)/shard_map/ppermute | solution.py:221
  20.5 1.7 %collective-permute-done.7.b_ref.x2_ref = bf16[64,768]{1,0:T(8,128)(2,1)S(1)} collective-permute-done((bf16[64,768]{1,0:T(8,128)(2,1)S(1)}, bf16[64,768]{1,0:T(8,128)(2,1)S(1)}, u32[]{:S(2)}, u32[]{:S(2)}) %collective-permute-start.7) | collective-permute-done | bytes 98336 | tf_op jit(solution)/shard_map/ppermute | solution.py:221
  22.3 1.5 %collective-permute-done.9.sib_b_ref = bf16[192,768]{1,0:T(8,128)(2,1)S(1)} collective-permute-done((bf16[192,768]{1,0:T(8,128)(2,1)S(1)}, bf16[192,768]{1,0:T(8,128)(2,1)S(1)}, u32[]{:S(2)}, u32[]{:S(2)}) %collective-permute-start.9) | collective-permute-done | bytes 294944 | tf_op jit(solution)/shard_map/ppermute | solution.py:221
  23.9 1.0 %shard_map.89 = (f32[256,512]{1,0:T(8,128)S(1)}, f32[8,64]{1,0:T(8,128)S(1)}) custom-call(f32[256,512]{1,0:T(8,128)S(1)} %get-tuple-element.18.total_ref, bf16[64,768]{1,0:T(8,128)(2,1)S(1)} %collective-permute-done.4.z2_ref, bf16[64,768]{1,0:T(8,128)(2,1)S(1)} %collective-permute-done.6.a_ref.z3_ref, ...), custom_call_target="tpu_custom_call" | custom-call | flops 402653184 | bytes 5755904 | tf_op jit(solution)/shard_map/pallas_call | solution.py:22
  24.8 0.7 %collective-permute-start.12 = (f32[8,64]{1,0:T(8,128)S(1)}, f32[8,64]{1,0:T(8,128)S(1)}, u32[]{:S(2)}, u32[]{:S(2)}) collective-permute-start(f32[8,64]{1,0:T(8,128)S(1)} %get-tuple-element.28), channel_id=1, source_target_pairs={{0,12},{1,13},{2,14},{3,15},{4,8},{5,9},{6,10},{7,11},{8,4},{9,5},... | collective-permute-start | bytes 6152 | tf_op jit(solution)/shard_map/ppermute | solution.py:221
  25.6 1.1 %collective-permute-start.11 = (f32[8,64]{1,0:T(8,128)S(1)}, f32[8,64]{1,0:T(8,128)S(1)}, u32[]{:S(2)}, u32[]{:S(2)}) collective-permute-start(f32[8,64]{1,0:T(8,128)S(1)} %get-tuple-element.28), channel_id=1, source_target_pairs={{0,8},{1,9},{2,10},{3,11},{4,12},{5,13},{6,14},{7,15},{8,0},{9,1},... | collective-permute-start | bytes 6152 | tf_op jit(solution)/shard_map/ppermute | solution.py:221
  26.8 1.2 %collective-permute-done.12 = f32[8,64]{1,0:T(8,128)S(1)} collective-permute-done((f32[8,64]{1,0:T(8,128)S(1)}, f32[8,64]{1,0:T(8,128)S(1)}, u32[]{:S(2)}, u32[]{:S(2)}) %collective-permute-start.12) | collective-permute-done | bytes 2080 | tf_op jit(solution)/shard_map/ppermute | solution.py:221
  27.9 1.2 %collective-permute-done.11 = f32[8,64]{1,0:T(8,128)S(1)} collective-permute-done((f32[8,64]{1,0:T(8,128)S(1)}, f32[8,64]{1,0:T(8,128)S(1)}, u32[]{:S(2)}, u32[]{:S(2)}) %collective-permute-start.11) | collective-permute-done | bytes 2080 | tf_op jit(solution)/shard_map/ppermute | solution.py:221
  29.2 1.6 %collective-permute-start.15 = (f32[8,64]{1,0:T(8,128)S(1)}, f32[8,64]{1,0:T(8,128)S(1)}, u32[]{:S(2)}, u32[]{:S(2)}) collective-permute-start(f32[8,64]{1,0:T(8,128)S(1)} %add_add_fusion.a_ref), channel_id=1, source_target_pairs={{0,3},{1,2},{2,1},{3,0},{4,7},{5,6},{6,5},{7,4},{8,11},{9,10},{10,... | collective-permute-start | bytes 6152 | tf_op jit(solution)/shard_map/ppermute | solution.py:221
  30.8 1.1 %collective-permute-start.14 = (f32[8,64]{1,0:T(8,128)S(1)}, f32[8,64]{1,0:T(8,128)S(1)}, u32[]{:S(2)}, u32[]{:S(2)}) collective-permute-start(f32[8,64]{1,0:T(8,128)S(1)} %add_add_fusion.a_ref), channel_id=1, source_target_pairs={{0,2},{1,3},{2,0},{3,1},{4,6},{5,7},{6,4},{7,5},{8,10},{9,11},{10,... | collective-permute-start | bytes 6152 | tf_op jit(solution)/shard_map/ppermute | solution.py:221
  31.9 1.7 %collective-permute-start.13 = (f32[8,64]{1,0:T(8,128)S(1)}, f32[8,64]{1,0:T(8,128)S(1)}, u32[]{:S(2)}, u32[]{:S(2)}) collective-permute-start(f32[8,64]{1,0:T(8,128)S(1)} %add_add_fusion.a_ref), channel_id=1, source_target_pairs={{0,1},{1,0},{2,3},{3,2},{4,5},{5,4},{6,7},{7,6},{8,9},{9,8},{10,11... | collective-permute-start | bytes 6152 | tf_op jit(solution)/shard_map/ppermute | solution.py:221
  33.7 1.0 %shard_map.90 = (bf16[256,512]{1,0:T(8,128)(2,1)}, bf16[256,512]{1,0:T(8,128)(2,1)}) custom-call(f32[256,512]{1,0:T(8,128)S(1)} %get-tuple-element.23.dh_ref, bf16[256,512]{1,0:T(8,128)(2,1)S(1)} %get-tuple-element.24.gate_ref, bf16[256,512]{1,0:T(8,128)(2,1)S(1)} %get-tuple-element.25.up_ref), custom_call_target="tpu_custom_call" | custom-call | bytes 1572864 | tf_op jit(solution)/shard_map/pallas_call | solution.py:22
  34.7 0.7 %collective-permute-done.14.c_ref = f32[8,64]{1,0:T(8,128)S(1)} collective-permute-done((f32[8,64]{1,0:T(8,128)S(1)}, f32[8,64]{1,0:T(8,128)S(1)}, u32[]{:S(2)}, u32[]{:S(2)}) %collective-permute-start.14) | collective-permute-done | bytes 2080 | tf_op jit(solution)/shard_map/ppermute | solution.py:221
  35.5 0.6 %shard_map.91 = f32[2,64]{1,0:T(2,128)} custom-call(f32[8,64]{1,0:T(8,128)S(1)} %add_add_fusion.a_ref, f32[8,64]{1,0:T(8,128)S(1)} %collective-permute-done.13.b_ref, f32[8,64]{1,0:T(8,128)S(1)} %collective-permute-done.14.c_ref, f32[8,64]{1,0:T(8,128)S(1)} %collective-permute-done.15.d_ref, f32[2,64]{1,0:T(2,128)S(1)} %bitcast.5), custom_call_target="tpu_custom_call" | custom-call | bytes 9216 | tf_op jit(solution)/shard_map/pallas_call | solution.py:22
  (24 shorter events, 1.5 us)
Async XLA Ops:
  0.6 13.2 %collective-permute-start.2 = (bf16[64,768]{1,0:T(8,128)(2,1)}, bf16[64,768]{1,0:T(8,128)(2,1)S(1)}, u32[]{:S(2)}, u32[]{:S(2)}) collective-permute-start(bf16[64,768]{1,0:T(8,128)(2,1)} %rows_hbm.1), channel_id=1, source_target_pairs={{0,1},{1,0},{2,3},{3,2},{4,5},{5,4},{6,7},{7,6},{8,9},{9,8},{10,11... | collective-permute-start | bytes 294920 | tf_op jit(solution)/shard_map/ppermute | solution.py:221
  3.7 10.1 %collective-permute-start.1 = (bf16[64,768]{1,0:T(8,128)(2,1)}, bf16[64,768]{1,0:T(8,128)(2,1)S(1)}, u32[]{:S(2)}, u32[]{:S(2)}) collective-permute-start(bf16[64,768]{1,0:T(8,128)(2,1)} %rows_hbm.1), channel_id=1, source_target_pairs={{0,8},{1,9},{2,10},{3,11},{4,12},{5,13},{6,14},{7,15},{8,0},{9,1},... | collective-permute-start | bytes 294920 | tf_op jit(solution)/shard_map/ppermute | solution.py:221
  5.2 8.7 %collective-permute-start.4 = (bf16[64,768]{1,0:T(8,128)(2,1)}, bf16[64,768]{1,0:T(8,128)(2,1)S(1)}, u32[]{:S(2)}, u32[]{:S(2)}) collective-permute-start(bf16[64,768]{1,0:T(8,128)(2,1)} %rows_hbm.1), channel_id=1, source_target_pairs={{0,2},{1,3},{2,0},{3,1},{4,6},{5,7},{6,4},{7,5},{8,10},{9,11},{10,... | collective-permute-start | bytes 294920 | tf_op jit(solution)/shard_map/ppermute | solution.py:221
  7.8 6.0 %collective-permute-start.3 = (bf16[64,768]{1,0:T(8,128)(2,1)}, bf16[64,768]{1,0:T(8,128)(2,1)S(1)}, u32[]{:S(2)}, u32[]{:S(2)}) collective-permute-start(bf16[64,768]{1,0:T(8,128)(2,1)} %rows_hbm.1), channel_id=1, source_target_pairs={{0,9},{1,8},{2,11},{3,10},{4,13},{5,12},{6,15},{7,14},{8,1},{9,0},... | collective-permute-start | bytes 294920 | tf_op jit(solution)/shard_map/ppermute | solution.py:221
  9.0 4.8 %collective-permute-start = (bf16[16,768]{1,0:T(8,128)(2,1)S(1)}, bf16[16,768]{1,0:T(8,128)(2,1)S(1)}, u32[]{:S(2)}, u32[]{:S(2)}) collective-permute-start(bf16[16,768]{1,0:T(8,128)(2,1)S(1)} %shard_map.85.facts_ref), channel_id=1, source_target_pairs={{0,8},{1,9},{2,10},{3,11},{4,12},{5,13},{6,14},{7,15},{8,0},{9,1},... | collective-permute-start | bytes 73736 | tf_op jit(solution)/shard_map/ppermute | solution.py:221
  13.9 3.6 %collective-permute-start.5 = (bf16[352,768]{1,0:T(8,128)(2,1)S(1)}, bf16[352,768]{1,0:T(8,128)(2,1)S(1)}, u32[]{:S(2)}, u32[]{:S(2)}) collective-permute-start(bf16[352,768]{1,0:T(8,128)(2,1)S(1)} %constant_dynamic-update-slice_fusion), channel_id=1, source_target_pairs={{0,4},{1,5},{2,6},{3,7},{4,0},{5,1},{6,2},{7,3},{8,12},{9,13},{10,... | collective-permute-start | bytes 1622024 | tf_op jit(solution)/shard_map/ppermute | solution.py:221
  14.0 6.6 %collective-permute-start.8 = (bf16[64,768]{1,0:T(8,128)(2,1)S(1)}, bf16[64,768]{1,0:T(8,128)(2,1)S(1)}, u32[]{:S(2)}, u32[]{:S(2)}) collective-permute-start(bf16[64,768]{1,0:T(8,128)(2,1)S(1)} %collective-permute-done.4.z2_ref), channel_id=1, source_target_pairs={{0,9},{1,8},{2,11},{3,10},{4,13},{5,12},{6,15},{7,14},{8,1},{9,0},... | collective-permute-start | bytes 294920 | tf_op jit(solution)/shard_map/ppermute | solution.py:221
  15.6 6.6 %collective-permute-start.7 = (bf16[64,768]{1,0:T(8,128)(2,1)S(1)}, bf16[64,768]{1,0:T(8,128)(2,1)S(1)}, u32[]{:S(2)}, u32[]{:S(2)}) collective-permute-start(bf16[64,768]{1,0:T(8,128)(2,1)S(1)} %collective-permute-done.4.z2_ref), channel_id=1, source_target_pairs={{0,8},{1,9},{2,10},{3,11},{4,12},{5,13},{6,14},{7,15},{8,0},{9,1},... | collective-permute-start | bytes 294920 | tf_op jit(solution)/shard_map/ppermute | solution.py:221
  16.1 6.1 %collective-permute-start.6 = (bf16[64,768]{1,0:T(8,128)(2,1)S(1)}, bf16[64,768]{1,0:T(8,128)(2,1)S(1)}, u32[]{:S(2)}, u32[]{:S(2)}) collective-permute-start(bf16[64,768]{1,0:T(8,128)(2,1)S(1)} %collective-permute-done.4.z2_ref), channel_id=1, source_target_pairs={{0,1},{1,0},{2,3},{3,2},{4,5},{5,4},{6,7},{7,6},{8,9},{9,8},{10,11... | collective-permute-start | bytes 294920 | tf_op jit(solution)/shard_map/ppermute | solution.py:221
  22.2 1.6 %collective-permute-start.9 = (bf16[192,768]{1,0:T(8,128)(2,1)S(1)}, bf16[192,768]{1,0:T(8,128)(2,1)S(1)}, u32[]{:S(2)}, u32[]{:S(2)}) collective-permute-start(bf16[192,768]{1,0:T(8,128)(2,1)S(1)} %shard_map.88), channel_id=1, source_target_pairs={{0,4},{1,5},{2,6},{3,7},{4,0},{5,1},{6,2},{7,3},{8,12},{9,13},{10,... | collective-permute-start | bytes 884744 | tf_op jit(solution)/shard_map/ppermute | solution.py:221
  23.9 11.7 %copy-start = (f32[64,2]{0,1:T(2,128)S(1)}, f32[64,2]{0,1:T(2,128)}, u32[]{:S(2)}) copy-start(f32[64,2]{0,1:T(2,128)} %param.7) | copy-start | bytes 1540
  24.8 3.1 %collective-permute-start.12 = (f32[8,64]{1,0:T(8,128)S(1)}, f32[8,64]{1,0:T(8,128)S(1)}, u32[]{:S(2)}, u32[]{:S(2)}) collective-permute-start(f32[8,64]{1,0:T(8,128)S(1)} %get-tuple-element.28), channel_id=1, source_target_pairs={{0,12},{1,13},{2,14},{3,15},{4,8},{5,9},{6,10},{7,11},{8,4},{9,5},... | collective-permute-start | bytes 6152 | tf_op jit(solution)/shard_map/ppermute | solution.py:221
  25.6 3.6 %collective-permute-start.11 = (f32[8,64]{1,0:T(8,128)S(1)}, f32[8,64]{1,0:T(8,128)S(1)}, u32[]{:S(2)}, u32[]{:S(2)}) collective-permute-start(f32[8,64]{1,0:T(8,128)S(1)} %get-tuple-element.28), channel_id=1, source_target_pairs={{0,8},{1,9},{2,10},{3,11},{4,12},{5,13},{6,14},{7,15},{8,0},{9,1},... | collective-permute-start | bytes 6152 | tf_op jit(solution)/shard_map/ppermute | solution.py:221
  26.7 2.5 %collective-permute-start.10 = (f32[8,64]{1,0:T(8,128)S(1)}, f32[8,64]{1,0:T(8,128)S(1)}, u32[]{:S(2)}, u32[]{:S(2)}) collective-permute-start(f32[8,64]{1,0:T(8,128)S(1)} %get-tuple-element.28), channel_id=1, source_target_pairs={{0,4},{1,5},{2,6},{3,7},{4,0},{5,1},{6,2},{7,3},{8,12},{9,13},{10,... | collective-permute-start | bytes 6152 | tf_op jit(solution)/shard_map/ppermute | solution.py:221
  29.2 5.5 %collective-permute-start.15 = (f32[8,64]{1,0:T(8,128)S(1)}, f32[8,64]{1,0:T(8,128)S(1)}, u32[]{:S(2)}, u32[]{:S(2)}) collective-permute-start(f32[8,64]{1,0:T(8,128)S(1)} %add_add_fusion.a_ref), channel_id=1, source_target_pairs={{0,3},{1,2},{2,1},{3,0},{4,7},{5,6},{6,5},{7,4},{8,11},{9,10},{10,... | collective-permute-start | bytes 6152 | tf_op jit(solution)/shard_map/ppermute | solution.py:221
  30.8 4.5 %collective-permute-start.14 = (f32[8,64]{1,0:T(8,128)S(1)}, f32[8,64]{1,0:T(8,128)S(1)}, u32[]{:S(2)}, u32[]{:S(2)}) collective-permute-start(f32[8,64]{1,0:T(8,128)S(1)} %add_add_fusion.a_ref), channel_id=1, source_target_pairs={{0,2},{1,3},{2,0},{3,1},{4,6},{5,7},{6,4},{7,5},{8,10},{9,11},{10,... | collective-permute-start | bytes 6152 | tf_op jit(solution)/shard_map/ppermute | solution.py:221
  31.9 3.6 %collective-permute-start.13 = (f32[8,64]{1,0:T(8,128)S(1)}, f32[8,64]{1,0:T(8,128)S(1)}, u32[]{:S(2)}, u32[]{:S(2)}) collective-permute-start(f32[8,64]{1,0:T(8,128)S(1)} %add_add_fusion.a_ref), channel_id=1, source_target_pairs={{0,1},{1,0},{2,3},{3,2},{4,5},{5,4},{6,7},{7,6},{8,9},{9,8},{10,11... | collective-permute-start | bytes 6152 | tf_op jit(solution)/shard_map/ppermute | solution.py:221

commit v3 on v2

--- a/solution.py
+++ b/solution.py
@@ -76,7 +76,7 @@
     copies[3].wait()
 
 
-def bundle_kernel(a_ref, b_ref, c_ref, order_ref, out_ref):
+def bundle_kernel(a_ref, b_ref, c_ref, out_ref):
     tokens = a_ref.shape[0]
     out_ref[:tokens, :] = a_ref[...]
     out_ref[tokens : 2 * tokens, :] = b_ref[...]
@@ -98,21 +98,22 @@
     tokens, width = z1_ref.shape
     long = tokens + META
     groups = total_ref.shape[0] // tokens
-    sib_z1 = long + META
-    sib_x = sib_z1 + tokens
-    sib_d1 = sib_x + tokens
+    sib_d1 = long + tokens
+    sib_x = sib_d1 + tokens
+    sib_z1 = sib_x + tokens
+    sib_facts = sib_z1 + tokens
     place_rows(
         rows_s, 0,
-        (own_ref[:tokens, :], sib_ref[:tokens, :], x_ref[...], sib_ref[sib_x:sib_d1, :]),
+        (own_ref[:tokens, :], sib_ref[:tokens, :], x_ref[...], sib_ref[sib_x : sib_x + tokens, :]),
         mine, tokens,
     )
     place_rows(
         rows_s, 1,
-        (z1_ref[...], sib_ref[sib_z1:sib_x, :], d1_ref[...], sib_ref[sib_d1 : sib_d1 + tokens, :]),
+        (z1_ref[...], sib_ref[sib_z1 : sib_z1 + tokens, :], d1_ref[...], sib_ref[sib_d1 : sib_d1 + tokens, :]),
         mine, tokens,
     )
     for other, (ref, start) in enumerate(
-        ((own_ref, tokens), (sib_ref, tokens), (x_facts_ref, 0), (sib_ref, long))
+        ((own_ref, tokens), (sib_ref, tokens), (x_facts_ref, 0), (sib_ref, sib_facts))
     ):
         facts_s[mine ^ other] = ref[start : start + META, :tokens].astype(F32)
     total = None
@@ -155,10 +156,10 @@
     mine, deep = lax.axis_index("expert"), lax.axis_index("etp")
     tokens, width = z2_ref.shape
     groups = total_ref.shape[0] // tokens
-    last = sib_a_ref.shape[0] - tokens
+    first = tokens + META
     place_rows(
         rows_s, 0,
-        (z2_ref[...], sib_a_ref[last:, :], x2_ref[...], sib_b_ref[tokens : 2 * tokens, :]),
+        (z2_ref[...], sib_a_ref[first : first + tokens, :], x2_ref[...], sib_b_ref[tokens : 2 * tokens, :]),
         mine, tokens,
     )
     place_rows(
@@ -255,7 +256,7 @@
     z3 = swap(z2, 0, 0, 1)
     x2 = swap(z2, 1, 0, 0)
     d3 = swap(z2, 1, 0, 1)
-    sib_a = swap(jnp.concatenate([own, x_facts, z1, xo, d1, z2], axis=0), 0, 1, 0)
+    sib_a = swap(jnp.concatenate([own, z2, d1, xo, z1, x_facts], axis=0), 0, 1, 0)
     half_flops = 2 * rows * hidden * width * 2
     total, place, chosen, row_weight = call(
         first_kernel,
@@ -272,7 +273,8 @@
     (bundle,) = call(
         bundle_kernel,
         [jax.ShapeDtypeStruct((3 * tokens, width), BF16)],
-        [z3, x2, d3, chosen],
+        [z3, x2, d3],
+        flops=4 * 10**9,
     )
     sib_b = swap(bundle, 0, 1, 0)
     dh, share = call(
@@ -285,8 +287,8 @@
         scratch=[pltpu.VMEM((2, rows, width), BF16)],
         flops=half_flops,
     )
-    share = share + swap(share, 0, 1, 0) + swap(share, 1, 0, 0) + swap(share, 1, 1, 0)
-    pieces = [share] + [swap(share, 0, 0, dz) for dz in range(1, deep)]
+    share = share + swap(share, 0, 0, 1) + swap(share, 0, 0, 2) + swap(share, 0, 0, 3)
+    pieces = [share, swap(share, 0, 1, 0), swap(share, 1, 0, 0), swap(share, 1, 1, 0)]
     grad_gate, grad_up = call(
         grads_kernel,
         [jax.ShapeDtypeStruct((rows, hidden), BF16)] * 2,

time: 36.3 us -> 33.7 us (0.928)
  waiting for transfers between devices: 9.98 us -> 7.29 us
    ppermute x16, waiting for transfers between devices: 9.98 us -> 7.29 us  [swap(): lax.ppermute(value, ('expert', 'etp'), [(i, i ^ mask) for i in range(slot...]
  transfers between devices with their start and end apart: 16 -> 16, of which waited for: 8 -> 9; matrix products, arithmetic and copies ran while one was open for 0% -> 0% of each run, Pallas kernels for 13% -> 14%
where the time goes in v3:
time: 33.7 us; the launch traced here: 33.5 us
  starting transfers between devices  19.3 us (57%)
  waiting for transfers between devices  7.29 us (22%)
  Pallas kernels  6.09 us (18%)
  between operations  0.75 us (2%)
    ppermute x16, starting transfers between devices, swap(): lax.ppermute(value, ('expert', 'etp'), [(i, i ^ mask) for i in range(slot...  19.3 us
    ppermute x16, waiting for transfers between devices, swap(): lax.ppermute(value, ('expert', 'etp'), [(i, i ^ mask) for i in range(slot...  7.29 us
    pallas_call x7, Pallas kernels, call(): pl.pallas_call(kernel, out_shape=tuple(outs), in_specs=[HBM] * hbm + [VME...  6.09 us
  transfers between devices with their start and end apart: 16, of which 9 were waited for; matrix products, arithmetic and copies ran while one was open for 0% of the time, Pallas kernels for 14%

profile of v3, /device:TPU:0, one launch (start us, length us, event | category | flops | bytes accessed | tf_op | source)
XLA Modules:
  0.0 33.5 jit_solution(13526697958019196188)
XLA Ops:
  0.6 3.1 %collective-permute-start.2 = (bf16[64,768]{1,0:T(8,128)(2,1)}, bf16[64,768]{1,0:T(8,128)(2,1)S(1)}, u32[]{:S(2)}, u32[]{:S(2)}) collective-permute-start(bf16[64,768]{1,0:T(8,128)(2,1)} %rows_hbm.1), channel_id=1, source_target_pairs={{0,1},{1,0},{2,3},{3,2},{4,5},{5,4},{6,7},{7,6},{8,9},{9,8},{10,11... | collective-permute-start | bytes 294920 | tf_op jit(solution)/shard_map/ppermute | solution.py:222
  3.7 1.5 %collective-permute-start.1 = (bf16[64,768]{1,0:T(8,128)(2,1)}, bf16[64,768]{1,0:T(8,128)(2,1)S(1)}, u32[]{:S(2)}, u32[]{:S(2)}) collective-permute-start(bf16[64,768]{1,0:T(8,128)(2,1)} %rows_hbm.1), channel_id=1, source_target_pairs={{0,8},{1,9},{2,10},{3,11},{4,12},{5,13},{6,14},{7,15},{8,0},{9,1},... | collective-permute-start | bytes 294920 | tf_op jit(solution)/shard_map/ppermute | solution.py:222
  5.2 2.6 %collective-permute-start.4 = (bf16[64,768]{1,0:T(8,128)(2,1)}, bf16[64,768]{1,0:T(8,128)(2,1)S(1)}, u32[]{:S(2)}, u32[]{:S(2)}) collective-permute-start(bf16[64,768]{1,0:T(8,128)(2,1)} %rows_hbm.1), channel_id=1, source_target_pairs={{0,2},{1,3},{2,0},{3,1},{4,6},{5,7},{6,4},{7,5},{8,10},{9,11},{10,... | collective-permute-start | bytes 294920 | tf_op jit(solution)/shard_map/ppermute | solution.py:222
  8.2 0.7 %shard_map.85.facts_ref = bf16[16,768]{1,0:T(8,128)(2,1)S(1)} custom-call(f32[2,64]{1,0:T(2,128)} %bitcast.4, s32[2,64]{1,0:T(2,128)} %bitcast.8), custom_call_target="tpu_custom_call" | custom-call | bytes 25600 | tf_op jit(solution)/shard_map/pallas_call | solution.py:22
  9.0 1.6 %collective-permute-start = (bf16[16,768]{1,0:T(8,128)(2,1)S(1)}, bf16[16,768]{1,0:T(8,128)(2,1)S(1)}, u32[]{:S(2)}, u32[]{:S(2)}) collective-permute-start(bf16[16,768]{1,0:T(8,128)(2,1)S(1)} %shard_map.85.facts_ref), channel_id=1, source_target_pairs={{0,8},{1,9},{2,10},{3,11},{4,12},{5,13},{6,14},{7,15},{8,0},{9,1},... | collective-permute-start | bytes 73736 | tf_op jit(solution)/shard_map/ppermute | solution.py:222
  10.5 2.1 %shard_map.86 = (bf16[512,3072]{1,0:T(8,128)(2,1)S(1)}, bf16[256,512]{1,0:T(8,128)(2,1)S(1)}, bf16[256,512]{1,0:T(8,128)(2,1)S(1)}, bf16[256,512]{1,0:T(8,128)(2,1)S(1)}, bf16[80,768]{1,0:T(8,128)(2,1)S(1)}) custom-call(bf16[512,3072]{1,0:T(8,128)(2,1)} %bitcast.6, bf16[256,512]{1,0:T(8,128)(2,1)} %gate_hbm.1, bf16[256,512]{1,0:T(8,128)(2,1)} %up_hbm.1, ...), custom_call_target="tpu_custom_call" | custom-call | bytes 7847936 | tf_op jit(solution)/shard_map/pallas_call | solution.py:22
  12.6 1.6 %collective-permute-start.8 = (bf16[64,768]{1,0:T(8,128)(2,1)S(1)}, bf16[64,768]{1,0:T(8,128)(2,1)S(1)}, u32[]{:S(2)}, u32[]{:S(2)}) collective-permute-start(bf16[64,768]{1,0:T(8,128)(2,1)S(1)} %collective-permute-done.4.z2_ref), channel_id=1, source_target_pairs={{0,9},{1,8},{2,11},{3,10},{4,13},{5,12},{6,15},{7,14},{8,1},{9,0},... | collective-permute-start | bytes 294920 | tf_op jit(solution)/shard_map/ppermute | solution.py:222
  14.3 1.6 %collective-permute-start.7 = (bf16[64,768]{1,0:T(8,128)(2,1)S(1)}, bf16[64,768]{1,0:T(8,128)(2,1)S(1)}, u32[]{:S(2)}, u32[]{:S(2)}) collective-permute-start(bf16[64,768]{1,0:T(8,128)(2,1)S(1)} %collective-permute-done.4.z2_ref), channel_id=1, source_target_pairs={{0,8},{1,9},{2,10},{3,11},{4,12},{5,13},{6,14},{7,15},{8,0},{9,1},... | collective-permute-start | bytes 294920 | tf_op jit(solution)/shard_map/ppermute | solution.py:222
  15.8 0.5 %collective-permute-start.6 = (bf16[64,768]{1,0:T(8,128)(2,1)S(1)}, bf16[64,768]{1,0:T(8,128)(2,1)S(1)}, u32[]{:S(2)}, u32[]{:S(2)}) collective-permute-start(bf16[64,768]{1,0:T(8,128)(2,1)S(1)} %collective-permute-done.4.z2_ref), channel_id=1, source_target_pairs={{0,1},{1,0},{2,3},{3,2},{4,5},{5,4},{6,7},{7,6},{8,9},{9,8},{10,11... | collective-permute-start | bytes 294920 | tf_op jit(solution)/shard_map/ppermute | solution.py:222
  16.5 2.0 %collective-permute-done.8.c_ref.d3_ref = bf16[64,768]{1,0:T(8,128)(2,1)S(1)} collective-permute-done((bf16[64,768]{1,0:T(8,128)(2,1)S(1)}, bf16[64,768]{1,0:T(8,128)(2,1)S(1)}, u32[]{:S(2)}, u32[]{:S(2)}) %collective-permute-start.8) | collective-permute-done | bytes 98336 | tf_op jit(solution)/shard_map/ppermute | solution.py:222
  18.5 1.0 %collective-permute-done.7.b_ref.x2_ref = bf16[64,768]{1,0:T(8,128)(2,1)S(1)} collective-permute-done((bf16[64,768]{1,0:T(8,128)(2,1)S(1)}, bf16[64,768]{1,0:T(8,128)(2,1)S(1)}, u32[]{:S(2)}, u32[]{:S(2)}) %collective-permute-start.7) | collective-permute-done | bytes 98336 | tf_op jit(solution)/shard_map/ppermute | solution.py:222
  19.5 1.0 %collective-permute-done.6.a_ref.z3_ref = bf16[64,768]{1,0:T(8,128)(2,1)S(1)} collective-permute-done((bf16[64,768]{1,0:T(8,128)(2,1)S(1)}, bf16[64,768]{1,0:T(8,128)(2,1)S(1)}, u32[]{:S(2)}, u32[]{:S(2)}) %collective-permute-start.6) | collective-permute-done | bytes 98336 | tf_op jit(solution)/shard_map/ppermute | solution.py:222
  20.6 0.7 %shard_map.87 = (f32[256,512]{1,0:T(8,128)S(1)}, f32[4,64,64]{2,1,0:T(8,128)S(1)}, f32[8,64]{1,0:T(8,128)S(1)}, f32[256,1]{1,0:T(8,128)S(1)}) custom-call(bf16[80,768]{1,0:T(8,128)(2,1)S(1)} %get-tuple-element.16.own_ref, bf16[16,768]{1,0:T(8,128)(2,1)S(1)} %collective-permute-done.x_facts_ref, bf16[64,768]{1,0:T(8,128)(2,1)S(1)} %collective-permute-done.1.x_ref, ...), custom_call_target="tpu_custom_call" | custom-call | flops 402653184 | bytes 4721664 | tf_op jit(solution)/shard_map/pallas_call | solution.py:22
  21.4 0.8 %collective-permute-done.9.sib_b_ref = bf16[192,768]{1,0:T(8,128)(2,1)S(1)} collective-permute-done((bf16[192,768]{1,0:T(8,128)(2,1)S(1)}, bf16[192,768]{1,0:T(8,128)(2,1)S(1)}, u32[]{:S(2)}, u32[]{:S(2)}) %collective-permute-start.9) | collective-permute-done | bytes 294944 | tf_op jit(solution)/shard_map/ppermute | solution.py:222
  22.2 1.0 %shard_map.89 = (f32[256,512]{1,0:T(8,128)S(1)}, f32[8,64]{1,0:T(8,128)S(1)}) custom-call(f32[256,512]{1,0:T(8,128)S(1)} %get-tuple-element.18.total_ref, bf16[64,768]{1,0:T(8,128)(2,1)S(1)} %collective-permute-done.4.z2_ref, bf16[64,768]{1,0:T(8,128)(2,1)S(1)} %collective-permute-done.6.a_ref.z3_ref, ...), custom_call_target="tpu_custom_call" | custom-call | flops 402653184 | bytes 5755904 | tf_op jit(solution)/shard_map/pallas_call | solution.py:22
  23.2 1.3 %collective-permute-start.12 = (f32[8,64]{1,0:T(8,128)S(1)}, f32[8,64]{1,0:T(8,128)S(1)}, u32[]{:S(2)}, u32[]{:S(2)}) collective-permute-start(f32[8,64]{1,0:T(8,128)S(1)} %get-tuple-element.28), channel_id=1, source_target_pairs={{0,3},{1,2},{2,1},{3,0},{4,7},{5,6},{6,5},{7,4},{8,11},{9,10},{10,... | collective-permute-start | bytes 6152 | tf_op jit(solution)/shard_map/ppermute | solution.py:222
  24.4 0.7 %collective-permute-start.11 = (f32[8,64]{1,0:T(8,128)S(1)}, f32[8,64]{1,0:T(8,128)S(1)}, u32[]{:S(2)}, u32[]{:S(2)}) collective-permute-start(f32[8,64]{1,0:T(8,128)S(1)} %get-tuple-element.28), channel_id=1, source_target_pairs={{0,2},{1,3},{2,0},{3,1},{4,6},{5,7},{6,4},{7,5},{8,10},{9,11},{10,... | collective-permute-start | bytes 6152 | tf_op jit(solution)/shard_map/ppermute | solution.py:222
  25.2 2.5 %collective-permute-start.10 = (f32[8,64]{1,0:T(8,128)S(1)}, f32[8,64]{1,0:T(8,128)S(1)}, u32[]{:S(2)}, u32[]{:S(2)}) collective-permute-start(f32[8,64]{1,0:T(8,128)S(1)} %get-tuple-element.28), channel_id=1, source_target_pairs={{0,1},{1,0},{2,3},{3,2},{4,5},{5,4},{6,7},{7,6},{8,9},{9,8},{10,11... | collective-permute-start | bytes 6152 | tf_op jit(solution)/shard_map/ppermute | solution.py:222
  27.6 1.0 %collective-permute-done.12 = f32[8,64]{1,0:T(8,128)S(1)} collective-permute-done((f32[8,64]{1,0:T(8,128)S(1)}, f32[8,64]{1,0:T(8,128)S(1)}, u32[]{:S(2)}, u32[]{:S(2)}) %collective-permute-start.12) | collective-permute-done | bytes 2080 | tf_op jit(solution)/shard_map/ppermute | solution.py:222
  29.2 0.6 %collective-permute-start.14 = (f32[8,64]{1,0:T(8,128)S(1)}, f32[8,64]{1,0:T(8,128)S(1)}, u32[]{:S(2)}, u32[]{:S(2)}) collective-permute-start(f32[8,64]{1,0:T(8,128)S(1)} %add_add_fusion.a_ref), channel_id=1, source_target_pairs={{0,8},{1,9},{2,10},{3,11},{4,12},{5,13},{6,14},{7,15},{8,0},{9,1},... | collective-permute-start | bytes 6152 | tf_op jit(solution)/shard_map/ppermute | solution.py:222
  29.9 1.2 %collective-permute-start.13 = (f32[8,64]{1,0:T(8,128)S(1)}, f32[8,64]{1,0:T(8,128)S(1)}, u32[]{:S(2)}, u32[]{:S(2)}) collective-permute-start(f32[8,64]{1,0:T(8,128)S(1)} %add_add_fusion.a_ref), channel_id=1, source_target_pairs={{0,4},{1,5},{2,6},{3,7},{4,0},{5,1},{6,2},{7,3},{8,12},{9,13},{10,... | collective-permute-start | bytes 6152 | tf_op jit(solution)/shard_map/ppermute | solution.py:222
  31.1 1.0 %shard_map.90 = (bf16[256,512]{1,0:T(8,128)(2,1)}, bf16[256,512]{1,0:T(8,128)(2,1)}) custom-call(f32[256,512]{1,0:T(8,128)S(1)} %get-tuple-element.23.dh_ref, bf16[256,512]{1,0:T(8,128)(2,1)S(1)} %get-tuple-element.24.gate_ref, bf16[256,512]{1,0:T(8,128)(2,1)S(1)} %get-tuple-element.25.up_ref), custom_call_target="tpu_custom_call" | custom-call | bytes 1572864 | tf_op jit(solution)/shard_map/pallas_call | solution.py:22
  32.2 0.6 %collective-permute-done.14.c_ref = f32[8,64]{1,0:T(8,128)S(1)} collective-permute-done((f32[8,64]{1,0:T(8,128)S(1)}, f32[8,64]{1,0:T(8,128)S(1)}, u32[]{:S(2)}, u32[]{:S(2)}) %collective-permute-start.14) | collective-permute-done | bytes 2080 | tf_op jit(solution)/shard_map/ppermute | solution.py:222
  32.9 0.6 %shard_map.91 = f32[2,64]{1,0:T(2,128)} custom-call(f32[8,64]{1,0:T(8,128)S(1)} %add_add_fusion.a_ref, f32[8,64]{1,0:T(8,128)S(1)} %collective-permute-done.13.b_ref, f32[8,64]{1,0:T(8,128)S(1)} %collective-permute-done.14.c_ref, f32[8,64]{1,0:T(8,128)S(1)} %collective-permute-done.15.d_ref, f32[2,64]{1,0:T(2,128)S(1)} %bitcast.5), custom_call_target="tpu_custom_call" | custom-call | bytes 9216 | tf_op jit(solution)/shard_map/pallas_call | solution.py:22
  (24 shorter events, 1.4 us)
Async XLA Ops:
  0.6 15.7 %collective-permute-start.2 = (bf16[64,768]{1,0:T(8,128)(2,1)}, bf16[64,768]{1,0:T(8,128)(2,1)S(1)}, u32[]{:S(2)}, u32[]{:S(2)}) collective-permute-start(bf16[64,768]{1,0:T(8,128)(2,1)} %rows_hbm.1), channel_id=1, source_target_pairs={{0,1},{1,0},{2,3},{3,2},{4,5},{5,4},{6,7},{7,6},{8,9},{9,8},{10,11... | collective-permute-start | bytes 294920 | tf_op jit(solution)/shard_map/ppermute | solution.py:222
  3.7 12.1 %collective-permute-start.1 = (bf16[64,768]{1,0:T(8,128)(2,1)}, bf16[64,768]{1,0:T(8,128)(2,1)S(1)}, u32[]{:S(2)}, u32[]{:S(2)}) collective-permute-start(bf16[64,768]{1,0:T(8,128)(2,1)} %rows_hbm.1), channel_id=1, source_target_pairs={{0,8},{1,9},{2,10},{3,11},{4,12},{5,13},{6,14},{7,15},{8,0},{9,1},... | collective-permute-start | bytes 294920 | tf_op jit(solution)/shard_map/ppermute | solution.py:222
  5.2 7.4 %collective-permute-start.4 = (bf16[64,768]{1,0:T(8,128)(2,1)}, bf16[64,768]{1,0:T(8,128)(2,1)S(1)}, u32[]{:S(2)}, u32[]{:S(2)}) collective-permute-start(bf16[64,768]{1,0:T(8,128)(2,1)} %rows_hbm.1), channel_id=1, source_target_pairs={{0,2},{1,3},{2,0},{3,1},{4,6},{5,7},{6,4},{7,5},{8,10},{9,11},{10,... | collective-permute-start | bytes 294920 | tf_op jit(solution)/shard_map/ppermute | solution.py:222
  7.8 6.5 %collective-permute-start.3 = (bf16[64,768]{1,0:T(8,128)(2,1)}, bf16[64,768]{1,0:T(8,128)(2,1)S(1)}, u32[]{:S(2)}, u32[]{:S(2)}) collective-permute-start(bf16[64,768]{1,0:T(8,128)(2,1)} %rows_hbm.1), channel_id=1, source_target_pairs={{0,9},{1,8},{2,11},{3,10},{4,13},{5,12},{6,15},{7,14},{8,1},{9,0},... | collective-permute-start | bytes 294920 | tf_op jit(solution)/shard_map/ppermute | solution.py:222
  9.0 7.4 %collective-permute-start = (bf16[16,768]{1,0:T(8,128)(2,1)S(1)}, bf16[16,768]{1,0:T(8,128)(2,1)S(1)}, u32[]{:S(2)}, u32[]{:S(2)}) collective-permute-start(bf16[16,768]{1,0:T(8,128)(2,1)S(1)} %shard_map.85.facts_ref), channel_id=1, source_target_pairs={{0,8},{1,9},{2,10},{3,11},{4,12},{5,13},{6,14},{7,15},{8,0},{9,1},... | collective-permute-start | bytes 73736 | tf_op jit(solution)/shard_map/ppermute | solution.py:222
  12.6 5.9 %collective-permute-start.8 = (bf16[64,768]{1,0:T(8,128)(2,1)S(1)}, bf16[64,768]{1,0:T(8,128)(2,1)S(1)}, u32[]{:S(2)}, u32[]{:S(2)}) collective-permute-start(bf16[64,768]{1,0:T(8,128)(2,1)S(1)} %collective-permute-done.4.z2_ref), channel_id=1, source_target_pairs={{0,9},{1,8},{2,11},{3,10},{4,13},{5,12},{6,15},{7,14},{8,1},{9,0},... | collective-permute-start | bytes 294920 | tf_op jit(solution)/shard_map/ppermute | solution.py:222
  14.3 5.2 %collective-permute-start.7 = (bf16[64,768]{1,0:T(8,128)(2,1)S(1)}, bf16[64,768]{1,0:T(8,128)(2,1)S(1)}, u32[]{:S(2)}, u32[]{:S(2)}) collective-permute-start(bf16[64,768]{1,0:T(8,128)(2,1)S(1)} %collective-permute-done.4.z2_ref), channel_id=1, source_target_pairs={{0,8},{1,9},{2,10},{3,11},{4,12},{5,13},{6,14},{7,15},{8,0},{9,1},... | collective-permute-start | bytes 294920 | tf_op jit(solution)/shard_map/ppermute | solution.py:222
  15.8 4.7 %collective-permute-start.6 = (bf16[64,768]{1,0:T(8,128)(2,1)S(1)}, bf16[64,768]{1,0:T(8,128)(2,1)S(1)}, u32[]{:S(2)}, u32[]{:S(2)}) collective-permute-start(bf16[64,768]{1,0:T(8,128)(2,1)S(1)} %collective-permute-done.4.z2_ref), channel_id=1, source_target_pairs={{0,1},{1,0},{2,3},{3,2},{4,5},{5,4},{6,7},{7,6},{8,9},{9,8},{10,11... | collective-permute-start | bytes 294920 | tf_op jit(solution)/shard_map/ppermute | solution.py:222
  16.4 4.2 %collective-permute-start.5 = (bf16[352,768]{1,0:T(8,128)(2,1)S(1)}, bf16[352,768]{1,0:T(8,128)(2,1)S(1)}, u32[]{:S(2)}, u32[]{:S(2)}) collective-permute-start(bf16[352,768]{1,0:T(8,128)(2,1)S(1)} %constant_dynamic-update-slice_fusion), channel_id=1, source_target_pairs={{0,4},{1,5},{2,6},{3,7},{4,0},{5,1},{6,2},{7,3},{8,12},{9,13},{10,... | collective-permute-start | bytes 1622024 | tf_op jit(solution)/shard_map/ppermute | solution.py:222
  20.6 1.6 %collective-permute-start.9 = (bf16[192,768]{1,0:T(8,128)(2,1)S(1)}, bf16[192,768]{1,0:T(8,128)(2,1)S(1)}, u32[]{:S(2)}, u32[]{:S(2)}) collective-permute-start(bf16[192,768]{1,0:T(8,128)(2,1)S(1)} %shard_map.88), channel_id=1, source_target_pairs={{0,4},{1,5},{2,6},{3,7},{4,0},{5,1},{6,2},{7,3},{8,12},{9,13},{10,... | collective-permute-start | bytes 884744 | tf_op jit(solution)/shard_map/ppermute | solution.py:222
  22.2 10.7 %copy-start = (f32[64,2]{0,1:T(2,128)S(1)}, f32[64,2]{0,1:T(2,128)}, u32[]{:S(2)}) copy-start(f32[64,2]{0,1:T(2,128)} %param.7) | copy-start | bytes 1540
  23.2 5.5 %collective-permute-start.12 = (f32[8,64]{1,0:T(8,128)S(1)}, f32[8,64]{1,0:T(8,128)S(1)}, u32[]{:S(2)}, u32[]{:S(2)}) collective-permute-start(f32[8,64]{1,0:T(8,128)S(1)} %get-tuple-element.28), channel_id=1, source_target_pairs={{0,3},{1,2},{2,1},{3,0},{4,7},{5,6},{6,5},{7,4},{8,11},{9,10},{10,... | collective-permute-start | bytes 6152 | tf_op jit(solution)/shard_map/ppermute | solution.py:222
  24.4 4.5 %collective-permute-start.11 = (f32[8,64]{1,0:T(8,128)S(1)}, f32[8,64]{1,0:T(8,128)S(1)}, u32[]{:S(2)}, u32[]{:S(2)}) collective-permute-start(f32[8,64]{1,0:T(8,128)S(1)} %get-tuple-element.28), channel_id=1, source_target_pairs={{0,2},{1,3},{2,0},{3,1},{4,6},{5,7},{6,4},{7,5},{8,10},{9,11},{10,... | collective-permute-start | bytes 6152 | tf_op jit(solution)/shard_map/ppermute | solution.py:222
  25.2 4.1 %collective-permute-start.10 = (f32[8,64]{1,0:T(8,128)S(1)}, f32[8,64]{1,0:T(8,128)S(1)}, u32[]{:S(2)}, u32[]{:S(2)}) collective-permute-start(f32[8,64]{1,0:T(8,128)S(1)} %get-tuple-element.28), channel_id=1, source_target_pairs={{0,1},{1,0},{2,3},{3,2},{4,5},{5,4},{6,7},{7,6},{8,9},{9,8},{10,11... | collective-permute-start | bytes 6152 | tf_op jit(solution)/shard_map/ppermute | solution.py:222
  29.2 3.0 %collective-permute-start.15 = (f32[8,64]{1,0:T(8,128)S(1)}, f32[8,64]{1,0:T(8,128)S(1)}, u32[]{:S(2)}, u32[]{:S(2)}) collective-permute-start(f32[8,64]{1,0:T(8,128)S(1)} %add_add_fusion.a_ref), channel_id=1, source_target_pairs={{0,12},{1,13},{2,14},{3,15},{4,8},{5,9},{6,10},{7,11},{8,4},{9,5},... | collective-permute-start | bytes 6152 | tf_op jit(solution)/shard_map/ppermute | solution.py:222
  29.2 3.7 %collective-permute-start.14 = (f32[8,64]{1,0:T(8,128)S(1)}, f32[8,64]{1,0:T(8,128)S(1)}, u32[]{:S(2)}, u32[]{:S(2)}) collective-permute-start(f32[8,64]{1,0:T(8,128)S(1)} %add_add_fusion.a_ref), channel_id=1, source_target_pairs={{0,8},{1,9},{2,10},{3,11},{4,12},{5,13},{6,14},{7,15},{8,0},{9,1},... | collective-permute-start | bytes 6152 | tf_op jit(solution)/shard_map/ppermute | solution.py:222
  29.9 3.0 %collective-permute-start.13 = (f32[8,64]{1,0:T(8,128)S(1)}, f32[8,64]{1,0:T(8,128)S(1)}, u32[]{:S(2)}, u32[]{:S(2)}) collective-permute-start(f32[8,64]{1,0:T(8,128)S(1)} %add_add_fusion.a_ref), channel_id=1, source_target_pairs={{0,4},{1,5},{2,6},{3,7},{4,0},{5,1},{6,2},{7,3},{8,12},{9,13},{10,... | collective-permute-start | bytes 6152 | tf_op jit(solution)/shard_map/ppermute | solution.py:222

commit v4 on v3

--- a/solution.py
+++ b/solution.py
@@ -32,51 +32,48 @@
     )(*args)
 
 
-def facts_kernel(logits_hbm, slots_hbm, out_ref, logits_ref, slots_ref, sems):
-    meta, width = out_ref.shape
-    tokens = logits_ref.shape[1]
+def pack_kernel(rows_hbm, logits_hbm, slots_hbm, out_ref, logits_ref, slots_ref, sems):
+    tokens, width = rows_hbm.shape
     copies = [
         pltpu.make_async_copy(logits_hbm, logits_ref, sems.at[0]),
         pltpu.make_async_copy(slots_hbm, slots_ref, sems.at[1]),
+        pltpu.make_async_copy(rows_hbm, out_ref.at[pl.ds(0, tokens)], sems.at[2]),
     ]
     for copy in copies:
         copy.start()
-    for copy in copies:
-        copy.wait()
+    copies[0].wait()
+    copies[1].wait()
     first = jax.nn.sigmoid(logits_ref[0:1, :] - logits_ref[1:2, :])
     facts = jnp.concatenate(
-        [slots_ref[...].astype(F32), first, 1.0 - first, jnp.zeros((meta - 4, tokens), F32)],
+        [slots_ref[...].astype(F32), first, 1.0 - first, jnp.zeros((META - 4, tokens), F32)],
         axis=0,
     )
-    out_ref[...] = jnp.concatenate(
-        [facts, jnp.zeros((meta, width - tokens), F32)], axis=1
+    out_ref[tokens:, :] = jnp.concatenate(
+        [facts, jnp.zeros((META, width - tokens), F32)], axis=1
     ).astype(BF16)
+    copies[2].wait()
 
 
 def load_kernel(
-    weight_hbm, gate_hbm, up_hbm, rows_hbm, facts_ref,
-    weight_ref, gate_ref, up_ref, hb_ref, own_ref,
+    weight_hbm, gate_hbm, up_hbm,
+    weight_ref, gate_ref, up_ref, hb_ref,
     sems,
 ):
-    tokens = rows_hbm.shape[0]
     copies = [
         pltpu.make_async_copy(gate_hbm, gate_ref, sems.at[0]),
         pltpu.make_async_copy(up_hbm, up_ref, sems.at[1]),
         pltpu.make_async_copy(weight_hbm, weight_ref, sems.at[2]),
-        pltpu.make_async_copy(rows_hbm, own_ref.at[pl.ds(0, tokens)], sems.at[3]),
     ]
     for copy in copies:
         copy.start()
-    own_ref[tokens:, :] = facts_ref[...]
     copies[0].wait()
     copies[1].wait()
     g = gate_ref[...].astype(F32)
     hb_ref[...] = (g * jax.nn.sigmoid(g) * up_ref[...].astype(F32)).astype(BF16)
     copies[2].wait()
-    copies[3].wait()
-
-
-def bundle_kernel(a_ref, b_ref, c_ref, out_ref):
+
+
+def bundle_kernel(a_ref, b_ref, c_ref, order_ref, out_ref):
     tokens = a_ref.shape[0]
     out_ref[:tokens, :] = a_ref[...]
     out_ref[tokens : 2 * tokens, :] = b_ref[...]
@@ -90,7 +87,7 @@
 
 
 def first_kernel(
-    own_ref, x_facts_ref, x_ref, z1_ref, d1_ref, sib_ref, weight_ref,
+    z2_ref, z1_ref, d1_ref, own_ref, x_ref, sib_ref, weight_ref,
     total_ref, place_ref, chosen_ref, row_weight_ref,
     rows_s, facts_s,
 ):
@@ -99,12 +96,12 @@
     long = tokens + META
     groups = total_ref.shape[0] // tokens
     sib_d1 = long + tokens
-    sib_x = sib_d1 + tokens
-    sib_z1 = sib_x + tokens
-    sib_facts = sib_z1 + tokens
+    sib_z1 = sib_d1 + tokens
+    sib_x = sib_z1 + tokens
+    sib_facts = sib_x + tokens
     place_rows(
         rows_s, 0,
-        (own_ref[:tokens, :], sib_ref[:tokens, :], x_ref[...], sib_ref[sib_x : sib_x + tokens, :]),
+        (own_ref[:tokens, :], sib_ref[:tokens, :], x_ref[:tokens, :], sib_ref[sib_x : sib_x + tokens, :]),
         mine, tokens,
     )
     place_rows(
@@ -113,7 +110,7 @@
         mine, tokens,
     )
     for other, (ref, start) in enumerate(
-        ((own_ref, tokens), (sib_ref, tokens), (x_facts_ref, 0), (sib_ref, sib_facts))
+        ((own_ref, tokens), (sib_ref, tokens), (x_ref, tokens), (sib_ref, sib_facts))
     ):
         facts_s[mine ^ other] = ref[start : start + META, :tokens].astype(F32)
     total = None
@@ -226,37 +223,35 @@
     logits_t, slots_t = router_logits.T, slot_of.T
     z2 = swap(out_grad, 0, 0, 2)
     z1 = swap(out_grad, 0, 0, 1)
-    xo = swap(out_grad, 1, 0, 0)
-    d1 = swap(out_grad, 1, 0, 1)
-    (facts,) = call(
-        facts_kernel,
-        [jax.ShapeDtypeStruct((META, width), BF16)],
-        [logits_t, slots_t],
+    (own,) = call(
+        pack_kernel,
+        [jax.ShapeDtypeStruct((tokens + META, width), BF16)],
+        [out_grad, logits_t, slots_t],
         scratch=[
             pltpu.VMEM((2, tokens), F32),
             pltpu.VMEM((2, tokens), jnp.int32),
-            pltpu.SemaphoreType.DMA((2,)),
+            pltpu.SemaphoreType.DMA((3,)),
         ],
-        hbm=2,
-    )
-    x_facts = swap(facts, 1, 0, 0)
-    weight, gate, up, hb, own = call(
+        hbm=3,
+    )
+    xo = swap(own, 1, 0, 0)
+    d1 = swap(out_grad, 1, 0, 1)
+    weight, gate, up, hb = call(
         load_kernel,
         [
             jax.ShapeDtypeStruct(weight.shape, BF16),
             jax.ShapeDtypeStruct((rows, hidden), BF16),
             jax.ShapeDtypeStruct((rows, hidden), BF16),
             jax.ShapeDtypeStruct((rows, hidden), BF16),
-            jax.ShapeDtypeStruct((tokens + META, width), BF16),
         ],
-        [weight, gate_pre, up_pre, out_grad, facts],
-        scratch=[pltpu.SemaphoreType.DMA((4,))],
-        hbm=4,
+        [weight, gate_pre, up_pre],
+        scratch=[pltpu.SemaphoreType.DMA((3,))],
+        hbm=3,
     )
     z3 = swap(z2, 0, 0, 1)
     x2 = swap(z2, 1, 0, 0)
     d3 = swap(z2, 1, 0, 1)
-    sib_a = swap(jnp.concatenate([own, z2, d1, xo, z1, x_facts], axis=0), 0, 1, 0)
+    sib_a = swap(jnp.concatenate([own, z2, d1, z1, xo], axis=0), 0, 1, 0)
     half_flops = 2 * rows * hidden * width * 2
     total, place, chosen, row_weight = call(
         first_kernel,
@@ -266,14 +261,14 @@
             jax.ShapeDtypeStruct((2 * slots, tokens), F32),
             jax.ShapeDtypeStruct((rows, 1), F32),
         ],
-        [own, x_facts, xo, z1, d1, sib_a, weight],
+        [z2, z1, d1, own, xo, sib_a, weight],
         scratch=[pltpu.VMEM((2, rows, width), BF16), pltpu.VMEM((slots, META, tokens), F32)],
         flops=half_flops,
     )
     (bundle,) = call(
         bundle_kernel,
         [jax.ShapeDtypeStruct((3 * tokens, width), BF16)],
-        [z3, x2, d3],
+        [z3, x2, d3, hb],
         flops=4 * 10**9,
     )
     sib_b = swap(bundle, 0, 1, 0)

time: 33.7 us -> 32.6 us (0.967)
  starting transfers between devices: 19.3 us -> 17.8 us
    ppermute x16 -> x15, starting transfers between devices: 19.3 us -> 17.8 us  [swap(): lax.ppermute(value, ('expert', 'etp'), [(i, i ^ mask) for i in range(slot...]
    ppermute x16 -> x15, waiting for transfers between devices: 7.29 us -> 7.54 us  [swap(): lax.ppermute(value, ('expert', 'etp'), [(i, i ^ mask) for i in range(slot...]
  transfers between devices with their start and end apart: 16 -> 15, of which waited for: 9 -> 9; matrix products, arithmetic and copies ran while one was open for 0% -> 0% of each run, Pallas kernels for 14% -> 15%
where the time goes in v4:
time: 32.6 us; the launch traced here: 32.4 us
  starting transfers between devices  17.8 us (55%)
  waiting for transfers between devices  7.54 us (23%)
  Pallas kernels  6.31 us (19%)
  between operations  0.74 us (2%)
    ppermute x15, starting transfers between devices, swap(): lax.ppermute(value, ('expert', 'etp'), [(i, i ^ mask) for i in range(slot...  17.8 us
    ppermute x15, waiting for transfers between devices, swap(): lax.ppermute(value, ('expert', 'etp'), [(i, i ^ mask) for i in range(slot...  7.54 us
    pallas_call x7, Pallas kernels, call(): pl.pallas_call(kernel, out_shape=tuple(outs), in_specs=[HBM] * hbm + [VME...  6.31 us
  transfers between devices with their start and end apart: 15, of which 9 were waited for; matrix products, arithmetic and copies ran while one was open for 0% of the time, Pallas kernels for 15%

profile of v4, /device:TPU:0, one launch (start us, length us, event | category | flops | bytes accessed | tf_op | source)
XLA Modules:
  0.0 32.4 jit_solution(10375030664160375995)
XLA Ops:
  0.6 3.1 %collective-permute-start.1 = (bf16[64,768]{1,0:T(8,128)(2,1)}, bf16[64,768]{1,0:T(8,128)(2,1)S(1)}, u32[]{:S(2)}, u32[]{:S(2)}) collective-permute-start(bf16[64,768]{1,0:T(8,128)(2,1)} %rows_hbm.1), channel_id=1, source_target_pairs={{0,1},{1,0},{2,3},{3,2},{4,5},{5,4},{6,7},{7,6},{8,9},{9,8},{10,11... | collective-permute-start | bytes 294920 | tf_op jit(solution)/shard_map/ppermute | solution.py:219
  3.7 2.6 %collective-permute-start = (bf16[64,768]{1,0:T(8,128)(2,1)}, bf16[64,768]{1,0:T(8,128)(2,1)S(1)}, u32[]{:S(2)}, u32[]{:S(2)}) collective-permute-start(bf16[64,768]{1,0:T(8,128)(2,1)} %rows_hbm.1), channel_id=1, source_target_pairs={{0,2},{1,3},{2,0},{3,1},{4,6},{5,7},{6,4},{7,5},{8,10},{9,11},{10,... | collective-permute-start | bytes 294920 | tf_op jit(solution)/shard_map/ppermute | solution.py:219
  6.3 1.4 %collective-permute-start.2 = (bf16[64,768]{1,0:T(8,128)(2,1)}, bf16[64,768]{1,0:T(8,128)(2,1)S(1)}, u32[]{:S(2)}, u32[]{:S(2)}) collective-permute-start(bf16[64,768]{1,0:T(8,128)(2,1)} %rows_hbm.1), channel_id=1, source_target_pairs={{0,9},{1,8},{2,11},{3,10},{4,13},{5,12},{6,15},{7,14},{8,1},{9,0},... | collective-permute-start | bytes 294920 | tf_op jit(solution)/shard_map/ppermute | solution.py:219
  7.7 1.0 %shard_map.85.own_ref = bf16[80,768]{1,0:T(8,128)(2,1)S(1)} custom-call(bf16[64,768]{1,0:T(8,128)(2,1)} %rows_hbm.1, f32[2,64]{1,0:T(2,128)} %bitcast.4, s32[2,64]{1,0:T(2,128)} %bitcast.7), custom_call_target="tpu_custom_call" | custom-call | bytes 222208 | tf_op jit(solution)/shard_map/pallas_call | solution.py:22
  8.6 0.6 %collective-permute-start.3 = (bf16[80,768]{1,0:T(8,128)(2,1)S(1)}, bf16[80,768]{1,0:T(8,128)(2,1)S(1)}, u32[]{:S(2)}, u32[]{:S(2)}) collective-permute-start(bf16[80,768]{1,0:T(8,128)(2,1)S(1)} %shard_map.85.own_ref), channel_id=1, source_target_pairs={{0,8},{1,9},{2,10},{3,11},{4,12},{5,13},{6,14},{7,15},{8,0},{9,1},... | collective-permute-start | bytes 368648 | tf_op jit(solution)/shard_map/ppermute | solution.py:219
  9.2 2.1 %shard_map.86 = (bf16[512,3072]{1,0:T(8,128)(2,1)S(1)}, bf16[256,512]{1,0:T(8,128)(2,1)S(1)}, bf16[256,512]{1,0:T(8,128)(2,1)S(1)}, bf16[256,512]{1,0:T(8,128)(2,1)S(1)}) custom-call(bf16[512,3072]{1,0:T(8,128)(2,1)} %bitcast.6, bf16[256,512]{1,0:T(8,128)(2,1)} %gate_hbm.1, bf16[256,512]{1,0:T(8,128)(2,1)} %up_hbm.1), custom_call_target="tpu_custom_call" | custom-call | bytes 7602176 | tf_op jit(solution)/shard_map/pallas_call | solution.py:22
  11.4 2.6 %collective-permute-start.7 = (bf16[64,768]{1,0:T(8,128)(2,1)S(1)}, bf16[64,768]{1,0:T(8,128)(2,1)S(1)}, u32[]{:S(2)}, u32[]{:S(2)}) collective-permute-start(bf16[64,768]{1,0:T(8,128)(2,1)S(1)} %collective-permute-done.z2_ref), channel_id=1, source_target_pairs={{0,9},{1,8},{2,11},{3,10},{4,13},{5,12},{6,15},{7,14},{8,1},{9,0},... | collective-permute-start | bytes 294920 | tf_op jit(solution)/shard_map/ppermute | solution.py:219
  13.9 0.5 %collective-permute-start.6 = (bf16[64,768]{1,0:T(8,128)(2,1)S(1)}, bf16[64,768]{1,0:T(8,128)(2,1)S(1)}, u32[]{:S(2)}, u32[]{:S(2)}) collective-permute-start(bf16[64,768]{1,0:T(8,128)(2,1)S(1)} %collective-permute-done.z2_ref), channel_id=1, source_target_pairs={{0,8},{1,9},{2,10},{3,11},{4,12},{5,13},{6,14},{7,15},{8,0},{9,1},... | collective-permute-start | bytes 294920 | tf_op jit(solution)/shard_map/ppermute | solution.py:219
  15.0 1.6 %collective-permute-done.3.x_ref = bf16[80,768]{1,0:T(8,128)(2,1)S(1)} collective-permute-done((bf16[80,768]{1,0:T(8,128)(2,1)S(1)}, bf16[80,768]{1,0:T(8,128)(2,1)S(1)}, u32[]{:S(2)}, u32[]{:S(2)}) %collective-permute-start.3) | collective-permute-done | bytes 122912 | tf_op jit(solution)/shard_map/ppermute | solution.py:219
  16.7 1.0 %collective-permute-done.7.c_ref.d3_ref = bf16[64,768]{1,0:T(8,128)(2,1)S(1)} collective-permute-done((bf16[64,768]{1,0:T(8,128)(2,1)S(1)}, bf16[64,768]{1,0:T(8,128)(2,1)S(1)}, u32[]{:S(2)}, u32[]{:S(2)}) %collective-permute-start.7) | collective-permute-done | bytes 98336 | tf_op jit(solution)/shard_map/ppermute | solution.py:219
  17.7 1.1 %collective-permute-done.6.b_ref.x2_ref = bf16[64,768]{1,0:T(8,128)(2,1)S(1)} collective-permute-done((bf16[64,768]{1,0:T(8,128)(2,1)S(1)}, bf16[64,768]{1,0:T(8,128)(2,1)S(1)}, u32[]{:S(2)}, u32[]{:S(2)}) %collective-permute-start.6) | collective-permute-done | bytes 98336 | tf_op jit(solution)/shard_map/ppermute | solution.py:219
  19.3 0.7 %shard_map.87 = (f32[256,512]{1,0:T(8,128)S(1)}, f32[4,64,64]{2,1,0:T(8,128)S(1)}, f32[8,64]{1,0:T(8,128)S(1)}, f32[256,1]{1,0:T(8,128)S(1)}) custom-call(bf16[64,768]{1,0:T(8,128)(2,1)S(1)} %collective-permute-done.z2_ref, bf16[64,768]{1,0:T(8,128)(2,1)S(1)} %collective-permute-done.1.z1_ref, bf16[64,768]{1,0:T(8,128)(2,1)S(1)} %collective-permute-done.2.d1_ref, ...), custom_call_target="tpu_custom_call" | custom-call | flops 402653184 | bytes 4819968 | tf_op jit(solution)/shard_map/pallas_call | solution.py:22
  20.0 0.8 %collective-permute-done.8.sib_b_ref = bf16[192,768]{1,0:T(8,128)(2,1)S(1)} collective-permute-done((bf16[192,768]{1,0:T(8,128)(2,1)S(1)}, bf16[192,768]{1,0:T(8,128)(2,1)S(1)}, u32[]{:S(2)}, u32[]{:S(2)}) %collective-permute-start.8) | collective-permute-done | bytes 294944 | tf_op jit(solution)/shard_map/ppermute | solution.py:219
  20.8 1.0 %shard_map.89 = (f32[256,512]{1,0:T(8,128)S(1)}, f32[8,64]{1,0:T(8,128)S(1)}) custom-call(f32[256,512]{1,0:T(8,128)S(1)} %get-tuple-element.16.total_ref, bf16[64,768]{1,0:T(8,128)(2,1)S(1)} %collective-permute-done.z2_ref, bf16[64,768]{1,0:T(8,128)(2,1)S(1)} %collective-permute-done.5.a_ref.z3_ref, bf16[64,768]{1,0:T(8,128)(2,1)S(1)} %collective-permute-done.6.b_ref.x2_ref, ...), custom_call_target="tpu_custom_call" | custom-call | flops 402653184 | bytes 5755904 | tf_op jit(solution)/shard_map/pallas_call | solution.py:22
  21.8 1.8 %collective-permute-start.11 = (f32[8,64]{1,0:T(8,128)S(1)}, f32[8,64]{1,0:T(8,128)S(1)}, u32[]{:S(2)}, u32[]{:S(2)}) collective-permute-start(f32[8,64]{1,0:T(8,128)S(1)} %get-tuple-element.26), channel_id=1, source_target_pairs={{0,3},{1,2},{2,1},{3,0},{4,7},{5,6},{6,5},{7,4},{8,11},{9,10},{10,... | collective-permute-start | bytes 6152 | tf_op jit(solution)/shard_map/ppermute | solution.py:219
  23.6 0.6 %collective-permute-start.10 = (f32[8,64]{1,0:T(8,128)S(1)}, f32[8,64]{1,0:T(8,128)S(1)}, u32[]{:S(2)}, u32[]{:S(2)}) collective-permute-start(f32[8,64]{1,0:T(8,128)S(1)} %get-tuple-element.26), channel_id=1, source_target_pairs={{0,2},{1,3},{2,0},{3,1},{4,6},{5,7},{6,4},{7,5},{8,10},{9,11},{10,... | collective-permute-start | bytes 6152 | tf_op jit(solution)/shard_map/ppermute | solution.py:219
  24.2 2.1 %collective-permute-start.9 = (f32[8,64]{1,0:T(8,128)S(1)}, f32[8,64]{1,0:T(8,128)S(1)}, u32[]{:S(2)}, u32[]{:S(2)}) collective-permute-start(f32[8,64]{1,0:T(8,128)S(1)} %get-tuple-element.26), channel_id=1, source_target_pairs={{0,1},{1,0},{2,3},{3,2},{4,5},{5,4},{6,7},{7,6},{8,9},{9,8},{10,11... | collective-permute-start | bytes 6152 | tf_op jit(solution)/shard_map/ppermute | solution.py:219
  26.3 1.0 %collective-permute-done.11 = f32[8,64]{1,0:T(8,128)S(1)} collective-permute-done((f32[8,64]{1,0:T(8,128)S(1)}, f32[8,64]{1,0:T(8,128)S(1)}, u32[]{:S(2)}, u32[]{:S(2)}) %collective-permute-start.11) | collective-permute-done | bytes 2080 | tf_op jit(solution)/shard_map/ppermute | solution.py:219
  27.3 0.8 %collective-permute-done.10 = f32[8,64]{1,0:T(8,128)S(1)} collective-permute-done((f32[8,64]{1,0:T(8,128)S(1)}, f32[8,64]{1,0:T(8,128)S(1)}, u32[]{:S(2)}, u32[]{:S(2)}) %collective-permute-start.10) | collective-permute-done | bytes 2080 | tf_op jit(solution)/shard_map/ppermute | solution.py:219
  28.2 1.2 %collective-permute-start.13 = (f32[8,64]{1,0:T(8,128)S(1)}, f32[8,64]{1,0:T(8,128)S(1)}, u32[]{:S(2)}, u32[]{:S(2)}) collective-permute-start(f32[8,64]{1,0:T(8,128)S(1)} %add_add_fusion.a_ref), channel_id=1, source_target_pairs={{0,8},{1,9},{2,10},{3,11},{4,12},{5,13},{6,14},{7,15},{8,0},{9,1},... | collective-permute-start | bytes 6152 | tf_op jit(solution)/shard_map/ppermute | solution.py:219
  29.4 0.6 %collective-permute-start.12 = (f32[8,64]{1,0:T(8,128)S(1)}, f32[8,64]{1,0:T(8,128)S(1)}, u32[]{:S(2)}, u32[]{:S(2)}) collective-permute-start(f32[8,64]{1,0:T(8,128)S(1)} %add_add_fusion.a_ref), channel_id=1, source_target_pairs={{0,4},{1,5},{2,6},{3,7},{4,0},{5,1},{6,2},{7,3},{8,12},{9,13},{10,... | collective-permute-start | bytes 6152 | tf_op jit(solution)/shard_map/ppermute | solution.py:219
  30.0 1.0 %shard_map.90 = (bf16[256,512]{1,0:T(8,128)(2,1)}, bf16[256,512]{1,0:T(8,128)(2,1)}) custom-call(f32[256,512]{1,0:T(8,128)S(1)} %get-tuple-element.21.dh_ref, bf16[256,512]{1,0:T(8,128)(2,1)S(1)} %get-tuple-element.22.gate_ref, bf16[256,512]{1,0:T(8,128)(2,1)S(1)} %get-tuple-element.23.up_ref), custom_call_target="tpu_custom_call" | custom-call | bytes 1572864 | tf_op jit(solution)/shard_map/pallas_call | solution.py:22
  31.2 0.7 %collective-permute-done.13.c_ref = f32[8,64]{1,0:T(8,128)S(1)} collective-permute-done((f32[8,64]{1,0:T(8,128)S(1)}, f32[8,64]{1,0:T(8,128)S(1)}, u32[]{:S(2)}, u32[]{:S(2)}) %collective-permute-start.13) | collective-permute-done | bytes 2080 | tf_op jit(solution)/shard_map/ppermute | solution.py:219
  31.9 0.6 %shard_map.91 = f32[2,64]{1,0:T(2,128)} custom-call(f32[8,64]{1,0:T(8,128)S(1)} %add_add_fusion.a_ref, f32[8,64]{1,0:T(8,128)S(1)} %collective-permute-done.12.b_ref, f32[8,64]{1,0:T(8,128)S(1)} %collective-permute-done.13.c_ref, f32[8,64]{1,0:T(8,128)S(1)} %collective-permute-done.14.d_ref, f32[2,64]{1,0:T(2,128)S(1)} %bitcast.5), custom_call_target="tpu_custom_call" | custom-call | bytes 9216 | tf_op jit(solution)/shard_map/pallas_call | solution.py:22
  (21 shorter events, 1.5 us)
Async XLA Ops:
  0.6 14.4 %collective-permute-start.1 = (bf16[64,768]{1,0:T(8,128)(2,1)}, bf16[64,768]{1,0:T(8,128)(2,1)S(1)}, u32[]{:S(2)}, u32[]{:S(2)}) collective-permute-start(bf16[64,768]{1,0:T(8,128)(2,1)} %rows_hbm.1), channel_id=1, source_target_pairs={{0,1},{1,0},{2,3},{3,2},{4,5},{5,4},{6,7},{7,6},{8,9},{9,8},{10,11... | collective-permute-start | bytes 294920 | tf_op jit(solution)/shard_map/ppermute | solution.py:219
  3.7 7.6 %collective-permute-start = (bf16[64,768]{1,0:T(8,128)(2,1)}, bf16[64,768]{1,0:T(8,128)(2,1)S(1)}, u32[]{:S(2)}, u32[]{:S(2)}) collective-permute-start(bf16[64,768]{1,0:T(8,128)(2,1)} %rows_hbm.1), channel_id=1, source_target_pairs={{0,2},{1,3},{2,0},{3,1},{4,6},{5,7},{6,4},{7,5},{8,10},{9,11},{10,... | collective-permute-start | bytes 294920 | tf_op jit(solution)/shard_map/ppermute | solution.py:219
  6.3 8.2 %collective-permute-start.2 = (bf16[64,768]{1,0:T(8,128)(2,1)}, bf16[64,768]{1,0:T(8,128)(2,1)S(1)}, u32[]{:S(2)}, u32[]{:S(2)}) collective-permute-start(bf16[64,768]{1,0:T(8,128)(2,1)} %rows_hbm.1), channel_id=1, source_target_pairs={{0,9},{1,8},{2,11},{3,10},{4,13},{5,12},{6,15},{7,14},{8,1},{9,0},... | collective-permute-start | bytes 294920 | tf_op jit(solution)/shard_map/ppermute | solution.py:219
  8.6 8.0 %collective-permute-start.3 = (bf16[80,768]{1,0:T(8,128)(2,1)S(1)}, bf16[80,768]{1,0:T(8,128)(2,1)S(1)}, u32[]{:S(2)}, u32[]{:S(2)}) collective-permute-start(bf16[80,768]{1,0:T(8,128)(2,1)S(1)} %shard_map.85.own_ref), channel_id=1, source_target_pairs={{0,8},{1,9},{2,10},{3,11},{4,12},{5,13},{6,14},{7,15},{8,0},{9,1},... | collective-permute-start | bytes 368648 | tf_op jit(solution)/shard_map/ppermute | solution.py:219
  11.4 6.3 %collective-permute-start.7 = (bf16[64,768]{1,0:T(8,128)(2,1)S(1)}, bf16[64,768]{1,0:T(8,128)(2,1)S(1)}, u32[]{:S(2)}, u32[]{:S(2)}) collective-permute-start(bf16[64,768]{1,0:T(8,128)(2,1)S(1)} %collective-permute-done.z2_ref), channel_id=1, source_target_pairs={{0,9},{1,8},{2,11},{3,10},{4,13},{5,12},{6,15},{7,14},{8,1},{9,0},... | collective-permute-start | bytes 294920 | tf_op jit(solution)/shard_map/ppermute | solution.py:219
  13.9 4.8 %collective-permute-start.6 = (bf16[64,768]{1,0:T(8,128)(2,1)S(1)}, bf16[64,768]{1,0:T(8,128)(2,1)S(1)}, u32[]{:S(2)}, u32[]{:S(2)}) collective-permute-start(bf16[64,768]{1,0:T(8,128)(2,1)S(1)} %collective-permute-done.z2_ref), channel_id=1, source_target_pairs={{0,8},{1,9},{2,10},{3,11},{4,12},{5,13},{6,14},{7,15},{8,0},{9,1},... | collective-permute-start | bytes 294920 | tf_op jit(solution)/shard_map/ppermute | solution.py:219
  14.5 4.7 %collective-permute-start.5 = (bf16[64,768]{1,0:T(8,128)(2,1)S(1)}, bf16[64,768]{1,0:T(8,128)(2,1)S(1)}, u32[]{:S(2)}, u32[]{:S(2)}) collective-permute-start(bf16[64,768]{1,0:T(8,128)(2,1)S(1)} %collective-permute-done.z2_ref), channel_id=1, source_target_pairs={{0,1},{1,0},{2,3},{3,2},{4,5},{5,4},{6,7},{7,6},{8,9},{9,8},{10,11... | collective-permute-start | bytes 294920 | tf_op jit(solution)/shard_map/ppermute | solution.py:219
  16.6 2.7 %collective-permute-start.4 = (bf16[352,768]{1,0:T(8,128)(2,1)S(1)}, bf16[352,768]{1,0:T(8,128)(2,1)S(1)}, u32[]{:S(2)}, u32[]{:S(2)}) collective-permute-start(bf16[352,768]{1,0:T(8,128)(2,1)S(1)} %constant_dynamic-update-slice_fusion), channel_id=1, source_target_pairs={{0,4},{1,5},{2,6},{3,7},{4,0},{5,1},{6,2},{7,3},{8,12},{9,13},{10,... | collective-permute-start | bytes 1622024 | tf_op jit(solution)/shard_map/ppermute | solution.py:219
  19.2 1.6 %collective-permute-start.8 = (bf16[192,768]{1,0:T(8,128)(2,1)S(1)}, bf16[192,768]{1,0:T(8,128)(2,1)S(1)}, u32[]{:S(2)}, u32[]{:S(2)}) collective-permute-start(bf16[192,768]{1,0:T(8,128)(2,1)S(1)} %shard_map.88), channel_id=1, source_target_pairs={{0,4},{1,5},{2,6},{3,7},{4,0},{5,1},{6,2},{7,3},{8,12},{9,13},{10,... | collective-permute-start | bytes 884744 | tf_op jit(solution)/shard_map/ppermute | solution.py:219
  20.8 11.0 %copy-start = (f32[64,2]{0,1:T(2,128)S(1)}, f32[64,2]{0,1:T(2,128)}, u32[]{:S(2)}) copy-start(f32[64,2]{0,1:T(2,128)} %param.7) | copy-start | bytes 1540
  21.8 5.5 %collective-permute-start.11 = (f32[8,64]{1,0:T(8,128)S(1)}, f32[8,64]{1,0:T(8,128)S(1)}, u32[]{:S(2)}, u32[]{:S(2)}) collective-permute-start(f32[8,64]{1,0:T(8,128)S(1)} %get-tuple-element.26), channel_id=1, source_target_pairs={{0,3},{1,2},{2,1},{3,0},{4,7},{5,6},{6,5},{7,4},{8,11},{9,10},{10,... | collective-permute-start | bytes 6152 | tf_op jit(solution)/shard_map/ppermute | solution.py:219
  23.6 4.5 %collective-permute-start.10 = (f32[8,64]{1,0:T(8,128)S(1)}, f32[8,64]{1,0:T(8,128)S(1)}, u32[]{:S(2)}, u32[]{:S(2)}) collective-permute-start(f32[8,64]{1,0:T(8,128)S(1)} %get-tuple-element.26), channel_id=1, source_target_pairs={{0,2},{1,3},{2,0},{3,1},{4,6},{5,7},{6,4},{7,5},{8,10},{9,11},{10,... | collective-permute-start | bytes 6152 | tf_op jit(solution)/shard_map/ppermute | solution.py:219
  24.2 3.9 %collective-permute-start.9 = (f32[8,64]{1,0:T(8,128)S(1)}, f32[8,64]{1,0:T(8,128)S(1)}, u32[]{:S(2)}, u32[]{:S(2)}) collective-permute-start(f32[8,64]{1,0:T(8,128)S(1)} %get-tuple-element.26), channel_id=1, source_target_pairs={{0,1},{1,0},{2,3},{3,2},{4,5},{5,4},{6,7},{7,6},{8,9},{9,8},{10,11... | collective-permute-start | bytes 6152 | tf_op jit(solution)/shard_map/ppermute | solution.py:219
  28.1 3.1 %collective-permute-start.14 = (f32[8,64]{1,0:T(8,128)S(1)}, f32[8,64]{1,0:T(8,128)S(1)}, u32[]{:S(2)}, u32[]{:S(2)}) collective-permute-start(f32[8,64]{1,0:T(8,128)S(1)} %add_add_fusion.a_ref), channel_id=1, source_target_pairs={{0,12},{1,13},{2,14},{3,15},{4,8},{5,9},{6,10},{7,11},{8,4},{9,5},... | collective-permute-start | bytes 6152 | tf_op jit(solution)/shard_map/ppermute | solution.py:219
  28.2 3.7 %collective-permute-start.13 = (f32[8,64]{1,0:T(8,128)S(1)}, f32[8,64]{1,0:T(8,128)S(1)}, u32[]{:S(2)}, u32[]{:S(2)}) collective-permute-start(f32[8,64]{1,0:T(8,128)S(1)} %add_add_fusion.a_ref), channel_id=1, source_target_pairs={{0,8},{1,9},{2,10},{3,11},{4,12},{5,13},{6,14},{7,15},{8,0},{9,1},... | collective-permute-start | bytes 6152 | tf_op jit(solution)/shard_map/ppermute | solution.py:219
  29.4 2.4 %collective-permute-start.12 = (f32[8,64]{1,0:T(8,128)S(1)}, f32[8,64]{1,0:T(8,128)S(1)}, u32[]{:S(2)}, u32[]{:S(2)}) collective-permute-start(f32[8,64]{1,0:T(8,128)S(1)} %add_add_fusion.a_ref), channel_id=1, source_target_pairs={{0,4},{1,5},{2,6},{3,7},{4,0},{5,1},{6,2},{7,3},{8,12},{9,13},{10,... | collective-permute-start | bytes 6152 | tf_op jit(solution)/shard_map/ppermute | solution.py:219

commit v5 on v4

--- a/solution.py
+++ b/solution.py
@@ -87,8 +87,8 @@
 
 
 def first_kernel(
-    z2_ref, z1_ref, d1_ref, own_ref, x_ref, sib_ref, weight_ref,
-    total_ref, place_ref, chosen_ref, row_weight_ref,
+    d1_ref, z2_ref, z1_ref, own_ref, x_ref, sib_ref, weight_ref, hb_ref,
+    total_ref, token_hb_ref, place_ref, chosen_ref, row_weight_ref,
     rows_s, facts_s,
 ):
     mine, deep = lax.axis_index("expert"), lax.axis_index("etp")
@@ -139,15 +139,21 @@
         place = hit.astype(F32)
         weight = firsts[j] * facts_s[j, 2:3, :] + seconds[j] * facts_s[j, 3:4, :]
         place_ref[j] = place
+        token_hb_ref[j * tokens : (j + 1) * tokens, :] = lax.dot_general(
+            place.astype(BF16),
+            hb_ref[j * tokens : (j + 1) * tokens, :],
+            (((0,), (0,)), ((), ())),
+            preferred_element_type=F32,
+        ).astype(BF16)
         row_weight_ref[j * tokens : (j + 1) * tokens, :] = jnp.sum(
             place * weight, axis=1, keepdims=True
         )
 
 
 def second_kernel(
-    total_ref, z2_ref, z3_ref, x2_ref, d3_ref, sib_a_ref, sib_b_ref, weight_ref,
-    hb_ref, place_ref, chosen_ref, row_weight_ref,
-    dh_ref, share_ref,
+    total_ref, z2_ref, d3_ref, x2_ref, z3_ref, sib_a_ref, sib_b_ref, weight_ref,
+    token_hb_ref, chosen_ref,
+    sum_ref, share_ref,
     rows_s,
 ):
     mine, deep = lax.axis_index("expert"), lax.axis_index("etp")
@@ -170,30 +176,36 @@
         total = total + lax.dot_general(
             rows_s[index], weight_ref[:, pl.ds(start, width)], NT, preferred_element_type=F32
         )
-    sums = []
+    sum_ref[...] = total
+    same = (
+        lax.broadcasted_iota(jnp.int32, (tokens, tokens), 0)
+        == lax.broadcasted_iota(jnp.int32, (tokens, tokens), 1)
+    ).astype(F32)
+    dp = jnp.sum(token_hb_ref[...].astype(F32) * total, axis=1, keepdims=True)
+    sums = [
+        jnp.sum(same * dp[j * tokens : (j + 1) * tokens], axis=0, keepdims=True) for j in range(groups)
+    ]
+    sums = jnp.concatenate(sums, axis=0)
+    share_ref[...] = chosen_ref[...] * jnp.concatenate([sums, sums], axis=0)
+
+
+def grads_kernel(total_ref, place_ref, row_weight_ref, gate_ref, up_ref, grad_gate_ref, grad_up_ref):
+    groups, tokens, _ = place_ref.shape
     for j in range(groups):
         part = slice(j * tokens, (j + 1) * tokens)
-        place = place_ref[j]
-        place_b = place.astype(BF16)
-        high = total[part].astype(BF16)
-        low = (total[part] - high.astype(F32)).astype(BF16)
+        place_b = place_ref[j].astype(BF16)
+        total = total_ref[part, :]
+        high = total.astype(BF16)
+        low = (total - high.astype(F32)).astype(BF16)
         z = jnp.dot(place_b, high, preferred_element_type=F32) + jnp.dot(
             place_b, low, preferred_element_type=F32
         )
-        dh_ref[part, :] = row_weight_ref[part, :] * z
-        dp = jnp.sum(hb_ref[part, :].astype(F32) * z, axis=1, keepdims=True)
-        sums.append(jnp.sum(place * dp, axis=0, keepdims=True))
-    sums = jnp.concatenate(sums, axis=0)
-    share_ref[...] = chosen_ref[...] * jnp.concatenate([sums, sums], axis=0)
-
-
-def grads_kernel(dh_ref, gate_ref, up_ref, grad_gate_ref, grad_up_ref):
-    g = gate_ref[...].astype(F32)
-    u = up_ref[...].astype(F32)
-    dh = dh_ref[...]
-    sig = jax.nn.sigmoid(g)
-    grad_up_ref[...] = (dh * (g * sig)).astype(BF16)
-    grad_gate_ref[...] = (dh * u * sig * (1.0 + g * (1.0 - sig))).astype(BF16)
+        dh = row_weight_ref[part, :] * z
+        g = gate_ref[part, :].astype(F32)
+        u = up_ref[part, :].astype(F32)
+        sig = jax.nn.sigmoid(g)
+        grad_up_ref[part, :] = (dh * (g * sig)).astype(BF16)
+        grad_gate_ref[part, :] = (dh * u * sig * (1.0 + g * (1.0 - sig))).astype(BF16)
 
 
 def logits_kernel(a_ref, b_ref, c_ref, d_ref, logits_ref, out_ref, sum_s):
@@ -253,15 +265,16 @@
     d3 = swap(z2, 1, 0, 1)
     sib_a = swap(jnp.concatenate([own, z2, d1, z1, xo], axis=0), 0, 1, 0)
     half_flops = 2 * rows * hidden * width * 2
-    total, place, chosen, row_weight = call(
+    total, token_hb, place, chosen, row_weight = call(
         first_kernel,
         [
             jax.ShapeDtypeStruct((rows, hidden), F32),
+            jax.ShapeDtypeStruct((rows, hidden), BF16),
             jax.ShapeDtypeStruct((slots, tokens, tokens), F32),
             jax.ShapeDtypeStruct((2 * slots, tokens), F32),
             jax.ShapeDtypeStruct((rows, 1), F32),
         ],
-        [z2, z1, d1, own, xo, sib_a, weight],
+        [d1, z2, z1, own, xo, sib_a, weight, hb],
         scratch=[pltpu.VMEM((2, rows, width), BF16), pltpu.VMEM((slots, META, tokens), F32)],
         flops=half_flops,
     )
@@ -272,22 +285,22 @@
         flops=4 * 10**9,
     )
     sib_b = swap(bundle, 0, 1, 0)
-    dh, share = call(
+    total, share = call(
         second_kernel,
         [
             jax.ShapeDtypeStruct((rows, hidden), F32),
             jax.ShapeDtypeStruct((2 * slots, tokens), F32),
         ],
-        [total, z2, z3, x2, d3, sib_a, sib_b, weight, hb, place, chosen, row_weight],
+        [total, z2, d3, x2, z3, sib_a, sib_b, weight, token_hb, chosen],
         scratch=[pltpu.VMEM((2, rows, width), BF16)],
         flops=half_flops,
     )
-    share = share + swap(share, 0, 0, 1) + swap(share, 0, 0, 2) + swap(share, 0, 0, 3)
-    pieces = [share, swap(share, 0, 1, 0), swap(share, 1, 0, 0), swap(share, 1, 1, 0)]
+    share = share + swap(share, 0, 0, 1) + swap(share, 0, 0, 3) + swap(share, 0, 0, 2)
+    pieces = [share, swap(share, 1, 1, 0), swap(share, 1, 0, 0), swap(share, 0, 1, 0)]
     grad_gate, grad_up = call(
         grads_kernel,
         [jax.ShapeDtypeStruct((rows, hidden), BF16)] * 2,
-        [dh, gate, up],
+        [total, place, row_weight, gate, up],
     )
     (logit_grad,) = call(
         logits_kernel,

time: 32.6 us -> 32.7 us (level)
  transfers between devices with their start and end apart: 15 -> 15, of which waited for: 9 -> 7; matrix products, arithmetic and copies ran while one was open for 0% -> 0% of each run, Pallas kernels for 15% -> 16%
where the time goes in v5:
time: 32.7 us; the launch traced here: 32.5 us
  starting transfers between devices  17.8 us (54%)
  waiting for transfers between devices  7.52 us (23%)
  Pallas kernels  6.44 us (20%)
  between operations  0.75 us (2%)
    ppermute x15, starting transfers between devices, swap(): lax.ppermute(value, ('expert', 'etp'), [(i, i ^ mask) for i in range(slot...  17.8 us
    ppermute x15, waiting for transfers between devices, swap(): lax.ppermute(value, ('expert', 'etp'), [(i, i ^ mask) for i in range(slot...  7.52 us
    pallas_call x7, Pallas kernels, call(): pl.pallas_call(kernel, out_shape=tuple(outs), in_specs=[HBM] * hbm + [VME...  6.44 us
  transfers between devices with their start and end apart: 15, of which 7 were waited for; matrix products, arithmetic and copies ran while one was open for 0% of the time, Pallas kernels for 16%

profile of v5, /device:TPU:0, one launch (start us, length us, event | category | flops | bytes accessed | tf_op | source)
XLA Modules:
  0.0 32.5 jit_solution(11072719310543967943)
XLA Ops:
  0.6 4.1 %collective-permute-start.1 = (bf16[64,768]{1,0:T(8,128)(2,1)}, bf16[64,768]{1,0:T(8,128)(2,1)S(1)}, u32[]{:S(2)}, u32[]{:S(2)}) collective-permute-start(bf16[64,768]{1,0:T(8,128)(2,1)} %rows_hbm.1), channel_id=1, source_target_pairs={{0,2},{1,3},{2,0},{3,1},{4,6},{5,7},{6,4},{7,5},{8,10},{9,11},{10,... | collective-permute-start | bytes 294920 | tf_op jit(solution)/shard_map/ppermute | solution.py:231
  4.7 2.5 %collective-permute-start = (bf16[64,768]{1,0:T(8,128)(2,1)}, bf16[64,768]{1,0:T(8,128)(2,1)S(1)}, u32[]{:S(2)}, u32[]{:S(2)}) collective-permute-start(bf16[64,768]{1,0:T(8,128)(2,1)} %rows_hbm.1), channel_id=1, source_target_pairs={{0,9},{1,8},{2,11},{3,10},{4,13},{5,12},{6,15},{7,14},{8,1},{9,0},... | collective-permute-start | bytes 294920 | tf_op jit(solution)/shard_map/ppermute | solution.py:231
  7.2 0.4 %collective-permute-start.2 = (bf16[64,768]{1,0:T(8,128)(2,1)}, bf16[64,768]{1,0:T(8,128)(2,1)S(1)}, u32[]{:S(2)}, u32[]{:S(2)}) collective-permute-start(bf16[64,768]{1,0:T(8,128)(2,1)} %rows_hbm.1), channel_id=1, source_target_pairs={{0,1},{1,0},{2,3},{3,2},{4,5},{5,4},{6,7},{7,6},{8,9},{9,8},{10,11... | collective-permute-start | bytes 294920 | tf_op jit(solution)/shard_map/ppermute | solution.py:231
  7.7 1.0 %shard_map.85.own_ref = bf16[80,768]{1,0:T(8,128)(2,1)S(1)} custom-call(bf16[64,768]{1,0:T(8,128)(2,1)} %rows_hbm.1, f32[2,64]{1,0:T(2,128)} %bitcast.4, s32[2,64]{1,0:T(2,128)} %bitcast.7), custom_call_target="tpu_custom_call" | custom-call | bytes 222208 | tf_op jit(solution)/shard_map/pallas_call | solution.py:22
  8.6 0.6 %collective-permute-start.3 = (bf16[80,768]{1,0:T(8,128)(2,1)S(1)}, bf16[80,768]{1,0:T(8,128)(2,1)S(1)}, u32[]{:S(2)}, u32[]{:S(2)}) collective-permute-start(bf16[80,768]{1,0:T(8,128)(2,1)S(1)} %shard_map.85.own_ref), channel_id=1, source_target_pairs={{0,8},{1,9},{2,10},{3,11},{4,12},{5,13},{6,14},{7,15},{8,0},{9,1},... | collective-permute-start | bytes 368648 | tf_op jit(solution)/shard_map/ppermute | solution.py:231
  9.2 2.1 %shard_map.86 = (bf16[512,3072]{1,0:T(8,128)(2,1)S(1)}, bf16[256,512]{1,0:T(8,128)(2,1)S(1)}, bf16[256,512]{1,0:T(8,128)(2,1)S(1)}, bf16[256,512]{1,0:T(8,128)(2,1)S(1)}) custom-call(bf16[512,3072]{1,0:T(8,128)(2,1)} %bitcast.6, bf16[256,512]{1,0:T(8,128)(2,1)} %gate_hbm.1, bf16[256,512]{1,0:T(8,128)(2,1)} %up_hbm.1), custom_call_target="tpu_custom_call" | custom-call | bytes 7602176 | tf_op jit(solution)/shard_map/pallas_call | solution.py:22
  11.4 2.6 %collective-permute-start.5 = (bf16[64,768]{1,0:T(8,128)(2,1)S(1)}, bf16[64,768]{1,0:T(8,128)(2,1)S(1)}, u32[]{:S(2)}, u32[]{:S(2)}) collective-permute-start(bf16[64,768]{1,0:T(8,128)(2,1)S(1)} %collective-permute-done.1.z2_ref), channel_id=1, source_target_pairs={{0,9},{1,8},{2,11},{3,10},{4,13},{5,12},{6,15},{7,14},{8,1},{9,0},... | collective-permute-start | bytes 294920 | tf_op jit(solution)/shard_map/ppermute | solution.py:231
  13.9 0.5 %collective-permute-start.6 = (bf16[64,768]{1,0:T(8,128)(2,1)S(1)}, bf16[64,768]{1,0:T(8,128)(2,1)S(1)}, u32[]{:S(2)}, u32[]{:S(2)}) collective-permute-start(bf16[64,768]{1,0:T(8,128)(2,1)S(1)} %collective-permute-done.1.z2_ref), channel_id=1, source_target_pairs={{0,8},{1,9},{2,10},{3,11},{4,12},{5,13},{6,14},{7,15},{8,0},{9,1},... | collective-permute-start | bytes 294920 | tf_op jit(solution)/shard_map/ppermute | solution.py:231
  14.5 0.5 %collective-permute-start.7 = (bf16[64,768]{1,0:T(8,128)(2,1)S(1)}, bf16[64,768]{1,0:T(8,128)(2,1)S(1)}, u32[]{:S(2)}, u32[]{:S(2)}) collective-permute-start(bf16[64,768]{1,0:T(8,128)(2,1)S(1)} %collective-permute-done.1.z2_ref), channel_id=1, source_target_pairs={{0,1},{1,0},{2,3},{3,2},{4,5},{5,4},{6,7},{7,6},{8,9},{9,8},{10,11... | collective-permute-start | bytes 294920 | tf_op jit(solution)/shard_map/ppermute | solution.py:231
  15.1 2.5 %collective-permute-done.5.c_ref.d3_ref = bf16[64,768]{1,0:T(8,128)(2,1)S(1)} collective-permute-done((bf16[64,768]{1,0:T(8,128)(2,1)S(1)}, bf16[64,768]{1,0:T(8,128)(2,1)S(1)}, u32[]{:S(2)}, u32[]{:S(2)}) %collective-permute-start.5) | collective-permute-done | bytes 98336 | tf_op jit(solution)/shard_map/ppermute | solution.py:231
  17.7 1.0 %collective-permute-done.6.b_ref.x2_ref = bf16[64,768]{1,0:T(8,128)(2,1)S(1)} collective-permute-done((bf16[64,768]{1,0:T(8,128)(2,1)S(1)}, bf16[64,768]{1,0:T(8,128)(2,1)S(1)}, u32[]{:S(2)}, u32[]{:S(2)}) %collective-permute-start.6) | collective-permute-done | bytes 98336 | tf_op jit(solution)/shard_map/ppermute | solution.py:231
  18.6 0.5 %collective-permute-done.7.a_ref.z3_ref = bf16[64,768]{1,0:T(8,128)(2,1)S(1)} collective-permute-done((bf16[64,768]{1,0:T(8,128)(2,1)S(1)}, bf16[64,768]{1,0:T(8,128)(2,1)S(1)}, u32[]{:S(2)}, u32[]{:S(2)}) %collective-permute-start.7) | collective-permute-done | bytes 98336 | tf_op jit(solution)/shard_map/ppermute | solution.py:231
  19.3 0.9 %shard_map.87 = (f32[256,512]{1,0:T(8,128)S(1)}, bf16[256,512]{1,0:T(8,128)(2,1)S(1)}, f32[4,64,64]{2,1,0:T(8,128)S(1)}, f32[8,64]{1,0:T(8,128)S(1)}, f32[256,1]{1,0:T(8,128)S(1)}) custom-call(bf16[64,768]{1,0:T(8,128)(2,1)S(1)} %collective-permute-done.d1_ref, bf16[64,768]{1,0:T(8,128)(2,1)S(1)} %collective-permute-done.1.z2_ref, ...), custom_call_target="tpu_custom_call" | custom-call | flops 402653184 | bytes 5344256 | tf_op jit(solution)/shard_map/pallas_call | solution.py:22
  20.2 0.7 %collective-permute-done.8.sib_b_ref = bf16[192,768]{1,0:T(8,128)(2,1)S(1)} collective-permute-done((bf16[192,768]{1,0:T(8,128)(2,1)S(1)}, bf16[192,768]{1,0:T(8,128)(2,1)S(1)}, u32[]{:S(2)}, u32[]{:S(2)}) %collective-permute-start.8) | collective-permute-done | bytes 294944 | tf_op jit(solution)/shard_map/ppermute | solution.py:231
  20.8 0.7 %shard_map.89 = (f32[256,512]{1,0:T(8,128)S(1)}, f32[8,64]{1,0:T(8,128)S(1)}) custom-call(f32[256,512]{1,0:T(8,128)S(1)} %get-tuple-element.18.total_ref, bf16[64,768]{1,0:T(8,128)(2,1)S(1)} %collective-permute-done.1.z2_ref, bf16[64,768]{1,0:T(8,128)(2,1)S(1)} %collective-permute-done.5.c_ref.d3_ref, ...), custom_call_target="tpu_custom_call" | custom-call | flops 402653184 | bytes 5689344 | tf_op jit(solution)/shard_map/pallas_call | solution.py:22
  21.6 2.1 %collective-permute-start.10 = (f32[8,64]{1,0:T(8,128)S(1)}, f32[8,64]{1,0:T(8,128)S(1)}, u32[]{:S(2)}, u32[]{:S(2)}) collective-permute-start(f32[8,64]{1,0:T(8,128)S(1)} %get-tuple-element.28), channel_id=1, source_target_pairs={{0,3},{1,2},{2,1},{3,0},{4,7},{5,6},{6,5},{7,4},{8,11},{9,10},{10,... | collective-permute-start | bytes 6152 | tf_op jit(solution)/shard_map/ppermute | solution.py:231
  23.7 2.3 %collective-permute-start.9 = (f32[8,64]{1,0:T(8,128)S(1)}, f32[8,64]{1,0:T(8,128)S(1)}, u32[]{:S(2)}, u32[]{:S(2)}) collective-permute-start(f32[8,64]{1,0:T(8,128)S(1)} %get-tuple-element.28), channel_id=1, source_target_pairs={{0,1},{1,0},{2,3},{3,2},{4,5},{5,4},{6,7},{7,6},{8,9},{9,8},{10,11... | collective-permute-start | bytes 6152 | tf_op jit(solution)/shard_map/ppermute | solution.py:231
  26.0 1.0 %collective-permute-done.10 = f32[8,64]{1,0:T(8,128)S(1)} collective-permute-done((f32[8,64]{1,0:T(8,128)S(1)}, f32[8,64]{1,0:T(8,128)S(1)}, u32[]{:S(2)}, u32[]{:S(2)}) %collective-permute-start.10) | collective-permute-done | bytes 2080 | tf_op jit(solution)/shard_map/ppermute | solution.py:231
  27.0 1.2 %collective-permute-done.11 = f32[8,64]{1,0:T(8,128)S(1)} collective-permute-done((f32[8,64]{1,0:T(8,128)S(1)}, f32[8,64]{1,0:T(8,128)S(1)}, u32[]{:S(2)}, u32[]{:S(2)}) %collective-permute-start.11) | collective-permute-done | bytes 2080 | tf_op jit(solution)/shard_map/ppermute | solution.py:231
  28.3 0.9 %collective-permute-start.13 = (f32[8,64]{1,0:T(8,128)S(1)}, f32[8,64]{1,0:T(8,128)S(1)}, u32[]{:S(2)}, u32[]{:S(2)}) collective-permute-start(f32[8,64]{1,0:T(8,128)S(1)} %add_add_fusion.a_ref), channel_id=1, source_target_pairs={{0,8},{1,9},{2,10},{3,11},{4,12},{5,13},{6,14},{7,15},{8,0},{9,1},... | collective-permute-start | bytes 6152 | tf_op jit(solution)/shard_map/ppermute | solution.py:231
  29.2 1.0 %collective-permute-start.14 = (f32[8,64]{1,0:T(8,128)S(1)}, f32[8,64]{1,0:T(8,128)S(1)}, u32[]{:S(2)}, u32[]{:S(2)}) collective-permute-start(f32[8,64]{1,0:T(8,128)S(1)} %add_add_fusion.a_ref), channel_id=1, source_target_pairs={{0,4},{1,5},{2,6},{3,7},{4,0},{5,1},{6,2},{7,3},{8,12},{9,13},{10,... | collective-permute-start | bytes 6152 | tf_op jit(solution)/shard_map/ppermute | solution.py:231
  30.1 1.2 %shard_map.90 = (bf16[256,512]{1,0:T(8,128)(2,1)}, bf16[256,512]{1,0:T(8,128)(2,1)}) custom-call(f32[256,512]{1,0:T(8,128)S(1)} %get-tuple-element.21.total_ref, f32[4,64,64]{2,1,0:T(8,128)S(1)} %get-tuple-element.22.place_ref, f32[256,1]{1,0:T(8,128)S(1)} %get-tuple-element.23.row_weight_ref, bf16[256,512]{1,0:T(8,128)(2,1)S(1)} %get-tuple-element.24.gate_ref, ...), custom_call_target="tpu_custom_call" | custom-call | bytes 1639424 | tf_op jit(solution)/shard_map/pallas_call | solution.py:22
  31.3 0.6 %collective-permute-done.13.c_ref = f32[8,64]{1,0:T(8,128)S(1)} collective-permute-done((f32[8,64]{1,0:T(8,128)S(1)}, f32[8,64]{1,0:T(8,128)S(1)}, u32[]{:S(2)}, u32[]{:S(2)}) %collective-permute-start.13) | collective-permute-done | bytes 2080 | tf_op jit(solution)/shard_map/ppermute | solution.py:231
  32.0 0.6 %shard_map.91 = f32[2,64]{1,0:T(2,128)} custom-call(f32[8,64]{1,0:T(8,128)S(1)} %add_add_fusion.a_ref, f32[8,64]{1,0:T(8,128)S(1)} %collective-permute-done.12.b_ref, f32[8,64]{1,0:T(8,128)S(1)} %collective-permute-done.13.c_ref, f32[8,64]{1,0:T(8,128)S(1)} %collective-permute-done.14.d_ref, f32[2,64]{1,0:T(2,128)S(1)} %bitcast.5), custom_call_target="tpu_custom_call" | custom-call | bytes 9216 | tf_op jit(solution)/shard_map/pallas_call | solution.py:22
  (21 shorter events, 0.4 us)
Async XLA Ops:
  0.6 10.7 %collective-permute-start.1 = (bf16[64,768]{1,0:T(8,128)(2,1)}, bf16[64,768]{1,0:T(8,128)(2,1)S(1)}, u32[]{:S(2)}, u32[]{:S(2)}) collective-permute-start(bf16[64,768]{1,0:T(8,128)(2,1)} %rows_hbm.1), channel_id=1, source_target_pairs={{0,2},{1,3},{2,0},{3,1},{4,6},{5,7},{6,4},{7,5},{8,10},{9,11},{10,... | collective-permute-start | bytes 294920 | tf_op jit(solution)/shard_map/ppermute | solution.py:231
  4.7 9.8 %collective-permute-start = (bf16[64,768]{1,0:T(8,128)(2,1)}, bf16[64,768]{1,0:T(8,128)(2,1)S(1)}, u32[]{:S(2)}, u32[]{:S(2)}) collective-permute-start(bf16[64,768]{1,0:T(8,128)(2,1)} %rows_hbm.1), channel_id=1, source_target_pairs={{0,9},{1,8},{2,11},{3,10},{4,13},{5,12},{6,15},{7,14},{8,1},{9,0},... | collective-permute-start | bytes 294920 | tf_op jit(solution)/shard_map/ppermute | solution.py:231
  7.2 7.8 %collective-permute-start.2 = (bf16[64,768]{1,0:T(8,128)(2,1)}, bf16[64,768]{1,0:T(8,128)(2,1)S(1)}, u32[]{:S(2)}, u32[]{:S(2)}) collective-permute-start(bf16[64,768]{1,0:T(8,128)(2,1)} %rows_hbm.1), channel_id=1, source_target_pairs={{0,1},{1,0},{2,3},{3,2},{4,5},{5,4},{6,7},{7,6},{8,9},{9,8},{10,11... | collective-permute-start | bytes 294920 | tf_op jit(solution)/shard_map/ppermute | solution.py:231
  8.6 6.4 %collective-permute-start.3 = (bf16[80,768]{1,0:T(8,128)(2,1)S(1)}, bf16[80,768]{1,0:T(8,128)(2,1)S(1)}, u32[]{:S(2)}, u32[]{:S(2)}) collective-permute-start(bf16[80,768]{1,0:T(8,128)(2,1)S(1)} %shard_map.85.own_ref), channel_id=1, source_target_pairs={{0,8},{1,9},{2,10},{3,11},{4,12},{5,13},{6,14},{7,15},{8,0},{9,1},... | collective-permute-start | bytes 368648 | tf_op jit(solution)/shard_map/ppermute | solution.py:231
  11.4 6.3 %collective-permute-start.5 = (bf16[64,768]{1,0:T(8,128)(2,1)S(1)}, bf16[64,768]{1,0:T(8,128)(2,1)S(1)}, u32[]{:S(2)}, u32[]{:S(2)}) collective-permute-start(bf16[64,768]{1,0:T(8,128)(2,1)S(1)} %collective-permute-done.1.z2_ref), channel_id=1, source_target_pairs={{0,9},{1,8},{2,11},{3,10},{4,13},{5,12},{6,15},{7,14},{8,1},{9,0},... | collective-permute-start | bytes 294920 | tf_op jit(solution)/shard_map/ppermute | solution.py:231
  13.9 4.7 %collective-permute-start.6 = (bf16[64,768]{1,0:T(8,128)(2,1)S(1)}, bf16[64,768]{1,0:T(8,128)(2,1)S(1)}, u32[]{:S(2)}, u32[]{:S(2)}) collective-permute-start(bf16[64,768]{1,0:T(8,128)(2,1)S(1)} %collective-permute-done.1.z2_ref), channel_id=1, source_target_pairs={{0,8},{1,9},{2,10},{3,11},{4,12},{5,13},{6,14},{7,15},{8,0},{9,1},... | collective-permute-start | bytes 294920 | tf_op jit(solution)/shard_map/ppermute | solution.py:231
  14.5 4.7 %collective-permute-start.7 = (bf16[64,768]{1,0:T(8,128)(2,1)S(1)}, bf16[64,768]{1,0:T(8,128)(2,1)S(1)}, u32[]{:S(2)}, u32[]{:S(2)}) collective-permute-start(bf16[64,768]{1,0:T(8,128)(2,1)S(1)} %collective-permute-done.1.z2_ref), channel_id=1, source_target_pairs={{0,1},{1,0},{2,3},{3,2},{4,5},{5,4},{6,7},{7,6},{8,9},{9,8},{10,11... | collective-permute-start | bytes 294920 | tf_op jit(solution)/shard_map/ppermute | solution.py:231
  15.1 4.2 %collective-permute-start.4 = (bf16[352,768]{1,0:T(8,128)(2,1)S(1)}, bf16[352,768]{1,0:T(8,128)(2,1)S(1)}, u32[]{:S(2)}, u32[]{:S(2)}) collective-permute-start(bf16[352,768]{1,0:T(8,128)(2,1)S(1)} %constant_dynamic-update-slice_fusion), channel_id=1, source_target_pairs={{0,4},{1,5},{2,6},{3,7},{4,0},{5,1},{6,2},{7,3},{8,12},{9,13},{10,... | collective-permute-start | bytes 1622024 | tf_op jit(solution)/shard_map/ppermute | solution.py:231
  19.2 1.6 %collective-permute-start.8 = (bf16[192,768]{1,0:T(8,128)(2,1)S(1)}, bf16[192,768]{1,0:T(8,128)(2,1)S(1)}, u32[]{:S(2)}, u32[]{:S(2)}) collective-permute-start(bf16[192,768]{1,0:T(8,128)(2,1)S(1)} %shard_map.88), channel_id=1, source_target_pairs={{0,4},{1,5},{2,6},{3,7},{4,0},{5,1},{6,2},{7,3},{8,12},{9,13},{10,... | collective-permute-start | bytes 884744 | tf_op jit(solution)/shard_map/ppermute | solution.py:231
  20.8 11.1 %copy-start = (f32[64,2]{0,1:T(2,128)S(1)}, f32[64,2]{0,1:T(2,128)}, u32[]{:S(2)}) copy-start(f32[64,2]{0,1:T(2,128)} %param.7) | copy-start | bytes 1540
  21.6 5.5 %collective-permute-start.10 = (f32[8,64]{1,0:T(8,128)S(1)}, f32[8,64]{1,0:T(8,128)S(1)}, u32[]{:S(2)}, u32[]{:S(2)}) collective-permute-start(f32[8,64]{1,0:T(8,128)S(1)} %get-tuple-element.28), channel_id=1, source_target_pairs={{0,3},{1,2},{2,1},{3,0},{4,7},{5,6},{6,5},{7,4},{8,11},{9,10},{10,... | collective-permute-start | bytes 6152 | tf_op jit(solution)/shard_map/ppermute | solution.py:231
  23.7 4.5 %collective-permute-start.11 = (f32[8,64]{1,0:T(8,128)S(1)}, f32[8,64]{1,0:T(8,128)S(1)}, u32[]{:S(2)}, u32[]{:S(2)}) collective-permute-start(f32[8,64]{1,0:T(8,128)S(1)} %get-tuple-element.28), channel_id=1, source_target_pairs={{0,2},{1,3},{2,0},{3,1},{4,6},{5,7},{6,4},{7,5},{8,10},{9,11},{10,... | collective-permute-start | bytes 6152 | tf_op jit(solution)/shard_map/ppermute | solution.py:231
  23.7 4.5 %collective-permute-start.9 = (f32[8,64]{1,0:T(8,128)S(1)}, f32[8,64]{1,0:T(8,128)S(1)}, u32[]{:S(2)}, u32[]{:S(2)}) collective-permute-start(f32[8,64]{1,0:T(8,128)S(1)} %get-tuple-element.28), channel_id=1, source_target_pairs={{0,1},{1,0},{2,3},{3,2},{4,5},{5,4},{6,7},{7,6},{8,9},{9,8},{10,11... | collective-permute-start | bytes 6152 | tf_op jit(solution)/shard_map/ppermute | solution.py:231
  28.2 3.1 %collective-permute-start.12 = (f32[8,64]{1,0:T(8,128)S(1)}, f32[8,64]{1,0:T(8,128)S(1)}, u32[]{:S(2)}, u32[]{:S(2)}) collective-permute-start(f32[8,64]{1,0:T(8,128)S(1)} %add_add_fusion.a_ref), channel_id=1, source_target_pairs={{0,12},{1,13},{2,14},{3,15},{4,8},{5,9},{6,10},{7,11},{8,4},{9,5},... | collective-permute-start | bytes 6152 | tf_op jit(solution)/shard_map/ppermute | solution.py:231
  28.3 3.7 %collective-permute-start.13 = (f32[8,64]{1,0:T(8,128)S(1)}, f32[8,64]{1,0:T(8,128)S(1)}, u32[]{:S(2)}, u32[]{:S(2)}) collective-permute-start(f32[8,64]{1,0:T(8,128)S(1)} %add_add_fusion.a_ref), channel_id=1, source_target_pairs={{0,8},{1,9},{2,10},{3,11},{4,12},{5,13},{6,14},{7,15},{8,0},{9,1},... | collective-permute-start | bytes 6152 | tf_op jit(solution)/shard_map/ppermute | solution.py:231
  29.2 2.8 %collective-permute-start.14 = (f32[8,64]{1,0:T(8,128)S(1)}, f32[8,64]{1,0:T(8,128)S(1)}, u32[]{:S(2)}, u32[]{:S(2)}) collective-permute-start(f32[8,64]{1,0:T(8,128)S(1)} %add_add_fusion.a_ref), channel_id=1, source_target_pairs={{0,4},{1,5},{2,6},{3,7},{4,0},{5,1},{6,2},{7,3},{8,12},{9,13},{10,... | collective-permute-start | bytes 6152 | tf_op jit(solution)/shard_map/ppermute | solution.py:231

commit v6 on v5

--- a/solution.py
+++ b/solution.py
@@ -54,6 +54,11 @@
     copies[2].wait()
 
 
+def half_of(weight_hbm, half):
+    width = weight_hbm.shape[1] // 2
+    return weight_hbm.at[:, pl.ds(pl.multiple_of(half * width, 128), width)]
+
+
 def load_kernel(
     weight_hbm, gate_hbm, up_hbm,
     weight_ref, gate_ref, up_ref, hb_ref,
@@ -62,7 +67,7 @@
     copies = [
         pltpu.make_async_copy(gate_hbm, gate_ref, sems.at[0]),
         pltpu.make_async_copy(up_hbm, up_ref, sems.at[1]),
-        pltpu.make_async_copy(weight_hbm, weight_ref, sems.at[2]),
+        pltpu.make_async_copy(half_of(weight_hbm, lax.axis_index("etp") // 2), weight_ref, sems.at[2]),
     ]
     for copy in copies:
         copy.start()
@@ -73,7 +78,13 @@
     copies[2].wait()
 
 
-def bundle_kernel(a_ref, b_ref, c_ref, order_ref, out_ref):
+def other_kernel(weight_hbm, order_ref, weight_ref, sem):
+    copy = pltpu.make_async_copy(half_of(weight_hbm, (lax.axis_index("etp") // 2) ^ 1), weight_ref, sem)
+    copy.start()
+    copy.wait()
+
+
+def bundle_kernel(a_ref, b_ref, c_ref, order_ref, load_order_ref, out_ref):
     tokens = a_ref.shape[0]
     out_ref[:tokens, :] = a_ref[...]
     out_ref[tokens : 2 * tokens, :] = b_ref[...]
@@ -115,7 +126,7 @@
         facts_s[mine ^ other] = ref[start : start + META, :tokens].astype(F32)
     total = None
     for index in range(2):
-        start = pl.multiple_of((deep ^ index) * width, 128)
+        start = pl.multiple_of(((deep ^ index) % 2) * width, 128)
         part = lax.dot_general(
             rows_s[index], weight_ref[:, pl.ds(start, width)], NT, preferred_element_type=F32
         )
@@ -172,7 +183,7 @@
     )
     total = total_ref[...]
     for index in range(2):
-        start = pl.multiple_of((deep ^ (2 + index)) * width, 128)
+        start = pl.multiple_of(((deep ^ index) % 2) * width, 128)
         total = total + lax.dot_general(
             rows_s[index], weight_ref[:, pl.ds(start, width)], NT, preferred_element_type=F32
         )
@@ -234,7 +245,6 @@
 
     logits_t, slots_t = router_logits.T, slot_of.T
     z2 = swap(out_grad, 0, 0, 2)
-    z1 = swap(out_grad, 0, 0, 1)
     (own,) = call(
         pack_kernel,
         [jax.ShapeDtypeStruct((tokens + META, width), BF16)],
@@ -246,12 +256,14 @@
         ],
         hbm=3,
     )
+    rows_here = own[:tokens]
+    z1 = swap(rows_here, 0, 0, 1)
     xo = swap(own, 1, 0, 0)
-    d1 = swap(out_grad, 1, 0, 1)
-    weight, gate, up, hb = call(
+    d1 = swap(rows_here, 1, 0, 1)
+    weight_a, gate, up, hb = call(
         load_kernel,
         [
-            jax.ShapeDtypeStruct(weight.shape, BF16),
+            jax.ShapeDtypeStruct((hidden, 2 * width), BF16),
             jax.ShapeDtypeStruct((rows, hidden), BF16),
             jax.ShapeDtypeStruct((rows, hidden), BF16),
             jax.ShapeDtypeStruct((rows, hidden), BF16),
@@ -274,14 +286,21 @@
             jax.ShapeDtypeStruct((2 * slots, tokens), F32),
             jax.ShapeDtypeStruct((rows, 1), F32),
         ],
-        [d1, z2, z1, own, xo, sib_a, weight, hb],
+        [d1, z2, z1, own, xo, sib_a, weight_a, hb],
         scratch=[pltpu.VMEM((2, rows, width), BF16), pltpu.VMEM((slots, META, tokens), F32)],
         flops=half_flops,
+    )
+    (weight_b,) = call(
+        other_kernel,
+        [jax.ShapeDtypeStruct((hidden, 2 * width), BF16)],
+        [weight, xo],
+        scratch=[pltpu.SemaphoreType.DMA],
+        hbm=1,
     )
     (bundle,) = call(
         bundle_kernel,
         [jax.ShapeDtypeStruct((3 * tokens, width), BF16)],
-        [z3, x2, d3, hb],
+        [z3, x2, d3, weight_b, hb],
         flops=4 * 10**9,
     )
     sib_b = swap(bundle, 0, 1, 0)
@@ -291,7 +310,7 @@
             jax.ShapeDtypeStruct((rows, hidden), F32),
             jax.ShapeDtypeStruct((2 * slots, tokens), F32),
         ],
-        [total, z2, d3, x2, z3, sib_a, sib_b, weight, token_hb, chosen],
+        [total, z2, d3, x2, z3, sib_a, sib_b, weight_b, token_hb, chosen],
         scratch=[pltpu.VMEM((2, rows, width), BF16)],
         flops=half_flops,
     )

time: 32.7 us -> 32.7 us (level)
  waiting for transfers between devices: 7.52 us -> 6.58 us
  Pallas kernels: 6.44 us -> 7.36 us
    ppermute x15, waiting for transfers between devices: 7.52 us -> 6.58 us  [swap(): lax.ppermute(value, ('expert', 'etp'), [(i, i ^ mask) for i in range(slot...]
    pallas_call x7 -> x8, Pallas kernels: 6.44 us -> 7.36 us  [call(): pl.pallas_call(kernel, out_shape=tuple(outs), in_specs=[HBM] * hbm + [VME...]
  transfers between devices with their start and end apart: 15 -> 15, of which waited for: 7 -> 7; matrix products, arithmetic and copies ran while one was open for 0% -> 0% of each run, Pallas kernels for 16% -> 19%
where the time goes in v6:
time: 32.7 us; the launch traced here: 32.5 us
  starting transfers between devices  17.8 us (54%)
  Pallas kernels  7.36 us (23%)
  waiting for transfers between devices  6.58 us (20%)
  between operations  0.76 us (2%)
    ppermute x15, starting transfers between devices, swap(): lax.ppermute(value, ('expert', 'etp'), [(i, i ^ mask) for i in range(slot...  17.8 us
    pallas_call x8, Pallas kernels, call(): pl.pallas_call(kernel, out_shape=tuple(outs), in_specs=[HBM] * hbm + [VME...  7.36 us
    ppermute x15, waiting for transfers between devices, swap(): lax.ppermute(value, ('expert', 'etp'), [(i, i ^ mask) for i in range(slot...  6.58 us
  transfers between devices with their start and end apart: 15, of which 7 were waited for; matrix products, arithmetic and copies ran while one was open for 0% of the time, Pallas kernels for 19%

profile of v6, /device:TPU:0, one launch (start us, length us, event | category | flops | bytes accessed | tf_op | source)
XLA Modules:
  0.0 32.5 jit_solution(15755404290668007023)
XLA Ops:
  0.6 4.1 %collective-permute-start.1 = (bf16[64,768]{1,0:T(8,128)(2,1)}, bf16[64,768]{1,0:T(8,128)(2,1)S(1)}, u32[]{:S(2)}, u32[]{:S(2)}) collective-permute-start(bf16[64,768]{1,0:T(8,128)(2,1)} %rows_hbm.1), channel_id=1, source_target_pairs={{0,2},{1,3},{2,0},{3,1},{4,6},{5,7},{6,4},{7,5},{8,10},{9,11},{10,... | collective-permute-start | bytes 294920 | tf_op jit(solution)/shard_map/ppermute | solution.py:242
  4.7 1.0 %shard_map.85.own_ref = bf16[80,768]{1,0:T(8,128)(2,1)S(1)} custom-call(bf16[64,768]{1,0:T(8,128)(2,1)} %rows_hbm.1, f32[2,64]{1,0:T(2,128)} %bitcast.4, s32[2,64]{1,0:T(2,128)} %bitcast.8), custom_call_target="tpu_custom_call" | custom-call | bytes 222208 | tf_op jit(solution)/shard_map/pallas_call | solution.py:22
  5.7 2.6 %collective-permute-start = (bf16[64,768]{1,0:T(8,128)(2,1)S(1)}, bf16[64,768]{1,0:T(8,128)(2,1)S(1)}, u32[]{:S(2)}, u32[]{:S(2)}) collective-permute-start(bf16[64,768]{1,0:T(8,128)(2,1)S(1)} %slice.4), channel_id=1, source_target_pairs={{0,9},{1,8},{2,11},{3,10},{4,13},{5,12},{6,15},{7,14},{8,1},{9,0},... | collective-permute-start | bytes 294920 | tf_op jit(solution)/shard_map/ppermute | solution.py:242
  8.3 0.4 %collective-permute-start.2 = (bf16[64,768]{1,0:T(8,128)(2,1)S(1)}, bf16[64,768]{1,0:T(8,128)(2,1)S(1)}, u32[]{:S(2)}, u32[]{:S(2)}) collective-permute-start(bf16[64,768]{1,0:T(8,128)(2,1)S(1)} %slice.4), channel_id=1, source_target_pairs={{0,1},{1,0},{2,3},{3,2},{4,5},{5,4},{6,7},{7,6},{8,9},{9,8},{10,11... | collective-permute-start | bytes 294920 | tf_op jit(solution)/shard_map/ppermute | solution.py:242
  8.7 0.5 %collective-permute-start.3 = (bf16[80,768]{1,0:T(8,128)(2,1)S(1)}, bf16[80,768]{1,0:T(8,128)(2,1)S(1)}, u32[]{:S(2)}, u32[]{:S(2)}) collective-permute-start(bf16[80,768]{1,0:T(8,128)(2,1)S(1)} %shard_map.85.own_ref), channel_id=1, source_target_pairs={{0,8},{1,9},{2,10},{3,11},{4,12},{5,13},{6,14},{7,15},{8,0},{9,1},... | collective-permute-start | bytes 368648 | tf_op jit(solution)/shard_map/ppermute | solution.py:242
  9.3 1.6 %shard_map.86 = (bf16[512,1536]{1,0:T(8,128)(2,1)S(1)}, bf16[256,512]{1,0:T(8,128)(2,1)S(1)}, bf16[256,512]{1,0:T(8,128)(2,1)S(1)}, bf16[256,512]{1,0:T(8,128)(2,1)S(1)}) custom-call(bf16[512,3072]{1,0:T(8,128)(2,1)} %bitcast.6, bf16[256,512]{1,0:T(8,128)(2,1)} %gate_hbm.1, bf16[256,512]{1,0:T(8,128)(2,1)} %up_hbm.1), custom_call_target="tpu_custom_call" | custom-call | bytes 6029312 | tf_op jit(solution)/shard_map/pallas_call | solution.py:22
  10.9 2.6 %collective-permute-start.5 = (bf16[64,768]{1,0:T(8,128)(2,1)S(1)}, bf16[64,768]{1,0:T(8,128)(2,1)S(1)}, u32[]{:S(2)}, u32[]{:S(2)}) collective-permute-start(bf16[64,768]{1,0:T(8,128)(2,1)S(1)} %collective-permute-done.1.z2_ref), channel_id=1, source_target_pairs={{0,9},{1,8},{2,11},{3,10},{4,13},{5,12},{6,15},{7,14},{8,1},{9,0},... | collective-permute-start | bytes 294920 | tf_op jit(solution)/shard_map/ppermute | solution.py:242
  13.5 0.5 %collective-permute-start.6 = (bf16[64,768]{1,0:T(8,128)(2,1)S(1)}, bf16[64,768]{1,0:T(8,128)(2,1)S(1)}, u32[]{:S(2)}, u32[]{:S(2)}) collective-permute-start(bf16[64,768]{1,0:T(8,128)(2,1)S(1)} %collective-permute-done.1.z2_ref), channel_id=1, source_target_pairs={{0,8},{1,9},{2,10},{3,11},{4,12},{5,13},{6,14},{7,15},{8,0},{9,1},... | collective-permute-start | bytes 294920 | tf_op jit(solution)/shard_map/ppermute | solution.py:242
  14.0 0.5 %collective-permute-start.7 = (bf16[64,768]{1,0:T(8,128)(2,1)S(1)}, bf16[64,768]{1,0:T(8,128)(2,1)S(1)}, u32[]{:S(2)}, u32[]{:S(2)}) collective-permute-start(bf16[64,768]{1,0:T(8,128)(2,1)S(1)} %collective-permute-done.1.z2_ref), channel_id=1, source_target_pairs={{0,1},{1,0},{2,3},{3,2},{4,5},{5,4},{6,7},{7,6},{8,9},{9,8},{10,11... | collective-permute-start | bytes 294920 | tf_op jit(solution)/shard_map/ppermute | solution.py:242
  14.6 1.8 %collective-permute-done.3.x_ref.order_ref = bf16[80,768]{1,0:T(8,128)(2,1)S(1)} collective-permute-done((bf16[80,768]{1,0:T(8,128)(2,1)S(1)}, bf16[80,768]{1,0:T(8,128)(2,1)S(1)}, u32[]{:S(2)}, u32[]{:S(2)}) %collective-permute-start.3) | collective-permute-done | bytes 122912 | tf_op jit(solution)/shard_map/ppermute | solution.py:242
  16.4 1.4 %shard_map.88.order_ref.weight_ref = bf16[512,1536]{1,0:T(8,128)(2,1)S(1)} custom-call(bf16[512,3072]{1,0:T(8,128)(2,1)} %bitcast.7, bf16[80,768]{1,0:T(8,128)(2,1)S(1)} %collective-permute-done.3.x_ref.order_ref), custom_call_target="tpu_custom_call" | custom-call | bytes 4841472 | tf_op jit(solution)/shard_map/pallas_call | solution.py:22
  17.9 0.6 %collective-permute-done.6.b_ref.x2_ref = bf16[64,768]{1,0:T(8,128)(2,1)S(1)} collective-permute-done((bf16[64,768]{1,0:T(8,128)(2,1)S(1)}, bf16[64,768]{1,0:T(8,128)(2,1)S(1)}, u32[]{:S(2)}, u32[]{:S(2)}) %collective-permute-start.6) | collective-permute-done | bytes 98336 | tf_op jit(solution)/shard_map/ppermute | solution.py:242
  18.8 0.9 %shard_map.87 = (f32[256,512]{1,0:T(8,128)S(1)}, bf16[256,512]{1,0:T(8,128)(2,1)S(1)}, f32[4,64,64]{2,1,0:T(8,128)S(1)}, f32[8,64]{1,0:T(8,128)S(1)}, f32[256,1]{1,0:T(8,128)S(1)}) custom-call(bf16[64,768]{1,0:T(8,128)(2,1)S(1)} %collective-permute-done.d1_ref, bf16[64,768]{1,0:T(8,128)(2,1)S(1)} %collective-permute-done.1.z2_ref, ...), custom_call_target="tpu_custom_call" | custom-call | flops 402653184 | bytes 3771392 | tf_op jit(solution)/shard_map/pallas_call | solution.py:22
  19.7 0.7 %collective-permute-done.8.sib_b_ref = bf16[192,768]{1,0:T(8,128)(2,1)S(1)} collective-permute-done((bf16[192,768]{1,0:T(8,128)(2,1)S(1)}, bf16[192,768]{1,0:T(8,128)(2,1)S(1)}, u32[]{:S(2)}, u32[]{:S(2)}) %collective-permute-start.8) | collective-permute-done | bytes 294944 | tf_op jit(solution)/shard_map/ppermute | solution.py:242
  20.4 0.7 %shard_map.90 = (f32[256,512]{1,0:T(8,128)S(1)}, f32[8,64]{1,0:T(8,128)S(1)}) custom-call(f32[256,512]{1,0:T(8,128)S(1)} %get-tuple-element.18.total_ref, bf16[64,768]{1,0:T(8,128)(2,1)S(1)} %collective-permute-done.1.z2_ref, bf16[64,768]{1,0:T(8,128)(2,1)S(1)} %collective-permute-done.5.c_ref.d3_ref, ...), custom_call_target="tpu_custom_call" | custom-call | flops 402653184 | bytes 4116480 | tf_op jit(solution)/shard_map/pallas_call | solution.py:22
  21.1 2.6 %collective-permute-start.10 = (f32[8,64]{1,0:T(8,128)S(1)}, f32[8,64]{1,0:T(8,128)S(1)}, u32[]{:S(2)}, u32[]{:S(2)}) collective-permute-start(f32[8,64]{1,0:T(8,128)S(1)} %get-tuple-element.28), channel_id=1, source_target_pairs={{0,3},{1,2},{2,1},{3,0},{4,7},{5,6},{6,5},{7,4},{8,11},{9,10},{10,... | collective-permute-start | bytes 6152 | tf_op jit(solution)/shard_map/ppermute | solution.py:242
  23.7 1.8 %collective-permute-start.9 = (f32[8,64]{1,0:T(8,128)S(1)}, f32[8,64]{1,0:T(8,128)S(1)}, u32[]{:S(2)}, u32[]{:S(2)}) collective-permute-start(f32[8,64]{1,0:T(8,128)S(1)} %get-tuple-element.28), channel_id=1, source_target_pairs={{0,1},{1,0},{2,3},{3,2},{4,5},{5,4},{6,7},{7,6},{8,9},{9,8},{10,11... | collective-permute-start | bytes 6152 | tf_op jit(solution)/shard_map/ppermute | solution.py:242
  25.5 1.0 %collective-permute-done.10 = f32[8,64]{1,0:T(8,128)S(1)} collective-permute-done((f32[8,64]{1,0:T(8,128)S(1)}, f32[8,64]{1,0:T(8,128)S(1)}, u32[]{:S(2)}, u32[]{:S(2)}) %collective-permute-start.10) | collective-permute-done | bytes 2080 | tf_op jit(solution)/shard_map/ppermute | solution.py:242
  26.6 1.6 %collective-permute-done.11 = f32[8,64]{1,0:T(8,128)S(1)} collective-permute-done((f32[8,64]{1,0:T(8,128)S(1)}, f32[8,64]{1,0:T(8,128)S(1)}, u32[]{:S(2)}, u32[]{:S(2)}) %collective-permute-start.11) | collective-permute-done | bytes 2080 | tf_op jit(solution)/shard_map/ppermute | solution.py:242
  28.3 0.7 %collective-permute-start.13 = (f32[8,64]{1,0:T(8,128)S(1)}, f32[8,64]{1,0:T(8,128)S(1)}, u32[]{:S(2)}, u32[]{:S(2)}) collective-permute-start(f32[8,64]{1,0:T(8,128)S(1)} %add_add_fusion.a_ref), channel_id=1, source_target_pairs={{0,8},{1,9},{2,10},{3,11},{4,12},{5,13},{6,14},{7,15},{8,0},{9,1},... | collective-permute-start | bytes 6152 | tf_op jit(solution)/shard_map/ppermute | solution.py:242
  29.0 1.1 %collective-permute-start.14 = (f32[8,64]{1,0:T(8,128)S(1)}, f32[8,64]{1,0:T(8,128)S(1)}, u32[]{:S(2)}, u32[]{:S(2)}) collective-permute-start(f32[8,64]{1,0:T(8,128)S(1)} %add_add_fusion.a_ref), channel_id=1, source_target_pairs={{0,4},{1,5},{2,6},{3,7},{4,0},{5,1},{6,2},{7,3},{8,12},{9,13},{10,... | collective-permute-start | bytes 6152 | tf_op jit(solution)/shard_map/ppermute | solution.py:242
  30.1 1.2 %shard_map.91 = (bf16[256,512]{1,0:T(8,128)(2,1)}, bf16[256,512]{1,0:T(8,128)(2,1)}) custom-call(f32[256,512]{1,0:T(8,128)S(1)} %get-tuple-element.21.total_ref, f32[4,64,64]{2,1,0:T(8,128)S(1)} %get-tuple-element.22.place_ref, f32[256,1]{1,0:T(8,128)S(1)} %get-tuple-element.23.row_weight_ref, bf16[256,512]{1,0:T(8,128)(2,1)S(1)} %get-tuple-element.24.gate_ref, ...), custom_call_target="tpu_custom_call" | custom-call | bytes 1639424 | tf_op jit(solution)/shard_map/pallas_call | solution.py:22
  31.3 0.6 %collective-permute-done.13.c_ref = f32[8,64]{1,0:T(8,128)S(1)} collective-permute-done((f32[8,64]{1,0:T(8,128)S(1)}, f32[8,64]{1,0:T(8,128)S(1)}, u32[]{:S(2)}, u32[]{:S(2)}) %collective-permute-start.13) | collective-permute-done | bytes 2080 | tf_op jit(solution)/shard_map/ppermute | solution.py:242
  32.0 0.6 %shard_map.92 = f32[2,64]{1,0:T(2,128)} custom-call(f32[8,64]{1,0:T(8,128)S(1)} %add_add_fusion.a_ref, f32[8,64]{1,0:T(8,128)S(1)} %collective-permute-done.12.b_ref, f32[8,64]{1,0:T(8,128)S(1)} %collective-permute-done.13.c_ref, f32[8,64]{1,0:T(8,128)S(1)} %collective-permute-done.14.d_ref, f32[2,64]{1,0:T(2,128)S(1)} %bitcast.5), custom_call_target="tpu_custom_call" | custom-call | bytes 9216 | tf_op jit(solution)/shard_map/pallas_call | solution.py:22
  (23 shorter events, 0.5 us)
Async XLA Ops:
  0.6 10.3 %collective-permute-start.1 = (bf16[64,768]{1,0:T(8,128)(2,1)}, bf16[64,768]{1,0:T(8,128)(2,1)S(1)}, u32[]{:S(2)}, u32[]{:S(2)}) collective-permute-start(bf16[64,768]{1,0:T(8,128)(2,1)} %rows_hbm.1), channel_id=1, source_target_pairs={{0,2},{1,3},{2,0},{3,1},{4,6},{5,7},{6,4},{7,5},{8,10},{9,11},{10,... | collective-permute-start | bytes 294920 | tf_op jit(solution)/shard_map/ppermute | solution.py:242
  5.7 8.3 %collective-permute-start = (bf16[64,768]{1,0:T(8,128)(2,1)S(1)}, bf16[64,768]{1,0:T(8,128)(2,1)S(1)}, u32[]{:S(2)}, u32[]{:S(2)}) collective-permute-start(bf16[64,768]{1,0:T(8,128)(2,1)S(1)} %slice.4), channel_id=1, source_target_pairs={{0,9},{1,8},{2,11},{3,10},{4,13},{5,12},{6,15},{7,14},{8,1},{9,0},... | collective-permute-start | bytes 294920 | tf_op jit(solution)/shard_map/ppermute | solution.py:242
  8.3 6.3 %collective-permute-start.2 = (bf16[64,768]{1,0:T(8,128)(2,1)S(1)}, bf16[64,768]{1,0:T(8,128)(2,1)S(1)}, u32[]{:S(2)}, u32[]{:S(2)}) collective-permute-start(bf16[64,768]{1,0:T(8,128)(2,1)S(1)} %slice.4), channel_id=1, source_target_pairs={{0,1},{1,0},{2,3},{3,2},{4,5},{5,4},{6,7},{7,6},{8,9},{9,8},{10,11... | collective-permute-start | bytes 294920 | tf_op jit(solution)/shard_map/ppermute | solution.py:242
  8.7 7.6 %collective-permute-start.3 = (bf16[80,768]{1,0:T(8,128)(2,1)S(1)}, bf16[80,768]{1,0:T(8,128)(2,1)S(1)}, u32[]{:S(2)}, u32[]{:S(2)}) collective-permute-start(bf16[80,768]{1,0:T(8,128)(2,1)S(1)} %shard_map.85.own_ref), channel_id=1, source_target_pairs={{0,8},{1,9},{2,10},{3,11},{4,12},{5,13},{6,14},{7,15},{8,0},{9,1},... | collective-permute-start | bytes 368648 | tf_op jit(solution)/shard_map/ppermute | solution.py:242
  10.9 7.0 %collective-permute-start.5 = (bf16[64,768]{1,0:T(8,128)(2,1)S(1)}, bf16[64,768]{1,0:T(8,128)(2,1)S(1)}, u32[]{:S(2)}, u32[]{:S(2)}) collective-permute-start(bf16[64,768]{1,0:T(8,128)(2,1)S(1)} %collective-permute-done.1.z2_ref), channel_id=1, source_target_pairs={{0,9},{1,8},{2,11},{3,10},{4,13},{5,12},{6,15},{7,14},{8,1},{9,0},... | collective-permute-start | bytes 294920 | tf_op jit(solution)/shard_map/ppermute | solution.py:242
  13.5 5.0 %collective-permute-start.6 = (bf16[64,768]{1,0:T(8,128)(2,1)S(1)}, bf16[64,768]{1,0:T(8,128)(2,1)S(1)}, u32[]{:S(2)}, u32[]{:S(2)}) collective-permute-start(bf16[64,768]{1,0:T(8,128)(2,1)S(1)} %collective-permute-done.1.z2_ref), channel_id=1, source_target_pairs={{0,8},{1,9},{2,10},{3,11},{4,12},{5,13},{6,14},{7,15},{8,0},{9,1},... | collective-permute-start | bytes 294920 | tf_op jit(solution)/shard_map/ppermute | solution.py:242
  14.0 4.7 %collective-permute-start.7 = (bf16[64,768]{1,0:T(8,128)(2,1)S(1)}, bf16[64,768]{1,0:T(8,128)(2,1)S(1)}, u32[]{:S(2)}, u32[]{:S(2)}) collective-permute-start(bf16[64,768]{1,0:T(8,128)(2,1)S(1)} %collective-permute-done.1.z2_ref), channel_id=1, source_target_pairs={{0,1},{1,0},{2,3},{3,2},{4,5},{5,4},{6,7},{7,6},{8,9},{9,8},{10,11... | collective-permute-start | bytes 294920 | tf_op jit(solution)/shard_map/ppermute | solution.py:242
  16.4 2.5 %collective-permute-start.4 = (bf16[352,768]{1,0:T(8,128)(2,1)S(1)}, bf16[352,768]{1,0:T(8,128)(2,1)S(1)}, u32[]{:S(2)}, u32[]{:S(2)}) collective-permute-start(bf16[352,768]{1,0:T(8,128)(2,1)S(1)} %constant_dynamic-update-slice_fusion), channel_id=1, source_target_pairs={{0,4},{1,5},{2,6},{3,7},{4,0},{5,1},{6,2},{7,3},{8,12},{9,13},{10,... | collective-permute-start | bytes 1622024 | tf_op jit(solution)/shard_map/ppermute | solution.py:242
  18.7 1.6 %collective-permute-start.8 = (bf16[192,768]{1,0:T(8,128)(2,1)S(1)}, bf16[192,768]{1,0:T(8,128)(2,1)S(1)}, u32[]{:S(2)}, u32[]{:S(2)}) collective-permute-start(bf16[192,768]{1,0:T(8,128)(2,1)S(1)} %shard_map.89), channel_id=1, source_target_pairs={{0,4},{1,5},{2,6},{3,7},{4,0},{5,1},{6,2},{7,3},{8,12},{9,13},{10,... | collective-permute-start | bytes 884744 | tf_op jit(solution)/shard_map/ppermute | solution.py:242
  20.4 11.6 %copy-start = (f32[64,2]{0,1:T(2,128)S(1)}, f32[64,2]{0,1:T(2,128)}, u32[]{:S(2)}) copy-start(f32[64,2]{0,1:T(2,128)} %param.7) | copy-start | bytes 1540
  21.1 5.5 %collective-permute-start.10 = (f32[8,64]{1,0:T(8,128)S(1)}, f32[8,64]{1,0:T(8,128)S(1)}, u32[]{:S(2)}, u32[]{:S(2)}) collective-permute-start(f32[8,64]{1,0:T(8,128)S(1)} %get-tuple-element.28), channel_id=1, source_target_pairs={{0,3},{1,2},{2,1},{3,0},{4,7},{5,6},{6,5},{7,4},{8,11},{9,10},{10,... | collective-permute-start | bytes 6152 | tf_op jit(solution)/shard_map/ppermute | solution.py:242
  23.7 4.5 %collective-permute-start.11 = (f32[8,64]{1,0:T(8,128)S(1)}, f32[8,64]{1,0:T(8,128)S(1)}, u32[]{:S(2)}, u32[]{:S(2)}) collective-permute-start(f32[8,64]{1,0:T(8,128)S(1)} %get-tuple-element.28), channel_id=1, source_target_pairs={{0,2},{1,3},{2,0},{3,1},{4,6},{5,7},{6,4},{7,5},{8,10},{9,11},{10,... | collective-permute-start | bytes 6152 | tf_op jit(solution)/shard_map/ppermute | solution.py:242
  23.7 4.5 %collective-permute-start.9 = (f32[8,64]{1,0:T(8,128)S(1)}, f32[8,64]{1,0:T(8,128)S(1)}, u32[]{:S(2)}, u32[]{:S(2)}) collective-permute-start(f32[8,64]{1,0:T(8,128)S(1)} %get-tuple-element.28), channel_id=1, source_target_pairs={{0,1},{1,0},{2,3},{3,2},{4,5},{5,4},{6,7},{7,6},{8,9},{9,8},{10,11... | collective-permute-start | bytes 6152 | tf_op jit(solution)/shard_map/ppermute | solution.py:242
  28.2 3.1 %collective-permute-start.12 = (f32[8,64]{1,0:T(8,128)S(1)}, f32[8,64]{1,0:T(8,128)S(1)}, u32[]{:S(2)}, u32[]{:S(2)}) collective-permute-start(f32[8,64]{1,0:T(8,128)S(1)} %add_add_fusion.a_ref), channel_id=1, source_target_pairs={{0,12},{1,13},{2,14},{3,15},{4,8},{5,9},{6,10},{7,11},{8,4},{9,5},... | collective-permute-start | bytes 6152 | tf_op jit(solution)/shard_map/ppermute | solution.py:242
  28.3 3.7 %collective-permute-start.13 = (f32[8,64]{1,0:T(8,128)S(1)}, f32[8,64]{1,0:T(8,128)S(1)}, u32[]{:S(2)}, u32[]{:S(2)}) collective-permute-start(f32[8,64]{1,0:T(8,128)S(1)} %add_add_fusion.a_ref), channel_id=1, source_target_pairs={{0,8},{1,9},{2,10},{3,11},{4,12},{5,13},{6,14},{7,15},{8,0},{9,1},... | collective-permute-start | bytes 6152 | tf_op jit(solution)/shard_map/ppermute | solution.py:242
  29.0 2.9 %collective-permute-start.14 = (f32[8,64]{1,0:T(8,128)S(1)}, f32[8,64]{1,0:T(8,128)S(1)}, u32[]{:S(2)}, u32[]{:S(2)}) collective-permute-start(f32[8,64]{1,0:T(8,128)S(1)} %add_add_fusion.a_ref), channel_id=1, source_target_pairs={{0,4},{1,5},{2,6},{3,7},{4,0},{5,1},{6,2},{7,3},{8,12},{9,13},{10,... | collective-permute-start | bytes 6152 | tf_op jit(solution)/shard_map/ppermute | solution.py:242

commit v7 on v4

--- a/solution.py
+++ b/solution.py
@@ -187,13 +187,14 @@
     share_ref[...] = chosen_ref[...] * jnp.concatenate([sums, sums], axis=0)
 
 
-def grads_kernel(dh_ref, gate_ref, up_ref, grad_gate_ref, grad_up_ref):
+def grads_kernel(dh_ref, gate_ref, up_ref, grad_gate_ref, grad_up_ref, zero_ref):
     g = gate_ref[...].astype(F32)
     u = up_ref[...].astype(F32)
     dh = dh_ref[...]
     sig = jax.nn.sigmoid(g)
     grad_up_ref[...] = (dh * (g * sig)).astype(BF16)
     grad_gate_ref[...] = (dh * u * sig * (1.0 + g * (1.0 - sig))).astype(BF16)
+    zero_ref[...] = jnp.zeros_like(zero_ref)
 
 
 def logits_kernel(a_ref, b_ref, c_ref, d_ref, logits_ref, out_ref, sum_s):
@@ -282,13 +283,14 @@
         scratch=[pltpu.VMEM((2, rows, width), BF16)],
         flops=half_flops,
     )
-    share = share + swap(share, 0, 0, 1) + swap(share, 0, 0, 2) + swap(share, 0, 0, 3)
+    grad_gate, grad_up, zero = call(
+        grads_kernel,
+        [jax.ShapeDtypeStruct((rows, hidden), BF16)] * 2
+        + [jax.ShapeDtypeStruct((2 * slots, tokens), F32)],
+        [dh, gate, up],
+    )
+    share = share + swap(share, 0, 0, 1) + swap(share, 0, 0, 2) + swap(share, 0, 0, 3) + zero
     pieces = [share, swap(share, 0, 1, 0), swap(share, 1, 0, 0), swap(share, 1, 1, 0)]
-    grad_gate, grad_up = call(
-        grads_kernel,
-        [jax.ShapeDtypeStruct((rows, hidden), BF16)] * 2,
-        [dh, gate, up],
-    )
     (logit_grad,) = call(
         logits_kernel,
         [jax.ShapeDtypeStruct((2, tokens), F32)],

time: 32.6 us -> 32.6 us (level)
  transfers between devices with their start and end apart: 15 -> 15, of which waited for: 9 -> 8; matrix products, arithmetic and copies ran while one was open for 0% -> 0% of each run, Pallas kernels for 15% -> 15%
where the time goes in v7:
time: 32.6 us; the launch traced here: 32.4 us
  starting transfers between devices  17.8 us (55%)
  waiting for transfers between devices  7.54 us (23%)
  Pallas kernels  6.31 us (19%)
  between operations  0.74 us (2%)
    ppermute x15, starting transfers between devices, swap(): lax.ppermute(value, ('expert', 'etp'), [(i, i ^ mask) for i in range(slot...  17.8 us
    ppermute x15, waiting for transfers between devices, swap(): lax.ppermute(value, ('expert', 'etp'), [(i, i ^ mask) for i in range(slot...  7.54 us
    pallas_call x7, Pallas kernels, call(): pl.pallas_call(kernel, out_shape=tuple(outs), in_specs=[HBM] * hbm + [VME...  6.31 us
  transfers between devices with their start and end apart: 15, of which 8 were waited for; matrix products, arithmetic and copies ran while one was open for 0% of the time, Pallas kernels for 15%

profile of v7, /device:TPU:0, one launch (start us, length us, event | category | flops | bytes accessed | tf_op | source)
XLA Modules:
  0.0 32.4 jit_solution(7535330734862223968)
XLA Ops:
  0.6 3.1 %collective-permute-start.1 = (bf16[64,768]{1,0:T(8,128)(2,1)}, bf16[64,768]{1,0:T(8,128)(2,1)S(1)}, u32[]{:S(2)}, u32[]{:S(2)}) collective-permute-start(bf16[64,768]{1,0:T(8,128)(2,1)} %rows_hbm.1), channel_id=1, source_target_pairs={{0,1},{1,0},{2,3},{3,2},{4,5},{5,4},{6,7},{7,6},{8,9},{9,8},{10,11... | collective-permute-start | bytes 294920 | tf_op jit(solution)/shard_map/ppermute | solution.py:220
  3.7 2.6 %collective-permute-start = (bf16[64,768]{1,0:T(8,128)(2,1)}, bf16[64,768]{1,0:T(8,128)(2,1)S(1)}, u32[]{:S(2)}, u32[]{:S(2)}) collective-permute-start(bf16[64,768]{1,0:T(8,128)(2,1)} %rows_hbm.1), channel_id=1, source_target_pairs={{0,2},{1,3},{2,0},{3,1},{4,6},{5,7},{6,4},{7,5},{8,10},{9,11},{10,... | collective-permute-start | bytes 294920 | tf_op jit(solution)/shard_map/ppermute | solution.py:220
  6.3 1.4 %collective-permute-start.2 = (bf16[64,768]{1,0:T(8,128)(2,1)}, bf16[64,768]{1,0:T(8,128)(2,1)S(1)}, u32[]{:S(2)}, u32[]{:S(2)}) collective-permute-start(bf16[64,768]{1,0:T(8,128)(2,1)} %rows_hbm.1), channel_id=1, source_target_pairs={{0,9},{1,8},{2,11},{3,10},{4,13},{5,12},{6,15},{7,14},{8,1},{9,0},... | collective-permute-start | bytes 294920 | tf_op jit(solution)/shard_map/ppermute | solution.py:220
  7.7 1.0 %shard_map.85.own_ref = bf16[80,768]{1,0:T(8,128)(2,1)S(1)} custom-call(bf16[64,768]{1,0:T(8,128)(2,1)} %rows_hbm.1, f32[2,64]{1,0:T(2,128)} %bitcast.4, s32[2,64]{1,0:T(2,128)} %bitcast.7), custom_call_target="tpu_custom_call" | custom-call | bytes 222208 | tf_op jit(solution)/shard_map/pallas_call | solution.py:22
  8.6 0.6 %collective-permute-start.3 = (bf16[80,768]{1,0:T(8,128)(2,1)S(1)}, bf16[80,768]{1,0:T(8,128)(2,1)S(1)}, u32[]{:S(2)}, u32[]{:S(2)}) collective-permute-start(bf16[80,768]{1,0:T(8,128)(2,1)S(1)} %shard_map.85.own_ref), channel_id=1, source_target_pairs={{0,8},{1,9},{2,10},{3,11},{4,12},{5,13},{6,14},{7,15},{8,0},{9,1},... | collective-permute-start | bytes 368648 | tf_op jit(solution)/shard_map/ppermute | solution.py:220
  9.2 2.1 %shard_map.86 = (bf16[512,3072]{1,0:T(8,128)(2,1)S(1)}, bf16[256,512]{1,0:T(8,128)(2,1)S(1)}, bf16[256,512]{1,0:T(8,128)(2,1)S(1)}, bf16[256,512]{1,0:T(8,128)(2,1)S(1)}) custom-call(bf16[512,3072]{1,0:T(8,128)(2,1)} %bitcast.6, bf16[256,512]{1,0:T(8,128)(2,1)} %gate_hbm.1, bf16[256,512]{1,0:T(8,128)(2,1)} %up_hbm.1), custom_call_target="tpu_custom_call" | custom-call | bytes 7602176 | tf_op jit(solution)/shard_map/pallas_call | solution.py:22
  11.4 2.6 %collective-permute-start.7 = (bf16[64,768]{1,0:T(8,128)(2,1)S(1)}, bf16[64,768]{1,0:T(8,128)(2,1)S(1)}, u32[]{:S(2)}, u32[]{:S(2)}) collective-permute-start(bf16[64,768]{1,0:T(8,128)(2,1)S(1)} %collective-permute-done.z2_ref), channel_id=1, source_target_pairs={{0,9},{1,8},{2,11},{3,10},{4,13},{5,12},{6,15},{7,14},{8,1},{9,0},... | collective-permute-start | bytes 294920 | tf_op jit(solution)/shard_map/ppermute | solution.py:220
  13.9 0.5 %collective-permute-start.6 = (bf16[64,768]{1,0:T(8,128)(2,1)S(1)}, bf16[64,768]{1,0:T(8,128)(2,1)S(1)}, u32[]{:S(2)}, u32[]{:S(2)}) collective-permute-start(bf16[64,768]{1,0:T(8,128)(2,1)S(1)} %collective-permute-done.z2_ref), channel_id=1, source_target_pairs={{0,8},{1,9},{2,10},{3,11},{4,12},{5,13},{6,14},{7,15},{8,0},{9,1},... | collective-permute-start | bytes 294920 | tf_op jit(solution)/shard_map/ppermute | solution.py:220
  15.0 1.6 %collective-permute-done.3.x_ref = bf16[80,768]{1,0:T(8,128)(2,1)S(1)} collective-permute-done((bf16[80,768]{1,0:T(8,128)(2,1)S(1)}, bf16[80,768]{1,0:T(8,128)(2,1)S(1)}, u32[]{:S(2)}, u32[]{:S(2)}) %collective-permute-start.3) | collective-permute-done | bytes 122912 | tf_op jit(solution)/shard_map/ppermute | solution.py:220
  16.7 1.0 %collective-permute-done.7.c_ref.d3_ref = bf16[64,768]{1,0:T(8,128)(2,1)S(1)} collective-permute-done((bf16[64,768]{1,0:T(8,128)(2,1)S(1)}, bf16[64,768]{1,0:T(8,128)(2,1)S(1)}, u32[]{:S(2)}, u32[]{:S(2)}) %collective-permute-start.7) | collective-permute-done | bytes 98336 | tf_op jit(solution)/shard_map/ppermute | solution.py:220
  17.7 1.1 %collective-permute-done.6.b_ref.x2_ref = bf16[64,768]{1,0:T(8,128)(2,1)S(1)} collective-permute-done((bf16[64,768]{1,0:T(8,128)(2,1)S(1)}, bf16[64,768]{1,0:T(8,128)(2,1)S(1)}, u32[]{:S(2)}, u32[]{:S(2)}) %collective-permute-start.6) | collective-permute-done | bytes 98336 | tf_op jit(solution)/shard_map/ppermute | solution.py:220
  19.3 0.7 %shard_map.87 = (f32[256,512]{1,0:T(8,128)S(1)}, f32[4,64,64]{2,1,0:T(8,128)S(1)}, f32[8,64]{1,0:T(8,128)S(1)}, f32[256,1]{1,0:T(8,128)S(1)}) custom-call(bf16[64,768]{1,0:T(8,128)(2,1)S(1)} %collective-permute-done.z2_ref, bf16[64,768]{1,0:T(8,128)(2,1)S(1)} %collective-permute-done.1.z1_ref, bf16[64,768]{1,0:T(8,128)(2,1)S(1)} %collective-permute-done.2.d1_ref, ...), custom_call_target="tpu_custom_call" | custom-call | flops 402653184 | bytes 4819968 | tf_op jit(solution)/shard_map/pallas_call | solution.py:22
  20.0 0.8 %collective-permute-done.8.sib_b_ref = bf16[192,768]{1,0:T(8,128)(2,1)S(1)} collective-permute-done((bf16[192,768]{1,0:T(8,128)(2,1)S(1)}, bf16[192,768]{1,0:T(8,128)(2,1)S(1)}, u32[]{:S(2)}, u32[]{:S(2)}) %collective-permute-start.8) | collective-permute-done | bytes 294944 | tf_op jit(solution)/shard_map/ppermute | solution.py:220
  20.8 1.0 %shard_map.89 = (f32[256,512]{1,0:T(8,128)S(1)}, f32[8,64]{1,0:T(8,128)S(1)}) custom-call(f32[256,512]{1,0:T(8,128)S(1)} %get-tuple-element.17.total_ref, bf16[64,768]{1,0:T(8,128)(2,1)S(1)} %collective-permute-done.z2_ref, bf16[64,768]{1,0:T(8,128)(2,1)S(1)} %collective-permute-done.5.a_ref.z3_ref, bf16[64,768]{1,0:T(8,128)(2,1)S(1)} %collective-permute-done.6.b_ref.x2_ref, ...), custom_call_target="tpu_custom_call" | custom-call | flops 402653184 | bytes 5755904 | tf_op jit(solution)/shard_map/pallas_call | solution.py:22
  21.8 1.8 %collective-permute-start.11 = (f32[8,64]{1,0:T(8,128)S(1)}, f32[8,64]{1,0:T(8,128)S(1)}, u32[]{:S(2)}, u32[]{:S(2)}) collective-permute-start(f32[8,64]{1,0:T(8,128)S(1)} %get-tuple-element.27), channel_id=1, source_target_pairs={{0,3},{1,2},{2,1},{3,0},{4,7},{5,6},{6,5},{7,4},{8,11},{9,10},{10,... | collective-permute-start | bytes 6152 | tf_op jit(solution)/shard_map/ppermute | solution.py:220
  23.6 0.6 %collective-permute-start.10 = (f32[8,64]{1,0:T(8,128)S(1)}, f32[8,64]{1,0:T(8,128)S(1)}, u32[]{:S(2)}, u32[]{:S(2)}) collective-permute-start(f32[8,64]{1,0:T(8,128)S(1)} %get-tuple-element.27), channel_id=1, source_target_pairs={{0,2},{1,3},{2,0},{3,1},{4,6},{5,7},{6,4},{7,5},{8,10},{9,11},{10,... | collective-permute-start | bytes 6152 | tf_op jit(solution)/shard_map/ppermute | solution.py:220
  24.2 2.1 %collective-permute-start.9 = (f32[8,64]{1,0:T(8,128)S(1)}, f32[8,64]{1,0:T(8,128)S(1)}, u32[]{:S(2)}, u32[]{:S(2)}) collective-permute-start(f32[8,64]{1,0:T(8,128)S(1)} %get-tuple-element.27), channel_id=1, source_target_pairs={{0,1},{1,0},{2,3},{3,2},{4,5},{5,4},{6,7},{7,6},{8,9},{9,8},{10,11... | collective-permute-start | bytes 6152 | tf_op jit(solution)/shard_map/ppermute | solution.py:220
  26.3 1.0 %shard_map.90 = (bf16[256,512]{1,0:T(8,128)(2,1)}, bf16[256,512]{1,0:T(8,128)(2,1)}, f32[8,64]{1,0:T(8,128)S(1)}) custom-call(f32[256,512]{1,0:T(8,128)S(1)} %get-tuple-element.22.dh_ref, bf16[256,512]{1,0:T(8,128)(2,1)S(1)} %get-tuple-element.23.gate_ref, bf16[256,512]{1,0:T(8,128)(2,1)S(1)} %get-tuple-element.24.up_ref), custom_call_target="tpu_custom_call" | custom-call | bytes 1574912 | tf_op jit(solution)/shard_map/pallas_call | solution.py:22
  27.3 0.8 %collective-permute-done.10 = f32[8,64]{1,0:T(8,128)S(1)} collective-permute-done((f32[8,64]{1,0:T(8,128)S(1)}, f32[8,64]{1,0:T(8,128)S(1)}, u32[]{:S(2)}, u32[]{:S(2)}) %collective-permute-start.10) | collective-permute-done | bytes 2080 | tf_op jit(solution)/shard_map/ppermute | solution.py:220
  28.2 1.2 %collective-permute-start.13 = (f32[8,64]{1,0:T(8,128)S(1)}, f32[8,64]{1,0:T(8,128)S(1)}, u32[]{:S(2)}, u32[]{:S(2)}) collective-permute-start(f32[8,64]{1,0:T(8,128)S(1)} %add_add_fusion.a_ref), channel_id=1, source_target_pairs={{0,8},{1,9},{2,10},{3,11},{4,12},{5,13},{6,14},{7,15},{8,0},{9,1},... | collective-permute-start | bytes 6152 | tf_op jit(solution)/shard_map/ppermute | solution.py:220
  29.4 0.6 %collective-permute-start.12 = (f32[8,64]{1,0:T(8,128)S(1)}, f32[8,64]{1,0:T(8,128)S(1)}, u32[]{:S(2)}, u32[]{:S(2)}) collective-permute-start(f32[8,64]{1,0:T(8,128)S(1)} %add_add_fusion.a_ref), channel_id=1, source_target_pairs={{0,4},{1,5},{2,6},{3,7},{4,0},{5,1},{6,2},{7,3},{8,12},{9,13},{10,... | collective-permute-start | bytes 6152 | tf_op jit(solution)/shard_map/ppermute | solution.py:220
  30.0 1.2 %collective-permute-done.14.d_ref = f32[8,64]{1,0:T(8,128)S(1)} collective-permute-done((f32[8,64]{1,0:T(8,128)S(1)}, f32[8,64]{1,0:T(8,128)S(1)}, u32[]{:S(2)}, u32[]{:S(2)}) %collective-permute-start.14) | collective-permute-done | bytes 2080 | tf_op jit(solution)/shard_map/ppermute | solution.py:220
  31.2 0.7 %collective-permute-done.13.c_ref = f32[8,64]{1,0:T(8,128)S(1)} collective-permute-done((f32[8,64]{1,0:T(8,128)S(1)}, f32[8,64]{1,0:T(8,128)S(1)}, u32[]{:S(2)}, u32[]{:S(2)}) %collective-permute-start.13) | collective-permute-done | bytes 2080 | tf_op jit(solution)/shard_map/ppermute | solution.py:220
  31.9 0.6 %shard_map.91 = f32[2,64]{1,0:T(2,128)} custom-call(f32[8,64]{1,0:T(8,128)S(1)} %add_add_fusion.a_ref, f32[8,64]{1,0:T(8,128)S(1)} %collective-permute-done.12.b_ref, f32[8,64]{1,0:T(8,128)S(1)} %collective-permute-done.13.c_ref, f32[8,64]{1,0:T(8,128)S(1)} %collective-permute-done.14.d_ref, f32[2,64]{1,0:T(2,128)S(1)} %bitcast.5), custom_call_target="tpu_custom_call" | custom-call | bytes 9216 | tf_op jit(solution)/shard_map/pallas_call | solution.py:22
  (21 shorter events, 1.3 us)
Async XLA Ops:
  0.6 14.4 %collective-permute-start.1 = (bf16[64,768]{1,0:T(8,128)(2,1)}, bf16[64,768]{1,0:T(8,128)(2,1)S(1)}, u32[]{:S(2)}, u32[]{:S(2)}) collective-permute-start(bf16[64,768]{1,0:T(8,128)(2,1)} %rows_hbm.1), channel_id=1, source_target_pairs={{0,1},{1,0},{2,3},{3,2},{4,5},{5,4},{6,7},{7,6},{8,9},{9,8},{10,11... | collective-permute-start | bytes 294920 | tf_op jit(solution)/shard_map/ppermute | solution.py:220
  3.7 7.6 %collective-permute-start = (bf16[64,768]{1,0:T(8,128)(2,1)}, bf16[64,768]{1,0:T(8,128)(2,1)S(1)}, u32[]{:S(2)}, u32[]{:S(2)}) collective-permute-start(bf16[64,768]{1,0:T(8,128)(2,1)} %rows_hbm.1), channel_id=1, source_target_pairs={{0,2},{1,3},{2,0},{3,1},{4,6},{5,7},{6,4},{7,5},{8,10},{9,11},{10,... | collective-permute-start | bytes 294920 | tf_op jit(solution)/shard_map/ppermute | solution.py:220
  6.3 8.2 %collective-permute-start.2 = (bf16[64,768]{1,0:T(8,128)(2,1)}, bf16[64,768]{1,0:T(8,128)(2,1)S(1)}, u32[]{:S(2)}, u32[]{:S(2)}) collective-permute-start(bf16[64,768]{1,0:T(8,128)(2,1)} %rows_hbm.1), channel_id=1, source_target_pairs={{0,9},{1,8},{2,11},{3,10},{4,13},{5,12},{6,15},{7,14},{8,1},{9,0},... | collective-permute-start | bytes 294920 | tf_op jit(solution)/shard_map/ppermute | solution.py:220
  8.6 8.0 %collective-permute-start.3 = (bf16[80,768]{1,0:T(8,128)(2,1)S(1)}, bf16[80,768]{1,0:T(8,128)(2,1)S(1)}, u32[]{:S(2)}, u32[]{:S(2)}) collective-permute-start(bf16[80,768]{1,0:T(8,128)(2,1)S(1)} %shard_map.85.own_ref), channel_id=1, source_target_pairs={{0,8},{1,9},{2,10},{3,11},{4,12},{5,13},{6,14},{7,15},{8,0},{9,1},... | collective-permute-start | bytes 368648 | tf_op jit(solution)/shard_map/ppermute | solution.py:220
  11.4 6.3 %collective-permute-start.7 = (bf16[64,768]{1,0:T(8,128)(2,1)S(1)}, bf16[64,768]{1,0:T(8,128)(2,1)S(1)}, u32[]{:S(2)}, u32[]{:S(2)}) collective-permute-start(bf16[64,768]{1,0:T(8,128)(2,1)S(1)} %collective-permute-done.z2_ref), channel_id=1, source_target_pairs={{0,9},{1,8},{2,11},{3,10},{4,13},{5,12},{6,15},{7,14},{8,1},{9,0},... | collective-permute-start | bytes 294920 | tf_op jit(solution)/shard_map/ppermute | solution.py:220
  13.9 4.8 %collective-permute-start.6 = (bf16[64,768]{1,0:T(8,128)(2,1)S(1)}, bf16[64,768]{1,0:T(8,128)(2,1)S(1)}, u32[]{:S(2)}, u32[]{:S(2)}) collective-permute-start(bf16[64,768]{1,0:T(8,128)(2,1)S(1)} %collective-permute-done.z2_ref), channel_id=1, source_target_pairs={{0,8},{1,9},{2,10},{3,11},{4,12},{5,13},{6,14},{7,15},{8,0},{9,1},... | collective-permute-start | bytes 294920 | tf_op jit(solution)/shard_map/ppermute | solution.py:220
  14.5 4.7 %collective-permute-start.5 = (bf16[64,768]{1,0:T(8,128)(2,1)S(1)}, bf16[64,768]{1,0:T(8,128)(2,1)S(1)}, u32[]{:S(2)}, u32[]{:S(2)}) collective-permute-start(bf16[64,768]{1,0:T(8,128)(2,1)S(1)} %collective-permute-done.z2_ref), channel_id=1, source_target_pairs={{0,1},{1,0},{2,3},{3,2},{4,5},{5,4},{6,7},{7,6},{8,9},{9,8},{10,11... | collective-permute-start | bytes 294920 | tf_op jit(solution)/shard_map/ppermute | solution.py:220
  16.6 2.7 %collective-permute-start.4 = (bf16[352,768]{1,0:T(8,128)(2,1)S(1)}, bf16[352,768]{1,0:T(8,128)(2,1)S(1)}, u32[]{:S(2)}, u32[]{:S(2)}) collective-permute-start(bf16[352,768]{1,0:T(8,128)(2,1)S(1)} %constant_dynamic-update-slice_fusion), channel_id=1, source_target_pairs={{0,4},{1,5},{2,6},{3,7},{4,0},{5,1},{6,2},{7,3},{8,12},{9,13},{10,... | collective-permute-start | bytes 1622024 | tf_op jit(solution)/shard_map/ppermute | solution.py:220
  19.2 1.6 %collective-permute-start.8 = (bf16[192,768]{1,0:T(8,128)(2,1)S(1)}, bf16[192,768]{1,0:T(8,128)(2,1)S(1)}, u32[]{:S(2)}, u32[]{:S(2)}) collective-permute-start(bf16[192,768]{1,0:T(8,128)(2,1)S(1)} %shard_map.88), channel_id=1, source_target_pairs={{0,4},{1,5},{2,6},{3,7},{4,0},{5,1},{6,2},{7,3},{8,12},{9,13},{10,... | collective-permute-start | bytes 884744 | tf_op jit(solution)/shard_map/ppermute | solution.py:220
  20.8 11.0 %copy-start = (f32[64,2]{0,1:T(2,128)S(1)}, f32[64,2]{0,1:T(2,128)}, u32[]{:S(2)}) copy-start(f32[64,2]{0,1:T(2,128)} %param.7) | copy-start | bytes 1540
  21.8 5.5 %collective-permute-start.11 = (f32[8,64]{1,0:T(8,128)S(1)}, f32[8,64]{1,0:T(8,128)S(1)}, u32[]{:S(2)}, u32[]{:S(2)}) collective-permute-start(f32[8,64]{1,0:T(8,128)S(1)} %get-tuple-element.27), channel_id=1, source_target_pairs={{0,3},{1,2},{2,1},{3,0},{4,7},{5,6},{6,5},{7,4},{8,11},{9,10},{10,... | collective-permute-start | bytes 6152 | tf_op jit(solution)/shard_map/ppermute | solution.py:220
  23.6 4.5 %collective-permute-start.10 = (f32[8,64]{1,0:T(8,128)S(1)}, f32[8,64]{1,0:T(8,128)S(1)}, u32[]{:S(2)}, u32[]{:S(2)}) collective-permute-start(f32[8,64]{1,0:T(8,128)S(1)} %get-tuple-element.27), channel_id=1, source_target_pairs={{0,2},{1,3},{2,0},{3,1},{4,6},{5,7},{6,4},{7,5},{8,10},{9,11},{10,... | collective-permute-start | bytes 6152 | tf_op jit(solution)/shard_map/ppermute | solution.py:220
  24.2 3.9 %collective-permute-start.9 = (f32[8,64]{1,0:T(8,128)S(1)}, f32[8,64]{1,0:T(8,128)S(1)}, u32[]{:S(2)}, u32[]{:S(2)}) collective-permute-start(f32[8,64]{1,0:T(8,128)S(1)} %get-tuple-element.27), channel_id=1, source_target_pairs={{0,1},{1,0},{2,3},{3,2},{4,5},{5,4},{6,7},{7,6},{8,9},{9,8},{10,11... | collective-permute-start | bytes 6152 | tf_op jit(solution)/shard_map/ppermute | solution.py:220
  28.1 3.1 %collective-permute-start.14 = (f32[8,64]{1,0:T(8,128)S(1)}, f32[8,64]{1,0:T(8,128)S(1)}, u32[]{:S(2)}, u32[]{:S(2)}) collective-permute-start(f32[8,64]{1,0:T(8,128)S(1)} %add_add_fusion.a_ref), channel_id=1, source_target_pairs={{0,12},{1,13},{2,14},{3,15},{4,8},{5,9},{6,10},{7,11},{8,4},{9,5},... | collective-permute-start | bytes 6152 | tf_op jit(solution)/shard_map/ppermute | solution.py:220
  28.2 3.7 %collective-permute-start.13 = (f32[8,64]{1,0:T(8,128)S(1)}, f32[8,64]{1,0:T(8,128)S(1)}, u32[]{:S(2)}, u32[]{:S(2)}) collective-permute-start(f32[8,64]{1,0:T(8,128)S(1)} %add_add_fusion.a_ref), channel_id=1, source_target_pairs={{0,8},{1,9},{2,10},{3,11},{4,12},{5,13},{6,14},{7,15},{8,0},{9,1},... | collective-permute-start | bytes 6152 | tf_op jit(solution)/shard_map/ppermute | solution.py:220
  29.4 2.4 %collective-permute-start.12 = (f32[8,64]{1,0:T(8,128)S(1)}, f32[8,64]{1,0:T(8,128)S(1)}, u32[]{:S(2)}, u32[]{:S(2)}) collective-permute-start(f32[8,64]{1,0:T(8,128)S(1)} %add_add_fusion.a_ref), channel_id=1, source_target_pairs={{0,4},{1,5},{2,6},{3,7},{4,0},{5,1},{6,2},{7,3},{8,12},{9,13},{10,... | collective-permute-start | bytes 6152 | tf_op jit(solution)/shard_map/ppermute | solution.py:220
